TPU v7x, 32 devices: a whole 2x2x4 slice. The times are simulated.
32 devices in a mesh: tm: 4 (over y, core), space: 8 (over z, x).
Axes of the slice: x: 2, y: 2, z: 4, core: 2. Of those that a mesh axis runs over, the one named last changes fastest.
Arguments:
- queries: bfloat16 [4096, 6144], P(('tm', 'space')), may hold values from -5 to 5
- key_rows: bfloat16 [4096, 6144], P(('tm', 'space')), may hold values from -5 to 5
- value_rows: bfloat16 [4096, 6144], P(('tm', 'space')), may hold values from -6 to 6
- tile_lists: int32 [4, 16, 2], P('tm'), may hold values from 0 to 15, as said below
- span_reach: int32 [4, 16], P('tm'), may hold values from 0 to 3, as said below
Outputs:
- attended: bfloat16 [4096, 6144], P(('tm', 'space'))
Inputs may be any that keep to these rules, and one draw needn't show every extreme that they name: Each row of tile_lists holds 2 different tiles and begins with the query tile itself. span_reach[c, t] <= c for every span c and tile t; in the last span, tile 0 reaches span 0 and tile 1 reaches only its own span.
All inputs are finite; a program needn't handle non-finite values.
Results may differ from a plain program's by a relative error of at most 0.009.
Values may be sent and summed in bfloat16 or wider, within the bound.
No kernel may reach another device: no remote copies, remote signals or barrier semaphores. Data moves between devices by JAX's collectives and lax.ppermute only.
A program may use at most 192 MiB of HBM per device.

v0:
```python
import jax
import jax.numpy as jnp
from jax import lax
from jax.sharding import PartitionSpec as P

DH = 128
TILE = 64
KT = 2


def merge_state(carry, state):
    numer_a, top_a, total_a = carry
    numer_b, top_b, total_b = state
    big = jnp.maximum(top_a, top_b)
    factor_a = jnp.exp(top_a - big)
    factor_b = jnp.exp(top_b - big)
    numer = factor_a[..., None] * numer_a + factor_b[..., None] * numer_b
    return (numer, big, factor_a * total_a + factor_b * total_b)


def body(queries, key_rows, value_rows, tile_lists, span_reach):
    groups = lax.axis_size("space")
    tok_rows = queries.shape[0]
    heads_local = queries.shape[1] // DH // groups
    lists = tile_lists[0]
    reach = span_reach[0][:, None, None]
    span = lax.axis_index("tm")
    scale = DH ** (-0.5)
    shape_split = (tok_rows, groups, heads_local, DH)
    query_part = lax.all_to_all(
        queries.reshape(shape_split), "space", split_axis=1, concat_axis=0, tiled=True
    )
    key_part = lax.all_to_all(
        key_rows.reshape(shape_split), "space", split_axis=1, concat_axis=0, tiled=True
    )
    value_part = lax.all_to_all(
        value_rows.reshape(shape_split), "space", split_axis=1, concat_axis=0, tiled=True
    )
    span_rows = query_part.shape[0]
    heads_here = query_part.shape[2]
    tiles = span_rows // TILE
    query_tiles = query_part.reshape(tiles, TILE, heads_here, DH)
    flat_width = heads_here * DH
    stacked = jnp.stack(
        [key_part.reshape(span_rows, flat_width), value_part.reshape(span_rows, flat_width)]
    )
    initial = (
        jnp.zeros((tiles, heads_here, TILE, DH), jnp.float32),
        jnp.full((tiles, heads_here, TILE), -1e30, jnp.float32),
        jnp.zeros((tiles, heads_here, TILE), jnp.float32),
    )
    carry = initial
    pieces = lax.all_gather(stacked[None], "tm", axis=0, tiled=True)
    start = jnp.int32(0)
    for offset in range(pieces.shape[0]):
        piece_stacked = pieces[offset]
        source = start + offset
        key_sel = (
            piece_stacked[0]
            .reshape(tiles, TILE, heads_here, DH)[lists]
            .reshape(tiles, KT * TILE, heads_here, DH)
        )
        value_sel = (
            piece_stacked[1]
            .reshape(tiles, TILE, heads_here, DH)[lists]
            .reshape(tiles, KT * TILE, heads_here, DH)
        )
        scores = (
            jnp.einsum("tqhd,tkhd->thqk", query_tiles, key_sel, preferred_element_type=jnp.float32)
            * scale
        )
        top = jnp.max(scores, axis=-1)
        expo = jnp.exp(scores - top[..., None])
        total = jnp.sum(expo, axis=-1)
        weights = expo.astype(jnp.bfloat16)
        partial_value = jnp.einsum(
            "thqk,tkhd->thqd", weights, value_sel, preferred_element_type=jnp.float32
        )
        valid = jnp.logical_and(source >= reach, source <= span)
        top = jnp.where(valid, top, jnp.float32(-1e30))
        total = jnp.where(valid, total, jnp.float32(0.0))
        partial_value = jnp.where(valid[..., None], partial_value, jnp.float32(0.0))
        carry = merge_state(carry, (partial_value, top, total))
    numer, big, denom = carry
    output = numer / denom[..., None]
    regrouped = (
        jnp.transpose(output, (0, 2, 1, 3)).reshape(span_rows, heads_here, DH).astype(jnp.bfloat16)
    )
    flat_out = regrouped.reshape(regrouped.shape[0], heads_local * DH)
    return lax.all_to_all(flat_out, "space", split_axis=0, concat_axis=1, tiled=True)


def solution(mesh):
    in_specs = (
        P(("tm", "space"), None),
        P(("tm", "space"), None),
        P(("tm", "space"), None),
        P("tm", None, None),
        P("tm", None),
    )
    out_specs = P(("tm", "space"), None)
    return jax.shard_map(body, mesh=mesh, in_specs=in_specs, out_specs=out_specs, check_vma=False)
```

profile of v0, /device:TPU:0, one launch (start us, length us, event | category | flops | bytes accessed | tf_op | source)
XLA Modules:
  0.0 364.6 jit_solution(14716302059868385434)
XLA Ops:
  9.3 7.3 %all-to-all-start = ((bf16[128,8,6,128]{0,3,2,1:T(8,128)(2,1)}), bf16[128,8,6,128]{0,3,2,1:T(8,128)(2,1)S(1)}, u32[]{:S(2)}, u32[]{:S(2)}) async-start(bf16[128,8,6,128]{0,3,2,1:T(8,128)(2,1)} %bitcast.1), calls=%async_computation | async-start | bytes 3145728 | tf_op jit(solution)/shard_map/all_to_all | solution.py:33
  18.1 35.4 %all-to-all-done = bf16[128,8,6,128]{0,3,2,1:T(8,128)(2,1)S(1)} async-done(((bf16[128,8,6,128]{0,3,2,1:T(8,128)(2,1)}), bf16[128,8,6,128]{0,3,2,1:T(8,128)(2,1)S(1)}, u32[]{:S(2)}, u32[]{:S(2)}) %all-to-all-start) | async-done | bytes 1572896 | tf_op jit(solution)/shard_map/all_to_all | solution.py:33
  53.5 3.6 all-to-all-start.1
  59.4 3.7 %stack_reshape.6 = bf16[1,1024,768]{1,2,0:T(8,128)(2,1)} reshape(bf16[8,128,1,6,128]{1,0,4,3,2:T(8,128)(2,1)} %copy.82) | data formatting | bytes 3145728 | tf_op jit(solution)/shard_map/stack;reshape | solution.py:44
  63.1 31.3 %all-to-all-done.1 = bf16[128,8,6,128]{0,3,2,1:T(8,128)(2,1)S(1)} async-done(((bf16[128,8,6,128]{0,3,2,1:T(8,128)(2,1)}), bf16[128,8,6,128]{0,3,2,1:T(8,128)(2,1)S(1)}, u32[]{:S(2)}, u32[]{:S(2)}) %all-to-all-start.1) | async-done | bytes 1572896 | tf_op jit(solution)/shard_map/all_to_all | solution.py:36
  105.4 3.8 %all-to-all-start.2 = ((bf16[128,8,6,128]{0,3,2,1:T(8,128)(2,1)}), bf16[128,8,6,128]{0,3,2,1:T(8,128)(2,1)S(1)}, u32[]{:S(2)}, u32[]{:S(2)}) async-start(bf16[128,8,6,128]{0,3,2,1:T(8,128)(2,1)} %bitcast.10), calls=%async_computation.2 | async-start | bytes 3145728 | tf_op jit(solution)/shard_map/all_to_all | solution.py:30
  110.1 36.2 %all-to-all-done.2 = bf16[128,8,6,128]{0,3,2,1:T(8,128)(2,1)S(1)} async-done(((bf16[128,8,6,128]{0,3,2,1:T(8,128)(2,1)}), bf16[128,8,6,128]{0,3,2,1:T(8,128)(2,1)S(1)}, u32[]{:S(2)}, u32[]{:S(2)}) %all-to-all-start.2) | async-done | bytes 1572896 | tf_op jit(solution)/shard_map/all_to_all | solution.py:30
  147.2 36.6 %all-gather.3.cloned.1.call-done = bf16[8,1024,768]{2,1,0:T(8,128)(2,1)} async-done(((bf16[2,1024,768]{2,1,0:T(8,128)(2,1)}), bf16[8,1024,768]{2,1,0:T(8,128)(2,1)}) %all-gather.3.cloned.1.call-update) | async-done | bytes 12582928 | tf_op jit(solution)/shard_map/all_gather | solution.py:53
  183.8 9.1 %fusion.79 = (bf16[1,1,1024,768]{3,2,1,0:T(8,128)(2,1)}, bf16[1,1,1024,768]{3,2,1,0:T(8,128)(2,1)}, bf16[1,1,1024,768]{3,2,1,0:T(8,128)(2,1)}, bf16[1,1,1024,768...) fusion(bf16[4,2,1024,768]{3,2,1,0:T(8,128)(2,1)} %bitcast.209), kind=kLoop, calls=%fused_computation.109 | loop fusion | bytes 25165824 | tf_op jit(solution)/shard_map/slice | solution.py:59
  192.9 4.3 %reshape_squeeze.25 = bf16[16,64,6,128]{3,2,1,0:T(8,128)(2,1)} reshape(bf16[1,1,1024,768]{3,2,1,0:T(8,128)(2,1)} %get-tuple-element.19) | data formatting | bytes 3145728 | tf_op jit(solution)/shard_map/reshape;squeeze | solution.py:60
  197.2 4.3 %reshape_squeeze.24 = bf16[16,64,6,128]{3,2,1,0:T(8,128)(2,1)} reshape(bf16[1,1,1024,768]{3,2,1,0:T(8,128)(2,1)} %get-tuple-element.12) | data formatting | bytes 3145728 | tf_op jit(solution)/shard_map/reshape;squeeze | solution.py:60
  201.5 4.6 %gather_fusion.1 = bf16[32,64,6,128]{3,2,1,0:T(8,128)(2,1)} fusion(bf16[16,64,6,128]{3,2,1,0:T(8,128)(2,1)} %reshape_squeeze.25, s32[1024]{0:T(1024)S(1)} %pad_clamp_fusion), kind=kCustom, calls=%fused_computation.1 | custom fusion | bytes 6291584 | tf_op jit(solution)/shard_map/gather | solution.py:59
  206.2 4.6 %gather_fusion = bf16[32,64,6,128]{3,2,1,0:T(8,128)(2,1)} fusion(bf16[16,64,6,128]{3,2,1,0:T(8,128)(2,1)} %reshape_squeeze.24, s32[1024]{0:T(1024)S(1)} %pad_clamp_fusion), kind=kCustom, calls=%fused_computation | custom fusion | bytes 6291584 | tf_op jit(solution)/shard_map/gather | solution.py:59
  210.8 6.3 %bitcast_reduce_fusion.2 = (f32[16,6,64]{2,1,0:T(8,128)S(1)}, f32[16,6,128,64]{2,3,1,0:T(8,128)}) fusion(bf16[16,64,6,128]{3,1,0,2:T(8,128)(2,1)S(1)} %bitcast.198, bf16[16,128,6,128]{3,2,1,0:T(8,128)(2,1)} %bitcast.206), kind=kOutput, calls=%fused_computation.41 | convolution fusion | flops 202893312 | bytes 7888896 | tf_op jit(solution)/shard_map/tqhd,tkhd->thqk/dot_general | solution.py:69
  217.1 3.9 %bitcast_reduce_fusion.3 = (f32[16,6,64]{2,1,0:T(8,128)S(1)}, f32[16,6,128,64]{2,3,1,0:T(8,128)}) fusion(bf16[16,64,6,128]{3,1,0,2:T(8,128)(2,1)S(1)} %bitcast.199, bf16[16,128,6,128]{3,2,1,0:T(8,128)(2,1)S(1)} %bitcast.204), kind=kOutput, calls=%fused_computation.46 | convolution fusion | flops 202893312 | bytes 7888896 | tf_op jit(solution)/shard_map/tqhd,tkhd->thqk/dot_general | solution.py:69
  221.0 4.3 %reshape_squeeze.27 = bf16[16,64,6,128]{3,2,1,0:T(8,128)(2,1)} reshape(bf16[1,1,1024,768]{3,2,1,0:T(8,128)(2,1)} %get-tuple-element.17) | data formatting | bytes 3145728 | tf_op jit(solution)/shard_map/reshape;squeeze | solution.py:60
  225.3 4.6 %gather_fusion.3 = bf16[32,64,6,128]{3,2,1,0:T(8,128)(2,1)} fusion(bf16[16,64,6,128]{3,2,1,0:T(8,128)(2,1)} %reshape_squeeze.27, s32[1024]{0:T(1024)S(1)} %pad_clamp_fusion), kind=kCustom, calls=%fused_computation.3 | custom fusion | bytes 6291584 | tf_op jit(solution)/shard_map/gather | solution.py:59
  229.9 6.1 %bitcast_reduce_fusion = (f32[16,6,64]{2,1,0:T(8,128)S(1)}, f32[16,6,128,64]{2,3,1,0:T(8,128)}) fusion(bf16[16,64,6,128]{3,1,0,2:T(8,128)(2,1)S(1)} %bitcast.200, bf16[16,128,6,128]{3,2,1,0:T(8,128)(2,1)} %bitcast.208), kind=kOutput, calls=%fused_computation.31 | convolution fusion | flops 202893312 | bytes 7888896 | tf_op jit(solution)/shard_map/tqhd,tkhd->thqk/dot_general | solution.py:69
  238.8 4.6 %gather_fusion.2 = bf16[32,64,6,128]{3,2,1,0:T(8,128)(2,1)} fusion(bf16[16,64,6,128]{3,2,1,0:T(8,128)(2,1)} %reshape_squeeze.26, s32[1024]{0:T(1024)S(1)} %pad_clamp_fusion), kind=kCustom, calls=%fused_computation.2 | custom fusion | bytes 6291584 | tf_op jit(solution)/shard_map/gather | solution.py:59
  243.5 6.1 %bitcast_reduce_fusion.1 = (f32[16,6,64]{2,1,0:T(8,128)S(1)}, f32[16,6,128,64]{2,3,1,0:T(8,128)}) fusion(bf16[16,64,6,128]{3,1,0,2:T(8,128)(2,1)S(1)} %bitcast.201, bf16[16,128,6,128]{3,2,1,0:T(8,128)(2,1)} %bitcast.207), kind=kOutput, calls=%fused_computation.36 | convolution fusion | flops 202893312 | bytes 7888896 | tf_op jit(solution)/shard_map/tqhd,tkhd->thqk/dot_general | solution.py:69
  249.6 3.4 reshape_squeeze.29
  256.0 3.4 reshape_squeeze.30
  262.5 4.3 %reshape_squeeze.31 = bf16[16,64,6,128]{3,2,1,0:T(8,128)(2,1)} reshape(bf16[1,1,1024,768]{3,2,1,0:T(8,128)(2,1)} %get-tuple-element.13) | data formatting | bytes 3145728 | tf_op jit(solution)/shard_map/reshape;squeeze | solution.py:65
  266.8 4.8 %gather_fusion.7 = bf16[32,64,6,128]{3,2,1,0:T(8,128)(2,1)} fusion(bf16[16,64,6,128]{3,2,1,0:T(8,128)(2,1)} %reshape_squeeze.31, s32[1024]{0:T(1024)S(1)} %pad_clamp_fusion), kind=kCustom, calls=%fused_computation.7 | custom fusion | bytes 6291584 | tf_op jit(solution)/shard_map/gather | solution.py:64
  271.6 5.0 %fusion.7 = f32[16,6,64,128]{3,2,1,0:T(8,128)} fusion(bf16[16,128,6,128]{3,2,1,0:T(8,128)(2,1)} %bitcast.205, f32[16,6,128,64]{2,3,1,0:T(8,128)S(1)} %copy-done.2, f32[16,6,64]{2,1,0:T(8,128)S(1)} %get-tuple-element.28), kind=kOutput, calls=%fused_computation.18 | convolution fusion | flops 203685888 | bytes 9461760 | tf_op jit(solution)/shard_map/thqk,tkhd->thqd/dot_general | solution.py:76
  276.6 3.7 %fusion.33 = (f32[16,6,64]{2,1,0:T(8,128)S(1)}, f32[16,6,64]{2,1,0:T(8,128)S(1)}) fusion(f32[16,6,128,64]{2,3,1,0:T(8,128)S(1)} %copy-done.2, f32[16,6,64]{2,1,0:T(8,128)S(1)} %get-tuple-element.28, f32[16,6,64]{2,1,0:T(8,128)S(1)} %get-tuple-element.26, f32[16,6,128,64]{2,3,1,0:T(8,128)S(1)} %copy-done.1), kind=kLoop, calls=%fused_computation.54 | loop fusion | flops 4706304 | bytes 6389760 | tf_op jit(solution)/shard_map/reduce_sum | solution.py:74
  280.3 3.1 fusion.3
  286.2 4.8 %gather_fusion.4 = bf16[32,64,6,128]{3,2,1,0:T(8,128)(2,1)} fusion(bf16[16,64,6,128]{3,2,1,0:T(8,128)(2,1)} %reshape_squeeze.28, s32[1024]{0:T(1024)S(1)} %pad_clamp_fusion), kind=kCustom, calls=%fused_computation.4 | custom fusion | bytes 6291584 | tf_op jit(solution)/shard_map/gather | solution.py:64
  291.0 3.3 fusion.11
  294.3 3.9 %fusion.29 = (f32[16,6,64]{2,1,0:T(8,128)S(1)}, f32[16,6,64]{2,1,0:T(8,128)S(1)}) fusion(f32[16,6,128,64]{2,3,1,0:T(8,128)S(1)} %copy-done.5, f32[16,6,64]{2,1,0:T(8,128)S(1)} %get-tuple-element.32, f32[16,6,64]{2,1,0:T(8,128)S(1)} %get-tuple-element.30, f32[16,6,128,64]{2,3,1,0:T(8,128)S(1)} %copy-done), kind=kLoop, calls=%fused_computation.50 | loop fusion | flops 4706304 | bytes 6389760 | tf_op jit(solution)/shard_map/reduce_sum | solution.py:74
  298.5 9.9 %fusion.2 = bf16[16,64,6,128]{3,1,2,0:T(8,128)(2,1)S(1)} fusion(f32[16,6,64,128]{3,2,1,0:T(8,128)S(1)} %copy-done.9, f32[16,6,64,128]{3,2,1,0:T(8,128)S(1)} %copy-done.8, f32[16,6,64,128]{3,2,1,0:T(8,128)S(1)} %fusion.11, bf16[16,128,6,128]{3,2,1,0:T(8,128)(2,1)S(1)} %bitcast.215, f32[16,6,128,64]{2,3,1,0:T(8,128)S(1)} %copy-done.5, ...), kind=kOutput, calls=%fused_computation.12 | convolution fusion | flops 217055232 | bytes 17547328 | tf_op jit(solution)/shard_map/thqk,tkhd->thqd/dot_general | solution.py:76
  312.4 42.9 %all_to_all.61 = bf16[8,128,768]{2,1,0:T(8,128)(2,1)S(1)} all-to-all(bf16[8,128,768]{2,1,0:T(8,128)(2,1)} %convert_element_type.25), channel_id=1, replica_groups=mesh['tm'=4,'space'=8] {'space'}, dimensions={0} | all-to-all | bytes 3145728 | tf_op jit(solution)/shard_map/all_to_all | solution.py:90
  (55 shorter events, 37.5 us)
Async XLA Ops:
  6.5 10.0 %copy-start.10 = (bf16[128,6144]{1,0:T(8,128)(2,1)S(1)}, bf16[128,6144]{1,0:T(8,128)(2,1)}, u32[]{:S(2)}) copy-start(bf16[128,6144]{1,0:T(8,128)(2,1)} %param.7) | copy-start | bytes 4718596
  9.3 44.3 %all-to-all-start = ((bf16[128,8,6,128]{0,3,2,1:T(8,128)(2,1)}), bf16[128,8,6,128]{0,3,2,1:T(8,128)(2,1)S(1)}, u32[]{:S(2)}, u32[]{:S(2)}) async-start(bf16[128,8,6,128]{0,3,2,1:T(8,128)(2,1)} %bitcast.1), calls=%async_computation | async-start | bytes 3145728 | tf_op jit(solution)/shard_map/all_to_all | solution.py:33
  53.5 40.8 %all-to-all-start.1 = ((bf16[128,8,6,128]{0,3,2,1:T(8,128)(2,1)}), bf16[128,8,6,128]{0,3,2,1:T(8,128)(2,1)S(1)}, u32[]{:S(2)}, u32[]{:S(2)}) async-start(bf16[128,8,6,128]{0,3,2,1:T(8,128)(2,1)} %bitcast.4), calls=%async_computation.1 | async-start | bytes 3145728 | tf_op jit(solution)/shard_map/all_to_all | solution.py:36
  57.2 126.7 %all-gather.3.cloned.1.call-start = ((), (), s32[]{:S(2)}) async-start(), calls=%async_computation.4 | async-start | bytes 15728640 | tf_op jit(solution)/shard_map/all_gather | solution.py:53
  102.5 1.4 copy-start.11
  103.9 5.4 %copy-start.13 = (s32[1,16,2]{1,2,0:T(2,128)S(1)}, s32[1,16,2]{1,2,0:T(2,128)}, u32[]{:S(2)}) copy-start(s32[1,16,2]{1,2,0:T(2,128)} %param.8) | copy-start | bytes 388
  103.9 5.6 %copy-start.14 = (s32[1,16]{1,0:T(1,128)S(1)}, s32[1,16]{1,0:T(1,128)}, u32[]{:S(2)}) copy-start(s32[1,16]{1,0:T(1,128)} %param.9) | copy-start | bytes 196
  105.4 40.9 %all-to-all-start.2 = ((bf16[128,8,6,128]{0,3,2,1:T(8,128)(2,1)}), bf16[128,8,6,128]{0,3,2,1:T(8,128)(2,1)S(1)}, u32[]{:S(2)}, u32[]{:S(2)}) async-start(bf16[128,8,6,128]{0,3,2,1:T(8,128)(2,1)} %bitcast.10), calls=%async_computation.2 | async-start | bytes 3145728 | tf_op jit(solution)/shard_map/all_to_all | solution.py:30
  210.8 6.3 %copy-start.4 = (bf16[32,64,6,128]{3,2,1,0:T(8,128)(2,1)S(1)}, bf16[32,64,6,128]{3,2,1,0:T(8,128)(2,1)}, u32[]{:S(2)}) copy-start(bf16[32,64,6,128]{3,2,1,0:T(8,128)(2,1)} %gather_fusion) | copy-start | bytes 9437188
  266.8 4.8 %copy-start.2 = (f32[16,6,128,64]{2,3,1,0:T(8,128)S(1)}, f32[16,6,128,64]{2,3,1,0:T(8,128)}, u32[]{:S(2)}) copy-start(f32[16,6,128,64]{2,3,1,0:T(8,128)} %get-tuple-element.29) | copy-start | bytes 9437188
  271.6 5.0 %copy-start.1 = (f32[16,6,128,64]{2,3,1,0:T(8,128)S(1)}, f32[16,6,128,64]{2,3,1,0:T(8,128)}, u32[]{:S(2)}) copy-start(f32[16,6,128,64]{2,3,1,0:T(8,128)} %get-tuple-element.27) | copy-start | bytes 9437188
  276.6 3.7 %copy-start.3 = (bf16[32,64,6,128]{3,2,1,0:T(8,128)(2,1)S(1)}, bf16[32,64,6,128]{3,2,1,0:T(8,128)(2,1)}, u32[]{:S(2)}) copy-start(bf16[32,64,6,128]{3,2,1,0:T(8,128)(2,1)} %gather_fusion.7) | copy-start | bytes 9437188
  280.3 3.1 copy-start.6
  286.2 4.8 %copy-start = (f32[16,6,128,64]{2,3,1,0:T(8,128)S(1)}, f32[16,6,128,64]{2,3,1,0:T(8,128)}, u32[]{:S(2)}) copy-start(f32[16,6,128,64]{2,3,1,0:T(8,128)} %get-tuple-element.31) | copy-start | bytes 9437188
  291.0 3.3 copy-start.5
  291.0 7.3 %copy-start.12 = (pred[16]{0:T(512)(128)(4,1)S(1)}, pred[16]{0:T(512)(128)(4,1)}, u32[]{:S(2)}) copy-start(pred[16]{0:T(512)(128)(4,1)} %get-tuple-element.25) | copy-start | bytes 52
  291.0 7.5 %copy-start.9 = (f32[16,6,64,128]{3,2,1,0:T(8,128)S(1)}, f32[16,6,64,128]{3,2,1,0:T(8,128)}, u32[]{:S(2)}) copy-start(f32[16,6,64,128]{3,2,1,0:T(8,128)} %fusion.3) | copy-start | bytes 9437188
  294.3 4.2 %copy-start.7 = (bf16[32,64,6,128]{3,2,1,0:T(8,128)(2,1)S(1)}, bf16[32,64,6,128]{3,2,1,0:T(8,128)(2,1)}, u32[]{:S(2)}) copy-start(bf16[32,64,6,128]{3,2,1,0:T(8,128)(2,1)} %gather_fusion.4) | copy-start | bytes 9437188
  294.3 4.2 %copy-start.8 = (f32[16,6,64,128]{3,2,1,0:T(8,128)S(1)}, f32[16,6,64,128]{3,2,1,0:T(8,128)}, u32[]{:S(2)}) copy-start(f32[16,6,64,128]{3,2,1,0:T(8,128)} %fusion.7) | copy-start | bytes 9437188
Sparse Core Ops, SparseCore 0:
  102.6 81.1 all-gather.2
where the time goes:
time: 366 us; the launch traced here: 365 us
  waiting for transfers between devices  140 us (38%)
  local copies, waits for them, and re-layouts  99.4 us (27%)
  matrix products  43.8 us (12%)
  blocking collectives  42.9 us (12%)
  starting transfers between devices  14.7 us (4%)
  between operations  13.6 us (4%)
  other arithmetic  10.6 us (3%)
    all_to_all x1, blocking collectives, body(): lax.all_to_all(flat_out, 'space', split_axis=0, concat_axis=1, tiled=True)  42.9 us
    all_gather x1, waiting for transfers between devices, body(): pieces = lax.all_gather(stacked[None], 'tm', axis=0, tiled=True)  36.6 us
    all_to_all x1, waiting for transfers between devices, body(): lax.all_to_all(queries.reshape(shape_split), 'space', split_axis=1, conca...  36.2 us
    all_to_all x1, waiting for transfers between devices, body(): lax.all_to_all(key_rows.reshape(shape_split), 'space', split_axis=1, conc...  35.4 us
    all_to_all x1, waiting for transfers between devices, body(): lax.all_to_all(value_rows.reshape(shape_split), 'space', split_axis=1, co...  31.3 us
    dot_general x4, matrix products, body(): jnp.einsum('tqhd,tkhd->thqk', query_tiles, key_sel, preferred_element_typ...  22.5 us
    dot_general x4, matrix products, body(): jnp.einsum('thqk,tkhd->thqd', weights, value_sel, preferred_element_type=...  21.3 us
    gather x4, local copies, waits for them, and re-layouts, body(): piece_stacked[0].reshape(tiles, TILE, heads_here, DH)[lists]  18.5 us
  transfers between devices with their start and end apart: 4, of which 4 were waited for; matrix products, arithmetic and copies ran while one was open for 3% of the time, Pallas kernels for 0%

commit v1 on v0

v1 whole, which is shorter than its diff:
```python
import functools
import math

import jax
import jax.numpy as jnp
from jax import lax
from jax.experimental import pallas as pl
from jax.experimental.pallas import tpu as pltpu
from jax.sharding import Mesh, PartitionSpec as P

DH = 128
TILE = 64
CORES = 2
EXP2_SCALE = DH ** (-0.5) * math.log2(math.e)
MASKED = -1e30
VMEM = pl.BlockSpec(memory_space=pltpu.VMEM)
SMEM = pl.BlockSpec(memory_space=pltpu.SMEM)


def pack_kernel(pieces, *refs):
    sources, out = refs[:-1], refs[-1]
    ways, _, width = out.shape
    for way in range(ways):
        row = 0
        for source, (start, rows) in zip(sources, pieces):
            out[way, pl.ds(row, rows), :] = source[pl.ds(start, rows), pl.ds(way * width, width)]
            row += rows


def pack(ways, sources, pieces):
    width = sources[0].shape[1] // ways
    rows = sum(count for _, count in pieces)
    return pl.pallas_call(
        functools.partial(pack_kernel, pieces),
        in_specs=[VMEM] * len(sources),
        out_specs=VMEM,
        out_shape=jax.ShapeDtypeStruct((ways, rows, width), sources[0].dtype),
        compiler_params=pltpu.CompilerParams(vmem_limit_bytes=24 * 2**20),
        cost_estimate=pl.CostEstimate(flops=0, bytes_accessed=4 * ways * rows * width, transcendentals=0),
        name="pack",
    )(*sources)


def attend_kernel(plan, table, own, swapped, q, o):
    groups, spans, rows, q_start = plan
    ways, _, width = o.shape
    per_device = rows // TILE
    kv = (own, swapped)

    def place_of(j, back, which):
        span = jnp.maximum(table[0, j] - back, 0)
        tile = table[1 + which, j]
        start = pl.multiple_of(tile % per_device * TILE, TILE)
        return span // CORES * groups + tile // per_device, start

    def pair(step, carry):
        tiles = (2 * step, 2 * step + 1)
        counts = [table[0, j] - table[3, j] + 1 for j in tiles]
        most = jnp.maximum(counts[0], counts[1])
        for many in range(1, spans + 1):

            @pl.when(most == many)
            def _(many=many):
                lane = lax.broadcasted_iota(jnp.int32, (1, many * 2 * TILE), 1)
                chains = []
                for j, count in zip(tiles, counts):
                    places = [(back % 2, *place_of(j, back, which)) for back in range(many) for which in range(2)]
                    for head in range(width // DH):
                        chains.append((j, places, lane < count * (2 * TILE), pl.ds(head * DH, DH)))

                def gather(first, places, cols):
                    return jnp.concatenate(
                        [kv[odd][at, pl.ds(start + first, TILE), cols] for odd, at, start in places], axis=0
                    )

                scores = [
                    lax.dot_general(
                        q[j, pl.ds(q_start, TILE), cols],
                        gather(0, places, cols),
                        (((1,), (1,)), ((), ())),
                        preferred_element_type=jnp.float32,
                    )
                    for j, places, _, cols in chains
                ]
                scores = [jnp.where(valid, s, MASKED) for s, (_, _, valid, _) in zip(scores, chains)]
                tops = [jnp.max(s, axis=-1, keepdims=True) for s in scores]
                expos = [jnp.exp2((s - top) * EXP2_SCALE) for s, top in zip(scores, tops)]
                totals = [jnp.sum(expo, axis=-1, keepdims=True) for expo in expos]
                partials = [
                    jnp.dot(
                        expo.astype(jnp.bfloat16), gather(rows, places, cols), preferred_element_type=jnp.float32
                    )
                    for expo, (_, places, _, cols) in zip(expos, chains)
                ]
                results = [(partial * (1.0 / total)).astype(o.dtype) for partial, total in zip(partials, totals)]
                for result, (j, _, _, cols) in zip(results, chains):
                    o[j, :, cols] = result

        return carry

    lax.fori_loop(0, ways // 2, pair, 0)


def attend(chips, groups, rows, table, own, swapped, q, q_start):
    ways, _, width = q.shape
    spans = chips * CORES
    keys = spans * TILE
    return pl.pallas_call(
        functools.partial(attend_kernel, (groups, spans, rows, q_start)),
        in_specs=[SMEM, VMEM, VMEM, VMEM],
        out_specs=VMEM,
        out_shape=jax.ShapeDtypeStruct((ways, TILE, width), q.dtype),
        compiler_params=pltpu.CompilerParams(vmem_limit_bytes=24 * 2**20),
        cost_estimate=pl.CostEstimate(
            flops=4 * ways * TILE * width * keys,
            bytes_accessed=4 * own.size + 4 * ways * TILE * width,
            transcendentals=ways * TILE * width // DH * keys,
        ),
        name="attend",
    )(table, own, swapped, q)


def body(queries, key_rows, value_rows, tile_lists, span_reach):
    chips = lax.axis_size("y")
    groups = lax.axis_size("space")
    rows, depth = queries.shape
    heads_group = depth // DH // groups
    core = lax.axis_index("core")
    chip = lax.axis_index("y")

    split_y = heads_group % chips == 0
    axes = ("y", "space") if split_y else ("space",)
    ways = chips * groups if split_y else groups
    width = depth // ways
    per_device = rows // TILE

    def exchange(x):
        return lax.all_to_all(x, axes, split_axis=0, concat_axis=0, tiled=True)

    table = jnp.concatenate([tile_lists[0], span_reach[0][:, None]], axis=1)
    if split_y:
        parts = [table]
        for step in range(1, chips):
            parts.append(lax.ppermute(table, "y", [(i, i ^ step) for i in range(chips)]))
        spans = jnp.arange(chips, dtype=jnp.int32)
        table = jnp.stack(parts)[spans ^ chip]
        spans = spans * CORES + core
    else:
        table = table[None]
        spans = (chip * CORES + core)[None]
    table = jnp.concatenate([jnp.broadcast_to(spans[:, None, None], table.shape[:2] + (1,)), table], axis=2)
    table = table.reshape(-1, per_device, 4).astype(jnp.int32)

    first = exchange(pack(ways, [key_rows, value_rows, queries], [(0, rows), (0, rows), (0, TILE)]))
    own = first if split_y else lax.all_gather(first, "y", axis=0, tiled=True)
    swapped = lax.ppermute(own, "core", [(0, 1), (1, 0)])
    q, q_start = first, 2 * rows
    outs = []
    for part in range(per_device):
        if part:
            q, q_start = exchange(pack(ways, [queries], [(part * TILE, TILE)])), 0
        out = attend(chips, groups, rows, table[:, part].T, own, swapped, q, q_start)
        outs.append(exchange(out).transpose(1, 0, 2).reshape(TILE, depth))
    return jnp.concatenate(outs, axis=0)


def solution(mesh):
    tm, groups = mesh.shape["tm"], mesh.shape["space"]
    fine = Mesh(mesh.devices.reshape(tm // CORES, CORES, groups), ("y", "core", "space"))
    rows = P(("y", "core", "space"), None)
    in_specs = (rows, rows, rows, P(("y", "core"), None, None), P(("y", "core"), None))
    return jax.shard_map(body, mesh=fine, in_specs=in_specs, out_specs=rows, check_vma=False)
```

time: 366 us -> 177 us (0.48)
  waiting for transfers between devices: 140 us -> 39.5 us
  local copies, waits for them, and re-layouts: 99.4 us -> 5.3 us
  blocking collectives: 42.9 us -> 96.9 us
  matrix products: 43.8 us -> 0 us
  Pallas kernels: 0 us -> 20.2 us
  between operations: 13.6 us -> 0.1 us
  other arithmetic: 10.6 us -> 1.3 us
    all_to_all x3, waiting for transfers between devices: 103 us -> 34.2 us  [exchange(): return lax.all_to_all(x, axes, split_axis=0, concat_axis=0, tiled=True)]
    all_to_all x1, blocking collectives: 42.9 us -> 96.9 us  [exchange(): return lax.all_to_all(x, axes, split_axis=0, concat_axis=0, tiled=True)]
    dot_general x8 -> x0, matrix products: 43.8 us -> none  [the longest x4 22.5 us: body(): jnp.einsum('tqhd,tkhd->thqk', query_tiles, key_sel, preferred_element_typ...]
    another operation x11 -> x0, local copies, waits for them, and re-layouts: 38.2 us -> none  [the longest x4 15.7 us: body(): key_sel = piece_stacked[0].reshape(tiles, TILE, heads_here, DH)[lists].re...]
    all_gather x1 -> x0, waiting for transfers between devices: 36.6 us -> none  [body(): pieces = lax.all_gather(stacked[None], 'tm', axis=0, tiled=True)]
    gather x8 -> x1, local copies, waits for them, and re-layouts: 34.2 us -> 0.57 us  [body(): table = jnp.stack(parts)[spans ^ chip]]
    pallas_call x0 -> x4, Pallas kernels: none -> 20.2 us  [the longest x2 18.8 us: attend(): pl.pallas_call(functools.partial(attend_kernel, (groups, spans, rows, q_s...]
    slice x1 -> x3, local copies, waits for them, and re-layouts: 9.06 us -> 0.17 us  [body(): table[:, part]]
  transfers between devices with their start and end apart: 4 -> 5, of which waited for: 4 -> 4; matrix products, arithmetic and copies ran while one was open for 3% -> 1% of each run, Pallas kernels for 0% -> 11%
where the time goes in v1:
time: 177 us; the launch traced here: 176 us
  blocking collectives  96.9 us (55%)
  waiting for transfers between devices  39.5 us (22%)
  Pallas kernels  20.2 us (11%)
  starting transfers between devices  13 us (7%)
  local copies, waits for them, and re-layouts  5.3 us (3%)
    all_to_all x1, blocking collectives, exchange(): return lax.all_to_all(x, axes, split_axis=0, concat_axis=0, tiled=True)  96.9 us
    all_to_all x3, waiting for transfers between devices, exchange(): return lax.all_to_all(x, axes, split_axis=0, concat_axis=0, tiled=True)  34.2 us
    pallas_call x2, Pallas kernels, attend(): pl.pallas_call(functools.partial(attend_kernel, (groups, spans, rows, q_s...  18.8 us
    all_to_all x3, starting transfers between devices, exchange(): return lax.all_to_all(x, axes, split_axis=0, concat_axis=0, tiled=True)  11 us
    ppermute x1, waiting for transfers between devices, body(): lax.ppermute(table, 'y', [(i, i ^ step) for i in range(chips)])  5.25 us
    unnamed x10, local copies, waits for them, and re-layouts  4.23 us
  transfers between devices with their start and end apart: 5, of which 4 were waited for; matrix products, arithmetic and copies ran while one was open for 1% of the time, Pallas kernels for 11%

profile of v1, /device:TPU:0, one launch (start us, length us, event | category | flops | bytes accessed | tf_op | source)
XLA Modules:
  0.0 176.2 jit_solution(17117873070031674435)
XLA Ops:
  0.0 0.0 copy-start
  0.0 1.4 copy-done
  1.4 0.0 copy-start.1
  1.4 1.4 copy-done.1
  2.8 0.0 copy-start.2
  2.8 1.4 copy-done.2
  4.2 0.4 pack.2
  4.6 96.9 %all_to_all.20.own.q = bf16[16,320,384]{2,1,0:T(8,128)(2,1)} all-to-all(bf16[16,320,384]{2,1,0:T(8,128)(2,1)S(1)} %pack.2), channel_id=1, replica_groups=mesh['y'=2,'core'=2,'space'=8] {'y','space'}, dimensions={0} | all-to-all | bytes 7864320 | tf_op jit(solution)/shard_map/all_to_all | solution.py:138
  101.5 0.0 copy-start.3
  101.5 0.0 collective-permute-start.1
  101.5 0.9 pack.3
  102.5 3.6 %all-to-all-start.2 = ((bf16[16,64,384]{2,1,0:T(8,128)(2,1)}), bf16[16,64,384]{2,1,0:T(8,128)(2,1)S(1)}, u32[]{:S(2)}, u32[]{:S(2)}) async-start(bf16[16,64,384]{2,1,0:T(8,128)(2,1)} %pack.3), calls=%async_computation.2 | async-start | bytes 1572864 | tf_op jit(solution)/shard_map/all_to_all | solution.py:138
  106.1 0.0 copy-done.3
  106.1 0.0 copy-done.4
  106.1 1.9 %collective-permute-start = (s32[16,3]{0,1:T(4,128)S(1)}, s32[16,3]{0,1:T(4,128)S(1)}, u32[]{:S(2)}, u32[]{:S(2)}) collective-permute-start(s32[16,3]{0,1:T(4,128)S(1)} %get-tuple-element.8), channel_id=1, source_target_pairs={{0,16},{16,0},{1,17},{17,1},{2,18},{18,2},{3,19},{19,3},{4,20},{20... | collective-permute-start | bytes 584 | tf_op jit(solution)/shard_map/ppermute | solution.py:144
  108.1 5.3 %collective-permute-done = s32[16,3]{0,1:T(4,128)S(1)} collective-permute-done((s32[16,3]{0,1:T(4,128)S(1)}, s32[16,3]{0,1:T(4,128)S(1)}, u32[]{:S(2)}, u32[]{:S(2)}) %collective-permute-start) | collective-permute-done | bytes 224 | tf_op jit(solution)/shard_map/ppermute | solution.py:144
  113.3 0.6 gather_fusion
  113.9 0.1 broadcast_in_dim.2
  114.0 0.1 copy.9
  114.1 0.1 copy.10
  114.2 0.0 collective-permute-done.1.swapped
  114.2 10.1 %attend.2 = bf16[16,64,384]{2,1,0:T(8,128)(2,1)} custom-call(s32[4,16]{1,0:T(4,128)S(1)} %bitcast.21, bf16[16,320,384]{2,1,0:T(8,128)(2,1)} %all_to_all.20.own.q, bf16[16,320,384]{2,1,0:T(8,128)(2,1)} %collective-permute-done.1.swapped, bf16[16,320,384]{2,1,0:T(8,128)(2,1)} %all_to_all.20.own.q), custom_call_target="tpu_custom_call" | custom-call | flops 402653184 | bytes 9437184 | tf_op jit(solution)/shard_map/attend/pallas_call | solution.py:108
  124.3 3.3 %all-to-all-done.2.q = bf16[16,64,384]{2,1,0:T(8,128)(2,1)S(1)} async-done(((bf16[16,64,384]{2,1,0:T(8,128)(2,1)}), bf16[16,64,384]{2,1,0:T(8,128)(2,1)S(1)}, u32[]{:S(2)}, u32[]{:S(2)}) %all-to-all-start.2) | async-done | bytes 786464 | tf_op jit(solution)/shard_map/all_to_all | solution.py:138
  127.6 3.6 %all-to-all-start.1 = ((bf16[16,64,384]{2,1,0:T(8,128)(2,1)}), bf16[16,64,384]{2,1,0:T(8,128)(2,1)S(1)}, u32[]{:S(2)}, u32[]{:S(2)}) async-start(bf16[16,64,384]{2,1,0:T(8,128)(2,1)} %attend.2), calls=%async_computation.1 | async-start | bytes 1572864 | tf_op jit(solution)/shard_map/all_to_all | solution.py:138
  131.2 0.1 copy.12
  131.3 8.8 %attend.3 = bf16[16,64,384]{2,1,0:T(8,128)(2,1)} custom-call(s32[4,16]{1,0:T(4,128)S(1)} %bitcast.20, bf16[16,320,384]{2,1,0:T(8,128)(2,1)} %all_to_all.20.own.q, bf16[16,320,384]{2,1,0:T(8,128)(2,1)} %collective-permute-done.1.swapped, bf16[16,64,384]{2,1,0:T(8,128)(2,1)S(1)} %all-to-all-done.2.q), custom_call_target="tpu_custom_call" | custom-call | flops 402653184 | bytes 9437184 | tf_op jit(solution)/shard_map/attend/pallas_call | solution.py:108
  140.0 11.4 %all-to-all-done.1 = bf16[16,64,384]{2,1,0:T(8,128)(2,1)S(1)} async-done(((bf16[16,64,384]{2,1,0:T(8,128)(2,1)}), bf16[16,64,384]{2,1,0:T(8,128)(2,1)S(1)}, u32[]{:S(2)}, u32[]{:S(2)}) %all-to-all-start.1) | async-done | bytes 786464 | tf_op jit(solution)/shard_map/all_to_all | solution.py:138
  151.5 3.8 %all-to-all-start.3 = ((bf16[16,64,384]{2,1,0:T(8,128)(2,1)}), bf16[16,64,384]{2,1,0:T(8,128)(2,1)S(1)}, u32[]{:S(2)}, u32[]{:S(2)}) async-start(bf16[16,64,384]{2,1,0:T(8,128)(2,1)} %attend.3), calls=%async_computation.3 | async-start | bytes 1572864 | tf_op jit(solution)/shard_map/all_to_all | solution.py:138
  155.3 0.1 copy.14
  155.4 19.5 %all-to-all-done.3 = bf16[16,64,384]{2,1,0:T(8,128)(2,1)S(1)} async-done(((bf16[16,64,384]{2,1,0:T(8,128)(2,1)}), bf16[16,64,384]{2,1,0:T(8,128)(2,1)S(1)}, u32[]{:S(2)}, u32[]{:S(2)}) %all-to-all-start.3) | async-done | bytes 786464 | tf_op jit(solution)/shard_map/all_to_all | solution.py:138
  174.8 0.1 copy.15
  174.9 1.3 pad_maximum_fusion
  (8 shorter events, 0.1 us)
Async XLA Ops:
  0.0 1.4 copy-start
  1.4 1.4 copy-start.1
  2.8 1.4 copy-start.2
  101.5 4.6 %copy-start.3 = (s32[1,16,2]{1,2,0:T(2,128)S(1)}, s32[1,16,2]{1,2,0:T(2,128)}, u32[]{:S(2)}) copy-start(s32[1,16,2]{1,2,0:T(2,128)} %param.8) | copy-start | bytes 388
  101.5 4.6 %copy-start.4 = (s32[1,16]{1,0:T(1,128)S(1)}, s32[1,16]{1,0:T(1,128)}, u32[]{:S(2)}) copy-start(s32[1,16]{1,0:T(1,128)} %param.9) | copy-start | bytes 196
  101.5 12.7 %collective-permute-start.1 = (bf16[16,320,384]{2,1,0:T(8,128)(2,1)}, bf16[16,320,384]{2,1,0:T(8,128)(2,1)}, u32[]{:S(2)}, u32[]{:S(2)}) collective-permute-start(bf16[16,320,384]{2,1,0:T(8,128)(2,1)} %all_to_all.20.own.q), channel_id=1, source_target_pairs={{0,8},{8,0},{1,9},{9,1},{2,10},{10,2},{3,11},{11,3},{4,12},{12,4},... | collective-permute-start | bytes 11796488 | tf_op jit(solution)/shard_map/ppermute | solution.py:156
  102.5 25.1 %all-to-all-start.2 = ((bf16[16,64,384]{2,1,0:T(8,128)(2,1)}), bf16[16,64,384]{2,1,0:T(8,128)(2,1)S(1)}, u32[]{:S(2)}, u32[]{:S(2)}) async-start(bf16[16,64,384]{2,1,0:T(8,128)(2,1)} %pack.3), calls=%async_computation.2 | async-start | bytes 1572864 | tf_op jit(solution)/shard_map/all_to_all | solution.py:138
  106.1 7.2 %collective-permute-start = (s32[16,3]{0,1:T(4,128)S(1)}, s32[16,3]{0,1:T(4,128)S(1)}, u32[]{:S(2)}, u32[]{:S(2)}) collective-permute-start(s32[16,3]{0,1:T(4,128)S(1)} %get-tuple-element.8), channel_id=1, source_target_pairs={{0,16},{16,0},{1,17},{17,1},{2,18},{18,2},{3,19},{19,3},{4,20},{20... | collective-permute-start | bytes 584 | tf_op jit(solution)/shard_map/ppermute | solution.py:144
  127.6 23.9 %all-to-all-start.1 = ((bf16[16,64,384]{2,1,0:T(8,128)(2,1)}), bf16[16,64,384]{2,1,0:T(8,128)(2,1)S(1)}, u32[]{:S(2)}, u32[]{:S(2)}) async-start(bf16[16,64,384]{2,1,0:T(8,128)(2,1)} %attend.2), calls=%async_computation.1 | async-start | bytes 1572864 | tf_op jit(solution)/shard_map/all_to_all | solution.py:138
  151.5 23.4 %all-to-all-start.3 = ((bf16[16,64,384]{2,1,0:T(8,128)(2,1)}), bf16[16,64,384]{2,1,0:T(8,128)(2,1)S(1)}, u32[]{:S(2)}, u32[]{:S(2)}) async-start(bf16[16,64,384]{2,1,0:T(8,128)(2,1)} %attend.3), calls=%async_computation.3 | async-start | bytes 1572864 | tf_op jit(solution)/shard_map/all_to_all | solution.py:138

commit v2 on v1

--- a/solution.py
+++ b/solution.py
@@ -11,38 +11,42 @@
 DH = 128
 TILE = 64
 CORES = 2
+HALVES = 2
 EXP2_SCALE = DH ** (-0.5) * math.log2(math.e)
 MASKED = -1e30
 VMEM = pl.BlockSpec(memory_space=pltpu.VMEM)
 SMEM = pl.BlockSpec(memory_space=pltpu.SMEM)
 
 
-def pack_kernel(pieces, *refs):
-    sources, out = refs[:-1], refs[-1]
-    ways, _, width = out.shape
+def pack_kernel(k, v, q, first, *later):
+    ways, _, width = first.shape
+    rows = k.shape[0]
     for way in range(ways):
-        row = 0
-        for source, (start, rows) in zip(sources, pieces):
-            out[way, pl.ds(row, rows), :] = source[pl.ds(start, rows), pl.ds(way * width, width)]
-            row += rows
+        cols = pl.ds(way * width, width)
+        first[way, pl.ds(0, rows), :] = k[:, cols]
+        first[way, pl.ds(rows, rows), :] = v[:, cols]
+        first[way, pl.ds(2 * rows, TILE), :] = q[pl.ds(0, TILE), cols]
+        for part, out in enumerate(later):
+            out[way] = q[pl.ds((part + 1) * TILE, TILE), cols]
 
 
-def pack(ways, sources, pieces):
-    width = sources[0].shape[1] // ways
-    rows = sum(count for _, count in pieces)
+def pack(ways, k, v, q):
+    rows, depth = k.shape
+    width = depth // ways
+    shapes = [(ways, 2 * rows + TILE, width)] + [(ways, TILE, width)] * (rows // TILE - 1)
     return pl.pallas_call(
-        functools.partial(pack_kernel, pieces),
-        in_specs=[VMEM] * len(sources),
-        out_specs=VMEM,
-        out_shape=jax.ShapeDtypeStruct((ways, rows, width), sources[0].dtype),
+        pack_kernel,
+        in_specs=[VMEM] * 3,
+        out_specs=[VMEM] * len(shapes),
+        out_shape=[jax.ShapeDtypeStruct(shape, k.dtype) for shape in shapes],
         compiler_params=pltpu.CompilerParams(vmem_limit_bytes=24 * 2**20),
-        cost_estimate=pl.CostEstimate(flops=0, bytes_accessed=4 * ways * rows * width, transcendentals=0),
+        cost_estimate=pl.CostEstimate(flops=0, bytes_accessed=12 * k.size, transcendentals=0),
         name="pack",
-    )(*sources)
+    )(k, v, q)
 
 
 def attend_kernel(plan, table, own, swapped, q, o):
-    groups, spans, rows, q_start = plan
+    rest, spans, rows, q_start = plan
     ways, _, width = o.shape
     per_device = rows // TILE
     kv = (own, swapped)
@@ -51,7 +55,9 @@
         span = jnp.maximum(table[0, j] - back, 0)
         tile = table[1 + which, j]
         start = pl.multiple_of(tile % per_device * TILE, TILE)
-        return span // CORES * groups + tile // per_device, start
+        group = tile // per_device
+        place = (span // CORES * rest + group % rest) * HALVES + group // rest
+        return place, start
 
     def pair(step, carry):
         tiles = (2 * step, 2 * step + 1)
@@ -101,12 +107,12 @@
     lax.fori_loop(0, ways // 2, pair, 0)
 
 
-def attend(chips, groups, rows, table, own, swapped, q, q_start):
+def attend(chips, rest, rows, table, own, swapped, q, q_start):
     ways, _, width = q.shape
     spans = chips * CORES
     keys = spans * TILE
     return pl.pallas_call(
-        functools.partial(attend_kernel, (groups, spans, rows, q_start)),
+        functools.partial(attend_kernel, (rest, spans, rows, q_start)),
         in_specs=[SMEM, VMEM, VMEM, VMEM],
         out_specs=VMEM,
         out_shape=jax.ShapeDtypeStruct((ways, TILE, width), q.dtype),
@@ -122,14 +128,15 @@
 
 def body(queries, key_rows, value_rows, tile_lists, span_reach):
     chips = lax.axis_size("y")
-    groups = lax.axis_size("space")
+    rest = lax.axis_size("rest")
+    groups = HALVES * rest
     rows, depth = queries.shape
     heads_group = depth // DH // groups
     core = lax.axis_index("core")
     chip = lax.axis_index("y")
 
     split_y = heads_group % chips == 0
-    axes = ("y", "space") if split_y else ("space",)
+    axes = ("y", "rest", "half") if split_y else ("rest", "half")
     ways = chips * groups if split_y else groups
     width = depth // ways
     per_device = rows // TILE
@@ -149,24 +156,26 @@
         table = table[None]
         spans = (chip * CORES + core)[None]
     table = jnp.concatenate([jnp.broadcast_to(spans[:, None, None], table.shape[:2] + (1,)), table], axis=2)
+    table = table.reshape(-1, HALVES, rest, per_device, 4).transpose(0, 2, 1, 3, 4)
     table = table.reshape(-1, per_device, 4).astype(jnp.int32)
 
-    first = exchange(pack(ways, [key_rows, value_rows, queries], [(0, rows), (0, rows), (0, TILE)]))
+    packed = pack(ways, key_rows, value_rows, queries)
+    first = exchange(packed[0])
     own = first if split_y else lax.all_gather(first, "y", axis=0, tiled=True)
     swapped = lax.ppermute(own, "core", [(0, 1), (1, 0)])
     q, q_start = first, 2 * rows
     outs = []
     for part in range(per_device):
         if part:
-            q, q_start = exchange(pack(ways, [queries], [(part * TILE, TILE)])), 0
-        out = attend(chips, groups, rows, table[:, part].T, own, swapped, q, q_start)
+            q, q_start = exchange(packed[part]), 0
+        out = attend(chips, rest, rows, table[:, part].T, own, swapped, q, q_start)
         outs.append(exchange(out).transpose(1, 0, 2).reshape(TILE, depth))
     return jnp.concatenate(outs, axis=0)
 
 
 def solution(mesh):
     tm, groups = mesh.shape["tm"], mesh.shape["space"]
-    fine = Mesh(mesh.devices.reshape(tm // CORES, CORES, groups), ("y", "core", "space"))
-    rows = P(("y", "core", "space"), None)
+    fine = Mesh(mesh.devices.reshape(tm // CORES, CORES, HALVES, groups // HALVES), ("y", "core", "half", "rest"))
+    rows = P(("y", "core", "half", "rest"), None)
     in_specs = (rows, rows, rows, P(("y", "core"), None, None), P(("y", "core"), None))
     return jax.shard_map(body, mesh=fine, in_specs=in_specs, out_specs=rows, check_vma=False)

time: 177 us -> 176 us (level)
  waiting for transfers between devices: 39.5 us -> 37.7 us
    pallas_call x4 -> x3, Pallas kernels: 20.2 us -> 19.9 us  [the longest x2 18.6 us: attend(): pl.pallas_call(functools.partial(attend_kernel, (rest, spans, rows, q_sta...]
where the time goes in v2:
time: 176 us
  blocking collectives  96.9 us (55%)
  waiting for transfers between devices  37.7 us (21%)
  Pallas kernels  19.9 us (11%)
  starting transfers between devices  14.5 us (8%)
  local copies, waits for them, and re-layouts  5.3 us (3%)
    all_to_all x1, blocking collectives, exchange(): return lax.all_to_all(x, axes, split_axis=0, concat_axis=0, tiled=True)  96.9 us
    all_to_all x3, waiting for transfers between devices, exchange(): return lax.all_to_all(x, axes, split_axis=0, concat_axis=0, tiled=True)  33.6 us
    pallas_call x2, Pallas kernels, attend(): pl.pallas_call(functools.partial(attend_kernel, (rest, spans, rows, q_sta...  18.6 us
    all_to_all x3, starting transfers between devices, exchange(): return lax.all_to_all(x, axes, split_axis=0, concat_axis=0, tiled=True)  12.5 us
    unnamed x10, local copies, waits for them, and re-layouts  4.23 us
    ppermute x1, waiting for transfers between devices, body(): lax.ppermute(table, 'y', [(i, i ^ step) for i in range(chips)])  4.12 us
  transfers between devices with their start and end apart: 5, of which 4 were waited for; matrix products, arithmetic and copies ran while one was open for 1% of the time, Pallas kernels for 11%

profile of v2, /device:TPU:0, one launch (start us, length us, event | category | flops | bytes accessed | tf_op | source)
XLA Modules:
  0.0 175.6 jit_solution(7634840072647533510)
XLA Ops:
  0.0 0.0 copy-start
  0.0 1.4 copy-done
  1.4 0.0 copy-start.1
  1.4 1.4 copy-done.1
  2.8 0.0 copy-start.2
  2.8 1.4 copy-done.2
  4.2 1.3 pack.1
  5.5 96.9 %all_to_all.20.own.q = bf16[16,320,384]{2,1,0:T(8,128)(2,1)} all-to-all(bf16[16,320,384]{2,1,0:T(8,128)(2,1)S(1)} %get-tuple-element.7), channel_id=1, replica_groups=mesh['y'=2,'core'=2,'half'=2,'rest'=4] {'y','rest','half'}, dimensions={0} | all-to-all | bytes 7864320 | tf_op jit(solution)/shard_map/all_to_all | solution.py:145
  102.4 0.0 copy-start.3
  102.4 0.0 copy-start.4
  102.4 0.0 collective-permute-start.1
  102.4 3.9 %all-to-all-start.2 = ((bf16[16,64,384]{2,1,0:T(8,128)(2,1)}), bf16[16,64,384]{2,1,0:T(8,128)(2,1)S(1)}, u32[]{:S(2)}, u32[]{:S(2)}) async-start(bf16[16,64,384]{2,1,0:T(8,128)(2,1)} %get-tuple-element.8), calls=%async_computation.2 | async-start | bytes 1572864 | tf_op jit(solution)/shard_map/all_to_all | solution.py:145
  106.3 0.0 copy-done.3
  106.3 0.0 copy-done.4
  106.3 2.0 %collective-permute-start = (s32[16,3]{0,1:T(4,128)S(1)}, s32[16,3]{0,1:T(4,128)S(1)}, u32[]{:S(2)}, u32[]{:S(2)}) collective-permute-start(s32[16,3]{0,1:T(4,128)S(1)} %get-tuple-element.12), channel_id=1, source_target_pairs={{0,16},{16,0},{1,17},{17,1},{2,18},{18,2},{3,19},{19,3},{4,20},{20... | collective-permute-start | bytes 584 | tf_op jit(solution)/shard_map/ppermute | solution.py:151
  108.3 4.1 %collective-permute-done = s32[16,3]{0,1:T(4,128)S(1)} collective-permute-done((s32[16,3]{0,1:T(4,128)S(1)}, s32[16,3]{0,1:T(4,128)S(1)}, u32[]{:S(2)}, u32[]{:S(2)}) %collective-permute-start) | collective-permute-done | bytes 224 | tf_op jit(solution)/shard_map/ppermute | solution.py:151
  112.4 0.6 gather_fusion
  113.0 0.1 broadcast_in_dim.2
  113.1 0.1 copy.10
  113.2 0.1 copy.12
  113.3 0.0 collective-permute-done.1.swapped
  113.3 9.9 %attend.2 = bf16[16,64,384]{2,1,0:T(8,128)(2,1)} custom-call(s32[4,16]{1,0:T(4,128)S(1)} %bitcast.24, bf16[16,320,384]{2,1,0:T(8,128)(2,1)} %all_to_all.20.own.q, bf16[16,320,384]{2,1,0:T(8,128)(2,1)} %collective-permute-done.1.swapped, bf16[16,320,384]{2,1,0:T(8,128)(2,1)} %all_to_all.20.own.q), custom_call_target="tpu_custom_call" | custom-call | flops 402653184 | bytes 9437184 | tf_op jit(solution)/shard_map/attend/pallas_call | solution.py:114
  123.2 4.1 %all-to-all-done.2.q = bf16[16,64,384]{2,1,0:T(8,128)(2,1)S(1)} async-done(((bf16[16,64,384]{2,1,0:T(8,128)(2,1)}), bf16[16,64,384]{2,1,0:T(8,128)(2,1)S(1)}, u32[]{:S(2)}, u32[]{:S(2)}) %all-to-all-start.2) | async-done | bytes 786464 | tf_op jit(solution)/shard_map/all_to_all | solution.py:145
  127.3 4.3 %all-to-all-start.1 = ((bf16[16,64,384]{2,1,0:T(8,128)(2,1)}), bf16[16,64,384]{2,1,0:T(8,128)(2,1)S(1)}, u32[]{:S(2)}, u32[]{:S(2)}) async-start(bf16[16,64,384]{2,1,0:T(8,128)(2,1)} %attend.2), calls=%async_computation.1 | async-start | bytes 1572864 | tf_op jit(solution)/shard_map/all_to_all | solution.py:145
  131.6 0.1 copy.14
  131.7 8.7 %attend.3 = bf16[16,64,384]{2,1,0:T(8,128)(2,1)} custom-call(s32[4,16]{1,0:T(4,128)S(1)} %bitcast.23, bf16[16,320,384]{2,1,0:T(8,128)(2,1)} %all_to_all.20.own.q, bf16[16,320,384]{2,1,0:T(8,128)(2,1)} %collective-permute-done.1.swapped, bf16[16,64,384]{2,1,0:T(8,128)(2,1)S(1)} %all-to-all-done.2.q), custom_call_target="tpu_custom_call" | custom-call | flops 402653184 | bytes 9437184 | tf_op jit(solution)/shard_map/attend/pallas_call | solution.py:114
  140.4 10.9 %all-to-all-done.1 = bf16[16,64,384]{2,1,0:T(8,128)(2,1)S(1)} async-done(((bf16[16,64,384]{2,1,0:T(8,128)(2,1)}), bf16[16,64,384]{2,1,0:T(8,128)(2,1)S(1)}, u32[]{:S(2)}, u32[]{:S(2)}) %all-to-all-start.1) | async-done | bytes 786464 | tf_op jit(solution)/shard_map/all_to_all | solution.py:145
  151.3 4.3 %all-to-all-start.3 = ((bf16[16,64,384]{2,1,0:T(8,128)(2,1)}), bf16[16,64,384]{2,1,0:T(8,128)(2,1)S(1)}, u32[]{:S(2)}, u32[]{:S(2)}) async-start(bf16[16,64,384]{2,1,0:T(8,128)(2,1)} %attend.3), calls=%async_computation.3 | async-start | bytes 1572864 | tf_op jit(solution)/shard_map/all_to_all | solution.py:145
  155.6 0.1 copy.16
  155.7 18.6 %all-to-all-done.3 = bf16[16,64,384]{2,1,0:T(8,128)(2,1)S(1)} async-done(((bf16[16,64,384]{2,1,0:T(8,128)(2,1)}), bf16[16,64,384]{2,1,0:T(8,128)(2,1)S(1)}, u32[]{:S(2)}, u32[]{:S(2)}) %all-to-all-start.3) | async-done | bytes 786464 | tf_op jit(solution)/shard_map/all_to_all | solution.py:145
  174.3 0.1 copy.17
  174.3 1.3 pad_maximum_fusion
  (8 shorter events, 0.1 us)
Async XLA Ops:
  0.0 1.4 copy-start
  1.4 1.4 copy-start.1
  2.8 1.4 copy-start.2
  102.4 3.9 %copy-start.3 = (s32[1,16,2]{1,2,0:T(2,128)S(1)}, s32[1,16,2]{1,2,0:T(2,128)}, u32[]{:S(2)}) copy-start(s32[1,16,2]{1,2,0:T(2,128)} %param.8) | copy-start | bytes 388
  102.4 3.9 %copy-start.4 = (s32[1,16]{1,0:T(1,128)S(1)}, s32[1,16]{1,0:T(1,128)}, u32[]{:S(2)}) copy-start(s32[1,16]{1,0:T(1,128)} %param.9) | copy-start | bytes 196
  102.4 10.9 %collective-permute-start.1 = (bf16[16,320,384]{2,1,0:T(8,128)(2,1)}, bf16[16,320,384]{2,1,0:T(8,128)(2,1)}, u32[]{:S(2)}, u32[]{:S(2)}) collective-permute-start(bf16[16,320,384]{2,1,0:T(8,128)(2,1)} %all_to_all.20.own.q), channel_id=1, source_target_pairs={{0,8},{8,0},{1,9},{9,1},{2,10},{10,2},{3,11},{11,3},{4,12},{12,4},... | collective-permute-start | bytes 11796488 | tf_op jit(solution)/shard_map/ppermute | solution.py:165
  102.4 24.8 %all-to-all-start.2 = ((bf16[16,64,384]{2,1,0:T(8,128)(2,1)}), bf16[16,64,384]{2,1,0:T(8,128)(2,1)S(1)}, u32[]{:S(2)}, u32[]{:S(2)}) async-start(bf16[16,64,384]{2,1,0:T(8,128)(2,1)} %get-tuple-element.8), calls=%async_computation.2 | async-start | bytes 1572864 | tf_op jit(solution)/shard_map/all_to_all | solution.py:145
  106.3 6.1 %collective-permute-start = (s32[16,3]{0,1:T(4,128)S(1)}, s32[16,3]{0,1:T(4,128)S(1)}, u32[]{:S(2)}, u32[]{:S(2)}) collective-permute-start(s32[16,3]{0,1:T(4,128)S(1)} %get-tuple-element.12), channel_id=1, source_target_pairs={{0,16},{16,0},{1,17},{17,1},{2,18},{18,2},{3,19},{19,3},{4,20},{20... | collective-permute-start | bytes 584 | tf_op jit(solution)/shard_map/ppermute | solution.py:151
  127.3 24.1 %all-to-all-start.1 = ((bf16[16,64,384]{2,1,0:T(8,128)(2,1)}), bf16[16,64,384]{2,1,0:T(8,128)(2,1)S(1)}, u32[]{:S(2)}, u32[]{:S(2)}) async-start(bf16[16,64,384]{2,1,0:T(8,128)(2,1)} %attend.2), calls=%async_computation.1 | async-start | bytes 1572864 | tf_op jit(solution)/shard_map/all_to_all | solution.py:145
  151.3 22.9 %all-to-all-start.3 = ((bf16[16,64,384]{2,1,0:T(8,128)(2,1)}), bf16[16,64,384]{2,1,0:T(8,128)(2,1)S(1)}, u32[]{:S(2)}, u32[]{:S(2)}) async-start(bf16[16,64,384]{2,1,0:T(8,128)(2,1)} %attend.3), calls=%async_computation.3 | async-start | bytes 1572864 | tf_op jit(solution)/shard_map/all_to_all | solution.py:145

commit v3 on v2

v3 whole, which is shorter than its diff:
```python
import functools
import math

import jax
import jax.numpy as jnp
from jax import lax
from jax.experimental import pallas as pl
from jax.experimental.pallas import tpu as pltpu
from jax.sharding import Mesh, PartitionSpec as P

DH = 128
TILE = 64
CORES = 2
LAST = 32
EXP2_SCALE = DH ** (-0.5) * math.log2(math.e)
MASKED = -1e30
VMEM = pl.BlockSpec(memory_space=pltpu.VMEM)
SMEM = pl.BlockSpec(memory_space=pltpu.SMEM)


def pack_kernel(k, v, q, first, last):
    ways, _, width = first.shape
    rows, early = k.shape[0], q.shape[0] - last.shape[1]
    for way in range(ways):
        cols = pl.ds(way * width, width)
        first[way, pl.ds(0, rows), :] = k[:, cols]
        first[way, pl.ds(rows, rows), :] = v[:, cols]
        first[way, pl.ds(2 * rows, early), :] = q[pl.ds(0, early), cols]
        last[way] = q[pl.ds(early, q.shape[0] - early), cols]


def pack(ways, k, v, q):
    rows, depth = k.shape
    width = depth // ways
    shapes = [(ways, 3 * rows - LAST, width), (ways, LAST, width)]
    return pl.pallas_call(
        pack_kernel,
        in_specs=[VMEM] * 3,
        out_specs=[VMEM] * 2,
        out_shape=[jax.ShapeDtypeStruct(shape, k.dtype) for shape in shapes],
        compiler_params=pltpu.CompilerParams(vmem_limit_bytes=24 * 2**20),
        cost_estimate=pl.CostEstimate(flops=0, bytes_accessed=12 * k.size, transcendentals=0),
        name="pack",
    )(k, v, q)


def attend_kernel(plan, table, own, swapped, q, *refs):
    spans, rows, span_rows, ways, pieces = plan
    o = refs[-1]
    width = o.shape[-1]
    kv = (own, swapped)
    for done in refs[:-1]:
        o[:, pl.ds(0, done.shape[1]), :] = done[...]

    for part, q_start, q_rows, o_start in pieces:

        def pair(step, carry, part=part, q_start=q_start, q_rows=q_rows, o_start=o_start):
            tiles = (2 * step, 2 * step + 1)
            columns = [part * ways + j for j in tiles]
            counts = [table[4, column] for column in columns]
            most = jnp.maximum(counts[0], counts[1])

            def places_of(column, many):
                places = []
                for back in range(many):
                    start = jnp.maximum(table[back % 2, column] - back // 2 * span_rows, 0)
                    for which in range(2):
                        places.append((back % 2, pl.multiple_of(start + table[2 + which, column], LAST)))
                return places

            def gather(first, places, cols):
                return jnp.concatenate([kv[odd][pl.ds(at + first, TILE), cols] for odd, at in places], axis=0)

            for many in range(1, spans + 1):

                @pl.when(most == many)
                def _(many=many):
                    lane = lax.broadcasted_iota(jnp.int32, (1, many * 2 * TILE), 1)
                    chains = []
                    for j, column, count in zip(tiles, columns, counts):
                        places = places_of(column, many)
                        for head in range(width // DH):
                            chains.append((j, places, lane < count * (2 * TILE), pl.ds(head * DH, DH)))
                    scores = [
                        lax.dot_general(
                            q[j, pl.ds(q_start, q_rows), cols],
                            gather(0, places, cols),
                            (((1,), (1,)), ((), ())),
                            preferred_element_type=jnp.float32,
                        )
                        for j, places, _, cols in chains
                    ]
                    scores = [jnp.where(valid, s, MASKED) for s, (_, _, valid, _) in zip(scores, chains)]
                    tops = [jnp.max(s, axis=-1, keepdims=True) for s in scores]
                    expos = [jnp.exp2((s - top) * EXP2_SCALE) for s, top in zip(scores, tops)]
                    totals = [jnp.sum(expo, axis=-1, keepdims=True) for expo in expos]
                    partials = [
                        jnp.dot(
                            expo.astype(jnp.bfloat16),
                            gather(rows, places, cols),
                            preferred_element_type=jnp.float32,
                        )
                        for expo, (_, places, _, cols) in zip(expos, chains)
                    ]
                    results = [(partial * (1.0 / total)).astype(o.dtype) for partial, total in zip(partials, totals)]
                    for result, (j, _, _, cols) in zip(results, chains):
                        o[j, pl.ds(o_start, q_rows), cols] = result

            return carry

        lax.fori_loop(0, ways // 2, pair, 0)


def attend(spans, rows, span_rows, pieces, table, own, swapped, q, done=()):
    ways, _, width = q.shape
    own, swapped = own.reshape(-1, width), swapped.reshape(-1, width)
    out_rows = max(o_start + q_rows for _, _, q_rows, o_start in pieces)
    q_rows = sum(piece[2] for piece in pieces)
    keys = spans * TILE
    return pl.pallas_call(
        functools.partial(attend_kernel, (spans, rows, span_rows, ways, pieces)),
        in_specs=[SMEM] + [VMEM] * (3 + len(done)),
        out_specs=VMEM,
        out_shape=jax.ShapeDtypeStruct((ways, out_rows, width), q.dtype),
        compiler_params=pltpu.CompilerParams(vmem_limit_bytes=24 * 2**20),
        cost_estimate=pl.CostEstimate(
            flops=4 * ways * q_rows * width * keys,
            bytes_accessed=4 * own.size + 4 * ways * q_rows * width,
            transcendentals=ways * q_rows * width // DH * keys,
        ),
        name="attend",
    )(table, own, swapped, q, *done)


def body(queries, key_rows, value_rows, tile_lists, span_reach):
    chips = lax.axis_size("y")
    groups = lax.axis_size("space")
    rows, depth = queries.shape
    core = lax.axis_index("core")
    chip = lax.axis_index("y")

    split_y = depth // DH // groups % chips == 0
    axes = ("y", "space") if split_y else ("space",)
    ways = chips * groups if split_y else groups
    per_device = rows // TILE
    early = rows - LAST
    block_rows = 2 * rows + early
    span_rows = groups * block_rows

    def exchange(x):
        return lax.all_to_all(x, axes, split_axis=0, concat_axis=0, tiled=True)

    lists = jnp.concatenate([tile_lists[0], span_reach[0][:, None]], axis=1)
    lists = jnp.concatenate(
        [lists[:, :2] // per_device * block_rows + lists[:, :2] % per_device * TILE, lists[:, 2:]], axis=1
    )
    if split_y:
        parts = [lists]
        for step in range(1, chips):
            parts.append(lax.ppermute(lists, "y", [(i, i ^ step) for i in range(chips)]))
        chip_of = jnp.arange(chips, dtype=jnp.int32)
        lists = jnp.stack(parts)[chip_of ^ chip]
    else:
        lists = lists[None]
        chip_of = chip[None]
    span = chip_of * CORES + core
    begins = jnp.stack([chip_of, (span - 1) // CORES], axis=1) * span_rows
    begins = jnp.broadcast_to(begins[:, None, :], lists.shape[:2] + (2,))
    counts = span[:, None, None] - lists[:, :, 2:] + 1
    table = jnp.concatenate([begins, lists[:, :, :2], counts], axis=2)
    table = table.reshape(ways, per_device, 5).transpose(2, 1, 0).reshape(5, -1).astype(jnp.int32)

    first, last = pack(ways, key_rows, value_rows, queries)
    first = exchange(first)
    own = first if split_y else lax.all_gather(first, "y", axis=0, tiled=True)
    swapped = lax.ppermute(own, "core", [(0, 1), (1, 0)])
    last = exchange(last)
    run = functools.partial(attend, chips * CORES, rows, span_rows)
    pieces = [
        (part, 2 * rows + part * TILE, min(TILE, early - part * TILE), part * TILE)
        for part in range(per_device)
        if part * TILE < early
    ]
    done = run(pieces, table, own, swapped, first)
    out = run([(per_device - 1, 0, LAST, early)], table, own, swapped, last, [done])
    return exchange(out).transpose(1, 0, 2).reshape(rows, depth)


def solution(mesh):
    tm, groups = mesh.shape["tm"], mesh.shape["space"]
    fine = Mesh(mesh.devices.reshape(tm // CORES, CORES, groups), ("y", "core", "space"))
    rows = P(("y", "core", "space"), None)
    in_specs = (rows, rows, rows, P(("y", "core"), None, None), P(("y", "core"), None))
    return jax.shard_map(body, mesh=fine, in_specs=in_specs, out_specs=rows, check_vma=False)
```

time: 176 us -> 186 us (1.057)
  blocking collectives: 96.9 us -> 149 us
  waiting for transfers between devices: 37.7 us -> 1.9 us
  starting transfers between devices: 14.5 us -> 4.55 us
  local copies, waits for them, and re-layouts: 5.3 us -> 7.76 us
    all_to_all x1 -> x2, blocking collectives: 96.9 us -> 149 us  [exchange(): return lax.all_to_all(x, axes, split_axis=0, concat_axis=0, tiled=True)]
    all_to_all x3 -> x1, waiting for transfers between devices: 33.6 us -> 0.01 us  [exchange(): return lax.all_to_all(x, axes, split_axis=0, concat_axis=0, tiled=True)]
    all_to_all x3 -> x1, starting transfers between devices: 12.5 us -> 3.74 us  [exchange(): return lax.all_to_all(x, axes, split_axis=0, concat_axis=0, tiled=True)]
    ppermute x1, waiting for transfers between devices: 4.12 us -> 0.01 us  [body(): lax.ppermute(lists, 'y', [(i, i ^ step) for i in range(chips)])]
    ppermute x1, waiting for transfers between devices: 0.01 us -> 1.9 us  [body(): swapped = lax.ppermute(own, 'core', [(0, 1), (1, 0)])]
  transfers between devices with their start and end apart: 5 -> 3, of which waited for: 4 -> 1; matrix products, arithmetic and copies ran while one was open for 1% -> 1% of each run, Pallas kernels for 11% -> 7%
where the time goes in v3:
time: 186 us; the launch traced here: 185 us
  blocking collectives  149 us (80%)
  Pallas kernels  21.7 us (12%)
  local copies, waits for them, and re-layouts  7.76 us (4%)
  starting transfers between devices  4.55 us (2%)
  waiting for transfers between devices  1.9 us (1%)
    all_to_all x2, blocking collectives, exchange(): return lax.all_to_all(x, axes, split_axis=0, concat_axis=0, tiled=True)  149 us
    pallas_call x2, Pallas kernels, attend(): pl.pallas_call(functools.partial(attend_kernel, (spans, rows, span_rows,...  20.5 us
    unnamed x10, local copies, waits for them, and re-layouts  4.23 us
    all_to_all x1, starting transfers between devices, exchange(): return lax.all_to_all(x, axes, split_axis=0, concat_axis=0, tiled=True)  3.74 us
  transfers between devices with their start and end apart: 3, of which 1 were waited for; matrix products, arithmetic and copies ran while one was open for 1% of the time, Pallas kernels for 7%

profile of v3, /device:TPU:0, one launch (start us, length us, event | category | flops | bytes accessed | tf_op | source)
XLA Modules:
  0.0 185.0 jit_solution(3984291792673919692)
XLA Ops:
  0.0 0.0 copy-start
  0.0 1.4 copy-done
  1.4 0.0 copy-start.1
  1.4 1.4 copy-done.1
  2.8 0.0 copy-start.2
  2.8 1.4 copy-done.2
  4.2 1.2 pack.1
  5.4 0.0 copy-start.3
  5.4 0.0 copy-start.4
  5.4 105.7 %all_to_all.15.q = bf16[16,352,384]{2,1,0:T(8,128)(2,1)} all-to-all(bf16[16,352,384]{2,1,0:T(8,128)(2,1)S(1)} %get-tuple-element.7), channel_id=1, replica_groups=mesh['y'=2,'core'=2,'space'=8] {'y','space'}, dimensions={0} | all-to-all | bytes 8650752 | tf_op jit(solution)/shard_map/all_to_all | solution.py:151
  111.1 0.0 collective-permute-start.1
  111.1 0.0 copy-done.3
  111.2 0.0 copy-done.4
  111.2 0.8 collective-permute-start
  112.0 3.7 %all-to-all-start.1 = ((bf16[16,32,384]{2,1,0:T(8,128)(2,1)}), bf16[16,32,384]{2,1,0:T(8,128)(2,1)S(1)}, u32[]{:S(2)}, u32[]{:S(2)}) async-start(bf16[16,32,384]{2,1,0:T(8,128)(2,1)} %get-tuple-element.8), calls=%async_computation.1 | async-start | bytes 786432 | tf_op jit(solution)/shard_map/all_to_all | solution.py:151
  115.8 0.1 copy.7
  115.9 0.0 collective-permute-done
  115.9 0.6 gather_fusion
  116.5 0.1 fusion.2
  116.6 0.1 broadcast_in_dim.2
  116.7 0.1 copy.8
  116.8 0.1 copy.9
  116.9 0.1 reshape.110.table
  116.9 1.9 %collective-permute-done.1 = bf16[16,352,384]{2,1,0:T(8,128)(2,1)} collective-permute-done((bf16[16,352,384]{2,1,0:T(8,128)(2,1)}, bf16[16,352,384]{2,1,0:T(8,128)(2,1)}, u32[]{:S(2)}, u32[]{:S(2)}) %collective-permute-start.1) | collective-permute-done | bytes 4325408 | tf_op jit(solution)/shard_map/ppermute | solution.py:176
  118.8 13.0 %attend.2.refs_0_ = bf16[16,96,384]{2,1,0:T(8,128)(2,1)S(1)} custom-call(s32[5,32]{1,0:T(8,128)S(1)} %reshape.110.table, bf16[5632,384]{1,0:T(8,128)(2,1)} %bitcast.7.own, bf16[5632,384]{1,0:T(8,128)(2,1)} %bitcast.8.swapped, bf16[16,352,384]{2,1,0:T(8,128)(2,1)} %all_to_all.15.q), custom_call_target="tpu_custom_call" | custom-call | flops 603979776 | bytes 11010048 | tf_op jit(solution)/shard_map/attend/pallas_call | solution.py:120
  131.9 0.0 all-to-all-done.1.q
  131.9 7.5 %attend.3 = bf16[16,128,384]{2,1,0:T(8,128)(2,1)S(1)} custom-call(s32[5,32]{1,0:T(8,128)S(1)} %reshape.110.table, bf16[5632,384]{1,0:T(8,128)(2,1)} %bitcast.7.own, bf16[5632,384]{1,0:T(8,128)(2,1)} %bitcast.8.swapped, bf16[16,32,384]{2,1,0:T(8,128)(2,1)S(1)} %all-to-all-done.1.q, bf16[16,96,384]{2,1,0:T(8,128)(2,1)S(1)} %attend.2.refs_0_), custom_call_target="tpu_custom_call" | custom-call | flops 201326592 | bytes 9437184 | tf_op jit(solution)/shard_map/attend/pallas_call | solution.py:120
  139.3 43.1 %all_to_all.16 = bf16[16,128,384]{2,1,0:T(8,128)(2,1)S(1)} all-to-all(bf16[16,128,384]{2,1,0:T(8,128)(2,1)S(1)} %attend.3), channel_id=1, replica_groups=mesh['y'=2,'core'=2,'space'=8] {'y','space'}, dimensions={0} | all-to-all | bytes 3145728 | tf_op jit(solution)/shard_map/all_to_all | solution.py:151
  182.5 0.9 copy.10
  183.4 1.6 copy.11
  (11 shorter events, 0.1 us)
Async XLA Ops:
  0.0 1.4 copy-start
  1.4 1.4 copy-start.1
  2.8 1.4 copy-start.2
  5.4 105.7 %copy-start.3 = (s32[1,16,2]{1,2,0:T(2,128)S(1)}, s32[1,16,2]{1,2,0:T(2,128)}, u32[]{:S(2)}) copy-start(s32[1,16,2]{1,2,0:T(2,128)} %param.8) | copy-start | bytes 388
  5.4 105.7 %copy-start.4 = (s32[1,16]{1,0:T(1,128)S(1)}, s32[1,16]{1,0:T(1,128)}, u32[]{:S(2)}) copy-start(s32[1,16]{1,0:T(1,128)} %param.9) | copy-start | bytes 196
  111.1 7.7 %collective-permute-start.1 = (bf16[16,352,384]{2,1,0:T(8,128)(2,1)}, bf16[16,352,384]{2,1,0:T(8,128)(2,1)}, u32[]{:S(2)}, u32[]{:S(2)}) collective-permute-start(bf16[16,352,384]{2,1,0:T(8,128)(2,1)} %all_to_all.15.q), channel_id=1, source_target_pairs={{0,8},{8,0},{1,9},{9,1},{2,10},{10,2},{3,11},{11,3},{4,12},{12,4},... | collective-permute-start | bytes 12976136 | tf_op jit(solution)/shard_map/ppermute | solution.py:176
  111.2 4.7 %collective-permute-start = (s32[16,3]{0,1:T(4,128)S(1)}, s32[16,3]{0,1:T(4,128)S(1)}, u32[]{:S(2)}, u32[]{:S(2)}) collective-permute-start(s32[16,3]{0,1:T(4,128)S(1)} %get-tuple-element.10), channel_id=1, source_target_pairs={{0,16},{16,0},{1,17},{17,1},{2,18},{18,2},{3,19},{19,3},{4,20},{20... | collective-permute-start | bytes 584 | tf_op jit(solution)/shard_map/ppermute | solution.py:160
  112.0 19.9 %all-to-all-start.1 = ((bf16[16,32,384]{2,1,0:T(8,128)(2,1)}), bf16[16,32,384]{2,1,0:T(8,128)(2,1)S(1)}, u32[]{:S(2)}, u32[]{:S(2)}) async-start(bf16[16,32,384]{2,1,0:T(8,128)(2,1)} %get-tuple-element.8), calls=%async_computation.1 | async-start | bytes 786432 | tf_op jit(solution)/shard_map/all_to_all | solution.py:151

commit v4 on v1

v4 whole, which is shorter than its diff:
```python
import functools
import math

import jax
import jax.numpy as jnp
from jax import lax
from jax.experimental import pallas as pl
from jax.experimental.pallas import tpu as pltpu
from jax.sharding import Mesh, PartitionSpec as P

DH = 128
TILE = 64
CORES = 2
LOW = 2
EXP2_SCALE = DH ** (-0.5) * math.log2(math.e)
MASKED = -1e30
VMEM = pl.BlockSpec(memory_space=pltpu.VMEM)
SMEM = pl.BlockSpec(memory_space=pltpu.SMEM)
ANY = pl.BlockSpec(memory_space=pl.ANY)


def rearrange(kernel, me, sources, shapes, after=()):
    first, count = 1 + len(sources), len(after)

    def held(*refs):
        kernel(*refs[:first], *refs[first + count:])

    moved = sum(math.prod(shape) for shape in shapes)
    return pl.pallas_call(
        held,
        in_specs=[SMEM] + [VMEM] * len(sources) + [ANY] * count,
        out_specs=[VMEM] * len(shapes),
        out_shape=[jax.ShapeDtypeStruct(shape, sources[0].dtype) for shape in shapes],
        compiler_params=pltpu.CompilerParams(vmem_limit_bytes=24 * 2**20),
        cost_estimate=pl.CostEstimate(flops=0, bytes_accessed=4 * moved, transcendentals=0),
        name="rearrange",
    )(me, *sources, *after)


def far_columns(me, source, *outs):
    width = outs[0].shape[1]
    for k, out in enumerate(outs):
        out[...] = source[:, pl.ds(pl.multiple_of((me[0] ^ k) * width, width), width)]


def near_columns(me, source, *outs):
    high, _, width = outs[0].shape
    near = len(outs)
    for e, out in enumerate(outs):
        for k in range(high):
            start = pl.multiple_of(((me[0] ^ k) * near + (me[1] ^ e)) * width, width)
            out[k] = source[:, pl.ds(start, width)]


def near_of_far(me, *refs):
    high = refs[-1].shape[0]
    sources, outs = refs[:high], refs[high:]
    width = outs[0].shape[2]
    for e, out in enumerate(outs):
        start = pl.multiple_of((me[1] ^ e) * width, width)
        for k, source in enumerate(sources):
            out[k] = source[:, pl.ds(start, width)]


def far_of_near(start, me, *refs):
    near = refs[-1].shape[0]
    sources, outs = refs[:near], refs[near:]
    rows = outs[0].shape[1]
    for k, out in enumerate(outs):
        for e, source in enumerate(sources):
            out[me[1] ^ e] = source[k, pl.ds(start, rows), :]


def copy(me, source, out):
    out[...] = source[...]


def join_near(me, *refs):
    for e, source in enumerate(refs[:-1]):
        refs[-1][me[1] ^ e] = source[...]


def join_far(me, *refs):
    for k, source in enumerate(refs[:-1]):
        refs[-1][:, k] = source[...]


def attend_kernel(plan, me, table, k_own, k_swap, v_own, v_swap, *refs):
    high, low, part = plan
    q_refs, o_refs, o = refs[:high], refs[high:-1], refs[-1]
    near, _, width = q_refs[0].shape
    rows = v_own.shape[2]
    per_device = rows // TILE
    spans = k_own.shape[0] // low * CORES
    tiles_span = high * low * per_device
    keys, values = (k_own, k_swap), (v_own, v_swap)

    for k in range(high):
        o[pl.ds(k * near, near)] = q_refs[k][...]

    def column_of(j):
        far, near_place = me[0] ^ (j // near), j % near
        return near_place // low * tiles_span + (far * low + near_place % low) * per_device + part

    def pair(step, carry):
        tiles = (2 * step, 2 * step + 1)
        cols_of = [column_of(j) for j in tiles]
        counts = [table[0, col] - table[3, col] + 1 for col in cols_of]
        most = jnp.maximum(counts[0], counts[1])

        def place_of(col, back, which):
            span = jnp.maximum(table[0, col] - back, 0)
            tile = table[1 + which, col]
            place = tile // per_device
            near_place = span // CORES * low + place % low
            return back % 2, near_place, (place // low) ^ me[0], pl.multiple_of(tile % per_device * TILE, TILE)

        def gather(refs, places, cols):
            return jnp.concatenate(
                [refs[odd][at, far, pl.ds(start, TILE), cols] for odd, at, far, start in places], axis=0
            )

        for many in range(1, spans + 1):

            @pl.when(most == many)
            def _(many=many):
                lane = lax.broadcasted_iota(jnp.int32, (1, many * 2 * TILE), 1)
                chains = []
                for j, col, count in zip(tiles, cols_of, counts):
                    places = [place_of(col, back, which) for back in range(many) for which in range(2)]
                    for head in range(width // DH):
                        chains.append((j, places, lane < count * (2 * TILE), pl.ds(head * DH, DH)))
                scores = [
                    lax.dot_general(
                        o[j, :, cols],
                        gather(keys, places, cols),
                        (((1,), (1,)), ((), ())),
                        preferred_element_type=jnp.float32,
                    )
                    for j, places, _, cols in chains
                ]
                scores = [jnp.where(valid, s, MASKED) for s, (_, _, valid, _) in zip(scores, chains)]
                tops = [jnp.max(s, axis=-1, keepdims=True) for s in scores]
                expos = [jnp.exp2((s - top) * EXP2_SCALE) for s, top in zip(scores, tops)]
                totals = [jnp.sum(expo, axis=-1, keepdims=True) for expo in expos]
                partials = [
                    jnp.dot(
                        expo.astype(jnp.bfloat16), gather(values, places, cols), preferred_element_type=jnp.float32
                    )
                    for expo, (_, places, _, cols) in zip(expos, chains)
                ]
                results = [(partial * (1.0 / total)).astype(o.dtype) for partial, total in zip(partials, totals)]
                for result, (j, _, _, cols) in zip(results, chains):
                    o[j, :, cols] = result

        return carry

    lax.fori_loop(0, high * near // 2, pair, 0)
    for k in range(high):
        o_refs[0][pl.ds((me[0] ^ k) * near, near)] = o[pl.ds(k * near, near)]


def attend(low, part, me, table, keys, values, q_blocks):
    high = len(q_blocks)
    near, rows, width = q_blocks[0].shape
    ways = high * near
    shapes = [(ways, rows, width)]
    seen = keys[0].shape[0] // low * CORES * TILE
    return pl.pallas_call(
        functools.partial(attend_kernel, (high, low, part)),
        in_specs=[SMEM, SMEM] + [VMEM] * (4 + high),
        out_specs=[VMEM] * len(shapes),
        out_shape=[jax.ShapeDtypeStruct(shape, q_blocks[0].dtype) for shape in shapes],
        scratch_shapes=[pltpu.VMEM((ways, rows, width), q_blocks[0].dtype)],
        compiler_params=pltpu.CompilerParams(vmem_limit_bytes=24 * 2**20),
        cost_estimate=pl.CostEstimate(
            flops=4 * ways * rows * width * seen,
            bytes_accessed=8 * keys[0].size + 4 * ways * rows * width,
            transcendentals=ways * rows * width // DH * seen,
        ),
        name="attend",
    )(me, table, *keys, *values, *q_blocks)


def body(queries, key_rows, value_rows, tile_lists, span_reach):
    chips, high, low = lax.axis_size("y"), lax.axis_size("far"), lax.axis_size("low")
    rows, depth = queries.shape
    core, chip = lax.axis_index("core"), lax.axis_index("y")

    split_y = depth // DH // (high * low) % chips == 0
    near_axes = ("y", "low") if split_y else ("low",)
    near = chips * low if split_y else low
    width = depth // (high * near)
    per_device = rows // TILE
    me = jnp.stack([lax.axis_index("far"), lax.axis_index(near_axes)]).astype(jnp.int32)

    def across(blocks):
        moved = {
            k: lax.ppermute(blocks[k], "far", [(i, i ^ k) for i in range(high)]) for k in range(high - 1, 0, -1)
        }
        return [blocks[0]] + [moved[k] for k in range(1, high)]

    def around(blocks):
        moved = [lax.ppermute(blocks[e], near_axes, [(i, i ^ e) for i in range(near)]) for e in range(1, near)]
        return [blocks[0]] + moved

    def with_swapped(x):
        if not split_y:
            x = lax.all_gather(x, "y", axis=0, tiled=True)
        return x, lax.ppermute(x, "core", [(0, 1), (1, 0)])

    table = jnp.concatenate([tile_lists[0], span_reach[0][:, None]], axis=1)
    if split_y:
        parts = [table]
        for step in range(1, chips):
            parts.append(lax.ppermute(table, "y", [(i, i ^ step) for i in range(chips)]))
        spans = jnp.arange(chips, dtype=jnp.int32)
        table = jnp.stack(parts)[spans ^ chip]
        spans = spans * CORES + core
    else:
        table = table[None]
        spans = (chip * CORES + core)[None]
    table = jnp.concatenate([jnp.broadcast_to(spans[:, None, None], table.shape[:2] + (1,)), table], axis=2)
    table = table.reshape(-1, 4).T.astype(jnp.int32)

    far_block, near_block, full = (near, rows, width), (high, rows, width), (near, high, rows, width)
    keys = across(rearrange(far_columns, me, [key_rows], [(rows, near * width)] * high))
    values = around(rearrange(near_columns, me, [value_rows], [near_block] * near))
    q = around(rearrange(near_columns, me, [queries], [near_block] * near, [keys[-1], values[1]]))
    q_parts = []
    for part in range(per_device):
        pick = functools.partial(far_of_near, part * TILE)
        before = [values[-1]] if part else []
        q_parts.append(across(rearrange(pick, me, q, [(near, TILE, width)] * high, before)))
        if not part:
            before = [q_parts[0][-1]]
            values = across(rearrange(functools.partial(far_of_near, 0), me, values, [far_block] * high, before))
    keys = around(rearrange(near_of_far, me, keys, [near_block] * near, q[1:] + [table]))
    keys = with_swapped(rearrange(join_near, me, keys, [full], q_parts[0][1:-1])[0])
    values = with_swapped(rearrange(join_far, me, values, [full])[0])
    outs = []
    for part in range(per_device):
        out = attend(low, part, me, table, keys, values, q_parts[part])[0]
        if part + 1 < per_device:
            out = rearrange(copy, me, [out], [out.shape], q_parts[part + 1][1:])[0]
        out = lax.all_to_all(out, ("far",) + near_axes, split_axis=0, concat_axis=0, tiled=True)
        outs.append(out.transpose(1, 0, 2).reshape(TILE, depth))
    return jnp.concatenate(outs, axis=0)


def solution(mesh):
    tm, groups = mesh.shape["tm"], mesh.shape["space"]
    fine = Mesh(mesh.devices.reshape(tm // CORES, CORES, groups // LOW, LOW), ("y", "core", "far", "low"))
    rows = P(("y", "core", "far", "low"), None)
    in_specs = (rows, rows, rows, P(("y", "core"), None, None), P(("y", "core"), None))
    return jax.shard_map(body, mesh=fine, in_specs=in_specs, out_specs=rows, check_vma=False)
```

time: 177 us -> 182 us (1.028)
  blocking collectives: 96.9 us -> 0 us
  starting transfers between devices: 13 us -> 60.9 us
  waiting for transfers between devices: 39.5 us -> 82.7 us
  local copies, waits for them, and re-layouts: 5.3 us -> 15.4 us
    all_to_all x1 -> x0, blocking collectives: 96.9 us -> none  [exchange(): return lax.all_to_all(x, axes, split_axis=0, concat_axis=0, tiled=True)]
    ppermute x1 -> x23, waiting for transfers between devices: 0.01 us -> 58.4 us  [the longest x12 47.5 us: across(): lax.ppermute(blocks[k], 'far', [(i, i ^ k) for i in range(high)])]
    ppermute x1 -> x23, starting transfers between devices: 0.01 us -> 47 us  [the longest x12 35.1 us: across(): lax.ppermute(blocks[k], 'far', [(i, i ^ k) for i in range(high)])]
    all_to_all x3 -> x2, waiting for transfers between devices: 34.2 us -> 24.2 us  [body(): lax.all_to_all(out, ('far',) + near_axes, split_axis=0, concat_axis=0, ti...]
    unnamed x10 -> x56, local copies, waits for them, and re-layouts: 4.23 us -> 13.3 us
    ppermute x1, waiting for transfers between devices: 5.25 us -> 0.01 us  [body(): lax.ppermute(table, 'y', [(i, i ^ step) for i in range(chips)])]
    all_to_all x3 -> x2, starting transfers between devices: 11 us -> 12.3 us  [body(): lax.all_to_all(out, ('far',) + near_axes, split_axis=0, concat_axis=0, ti...]
    pallas_call x4 -> x12, Pallas kernels: 20.2 us -> 21 us  [the longest x2 11.1 us: attend(): pl.pallas_call(functools.partial(attend_kernel, (high, low, part)), in_sp...]
  transfers between devices with their start and end apart: 5 -> 26, of which waited for: 4 -> 11; matrix products, arithmetic and copies ran while one was open for 1% -> 1% of each run, Pallas kernels for 11% -> 10%
where the time goes in v4:
time: 182 us
  waiting for transfers between devices  82.7 us (45%)
  starting transfers between devices  60.9 us (33%)
  Pallas kernels  21 us (12%)
  local copies, waits for them, and re-layouts  15.4 us (8%)
    ppermute x12, waiting for transfers between devices, across(): lax.ppermute(blocks[k], 'far', [(i, i ^ k) for i in range(high)])  47.5 us
    ppermute x12, starting transfers between devices, across(): lax.ppermute(blocks[k], 'far', [(i, i ^ k) for i in range(high)])  35.1 us
    all_to_all x2, waiting for transfers between devices, body(): lax.all_to_all(out, ('far',) + near_axes, split_axis=0, concat_axis=0, ti...  24.2 us
    unnamed x56, local copies, waits for them, and re-layouts  13.3 us
    all_to_all x2, starting transfers between devices, body(): lax.all_to_all(out, ('far',) + near_axes, split_axis=0, concat_axis=0, ti...  12.3 us
    ppermute x9, starting transfers between devices, around(): lax.ppermute(blocks[e], near_axes, [(i, i ^ e) for i in range(near)])  11.8 us
    pallas_call x2, Pallas kernels, attend(): pl.pallas_call(functools.partial(attend_kernel, (high, low, part)), in_sp...  11.1 us
    ppermute x9, waiting for transfers between devices, around(): lax.ppermute(blocks[e], near_axes, [(i, i ^ e) for i in range(near)])  10.9 us
  transfers between devices with their start and end apart: 26, of which 11 were waited for; matrix products, arithmetic and copies ran while one was open for 1% of the time, Pallas kernels for 10%

profile of v4, /device:TPU:0, one launch (start us, length us, event | category | flops | bytes accessed | tf_op | source)
XLA Modules:
  0.0 181.6 jit_solution(9957514156451698601)
XLA Ops:
  0.1 1.4 copy-done.10
  1.5 1.6 rearrange.10
  3.1 5.0 %collective-permute-start.3 = (bf16[128,1536]{1,0:T(8,128)(2,1)S(1)}, bf16[128,1536]{1,0:T(8,128)(2,1)S(1)}, u32[]{:S(2)}, u32[]{:S(2)}) collective-permute-start(bf16[128,1536]{1,0:T(8,128)(2,1)S(1)} %get-tuple-element.36), channel_id=1, source_target_pairs={{0,6},{2,4},{4,2},{6,0},{1,7},{3,5},{5,3},{7,1},{8,14},{10,12},{12... | collective-permute-start | bytes 1179656 | tf_op jit(solution)/shard_map/ppermute | solution.py:199
  8.1 1.6 rearrange.11
  10.4 1.5 collective-permute-start.4
  12.0 1.6 collective-permute-start
  14.3 3.8 %collective-permute-done.3.refs_2_.refs_4_ = bf16[128,1536]{1,0:T(8,128)(2,1)S(1)} collective-permute-done((bf16[128,1536]{1,0:T(8,128)(2,1)S(1)}, bf16[128,1536]{1,0:T(8,128)(2,1)S(1)}, u32[]{:S(2)}, u32[]{:S(2)}) %collective-permute-start.3) | collective-permute-done | bytes 393248 | tf_op jit(solution)/shard_map/ppermute | solution.py:199
  18.1 3.1 %collective-permute-done.4.refs_3_.refs_2_ = bf16[4,128,384]{2,1,0:T(8,128)(2,1)S(1)} collective-permute-done((bf16[4,128,384]{2,1,0:T(8,128)(2,1)}, bf16[4,128,384]{2,1,0:T(8,128)(2,1)S(1)}, u32[]{:S(2)}, u32[]{:S(2)}) %collective-permute-start.4) | collective-permute-done | bytes 393248 | tf_op jit(solution)/shard_map/ppermute | solution.py:204
  21.2 1.7 rearrange.12
  22.9 1.5 collective-permute-start.5
  24.4 1.5 collective-permute-start.6
  26.8 1.4 collective-permute-start.14
  28.9 12.9 %collective-permute-done.2.refs_3_ = bf16[128,1536]{1,0:T(8,128)(2,1)} collective-permute-done((bf16[128,1536]{1,0:T(8,128)(2,1)}, bf16[128,1536]{1,0:T(8,128)(2,1)}, u32[]{:S(2)}, u32[]{:S(2)}) %collective-permute-start.2) | collective-permute-done | bytes 393248 | tf_op jit(solution)/shard_map/ppermute | solution.py:199
  41.8 2.4 %collective-permute-start.15 = (bf16[4,128,384]{2,1,0:T(8,128)(2,1)}, bf16[4,128,384]{2,1,0:T(8,128)(2,1)S(1)}, u32[]{:S(2)}, u32[]{:S(2)}) collective-permute-start(bf16[4,128,384]{2,1,0:T(8,128)(2,1)} %copy-done.25), channel_id=1, source_target_pairs={{0,17},{1,16},{16,1},{17,0},{2,19},{3,18},{18,3},{19,2},{4,21},{5,... | collective-permute-start | bytes 1179656 | tf_op jit(solution)/shard_map/ppermute | solution.py:204
  44.4 7.7 %collective-permute-done.6.refs_6_.refs_3_ = bf16[4,128,384]{2,1,0:T(8,128)(2,1)S(1)} collective-permute-done((bf16[4,128,384]{2,1,0:T(8,128)(2,1)}, bf16[4,128,384]{2,1,0:T(8,128)(2,1)S(1)}, u32[]{:S(2)}, u32[]{:S(2)}) %collective-permute-start.6) | collective-permute-done | bytes 393248 | tf_op jit(solution)/shard_map/ppermute | solution.py:204
  55.5 8.5 %collective-permute-start.11 = (bf16[4,64,384]{2,1,0:T(8,128)(2,1)S(1)}, bf16[4,64,384]{2,1,0:T(8,128)(2,1)S(1)}, u32[]{:S(2)}, u32[]{:S(2)}) collective-permute-start(bf16[4,64,384]{2,1,0:T(8,128)(2,1)S(1)} %get-tuple-element.46), channel_id=1, source_target_pairs={{0,2},{2,0},{4,6},{6,4},{1,3},{3,1},{5,7},{7,5},{8,10},{10,8},{12,... | collective-permute-start | bytes 589832 | tf_op jit(solution)/shard_map/ppermute | solution.py:199
  64.0 2.0 %collective-permute-start.12 = (bf16[4,64,384]{2,1,0:T(8,128)(2,1)S(1)}, bf16[4,64,384]{2,1,0:T(8,128)(2,1)S(1)}, u32[]{:S(2)}, u32[]{:S(2)}) collective-permute-start(bf16[4,64,384]{2,1,0:T(8,128)(2,1)S(1)} %get-tuple-element.47), channel_id=1, source_target_pairs={{0,4},{2,6},{4,0},{6,2},{1,5},{3,7},{5,1},{7,3},{8,12},{10,14},{12... | collective-permute-start | bytes 589832 | tf_op jit(solution)/shard_map/ppermute | solution.py:199
  66.1 2.9 %collective-permute-start.9 = (bf16[4,128,384]{2,1,0:T(8,128)(2,1)S(1)}, bf16[4,128,384]{2,1,0:T(8,128)(2,1)S(1)}, u32[]{:S(2)}, u32[]{:S(2)}) collective-permute-start(bf16[4,128,384]{2,1,0:T(8,128)(2,1)S(1)} %get-tuple-element.43), channel_id=1, source_target_pairs={{0,16},{1,17},{16,0},{17,1},{2,18},{3,19},{18,2},{19,3},{4,20},{5,... | collective-permute-start | bytes 1179656 | tf_op jit(solution)/shard_map/ppermute | solution.py:204
  69.6 4.4 %collective-permute-done.11.refs_5_.refs_1_ = bf16[4,64,384]{2,1,0:T(8,128)(2,1)S(1)} collective-permute-done((bf16[4,64,384]{2,1,0:T(8,128)(2,1)S(1)}, bf16[4,64,384]{2,1,0:T(8,128)(2,1)S(1)}, u32[]{:S(2)}, u32[]{:S(2)}) %collective-permute-start.11) | collective-permute-done | bytes 196640 | tf_op jit(solution)/shard_map/ppermute | solution.py:199
  74.0 3.0 %collective-permute-start.18 = (bf16[4,128,384]{2,1,0:T(8,128)(2,1)S(1)}, bf16[4,128,384]{2,1,0:T(8,128)(2,1)S(1)}, u32[]{:S(2)}, u32[]{:S(2)}) collective-permute-start(bf16[4,128,384]{2,1,0:T(8,128)(2,1)S(1)} %get-tuple-element.54), channel_id=1, source_target_pairs={{0,4},{2,6},{4,0},{6,2},{1,5},{3,7},{5,1},{7,3},{8,12},{10,14},{12... | collective-permute-start | bytes 1179656 | tf_op jit(solution)/shard_map/ppermute | solution.py:199
  77.1 5.0 %collective-permute-start.19 = (bf16[4,128,384]{2,1,0:T(8,128)(2,1)S(1)}, bf16[4,128,384]{2,1,0:T(8,128)(2,1)S(1)}, u32[]{:S(2)}, u32[]{:S(2)}) collective-permute-start(bf16[4,128,384]{2,1,0:T(8,128)(2,1)S(1)} %get-tuple-element.55), channel_id=1, source_target_pairs={{0,6},{2,4},{4,2},{6,0},{1,7},{3,5},{5,3},{7,1},{8,14},{10,12},{12... | collective-permute-start | bytes 1179656 | tf_op jit(solution)/shard_map/ppermute | solution.py:199
  82.9 7.3 %collective-permute-done.17.refs_2_ = bf16[4,128,384]{2,1,0:T(8,128)(2,1)S(1)} collective-permute-done((bf16[4,128,384]{2,1,0:T(8,128)(2,1)S(1)}, bf16[4,128,384]{2,1,0:T(8,128)(2,1)S(1)}, u32[]{:S(2)}, u32[]{:S(2)}) %collective-permute-start.17) | collective-permute-done | bytes 393248 | tf_op jit(solution)/shard_map/ppermute | solution.py:199
  90.1 9.7 %collective-permute-done.18.refs_3_ = bf16[4,128,384]{2,1,0:T(8,128)(2,1)S(1)} collective-permute-done((bf16[4,128,384]{2,1,0:T(8,128)(2,1)S(1)}, bf16[4,128,384]{2,1,0:T(8,128)(2,1)S(1)}, u32[]{:S(2)}, u32[]{:S(2)}) %collective-permute-start.18) | collective-permute-done | bytes 393248 | tf_op jit(solution)/shard_map/ppermute | solution.py:199
  101.7 8.1 %collective-permute-start.21 = (bf16[4,64,384]{2,1,0:T(8,128)(2,1)S(1)}, bf16[4,64,384]{2,1,0:T(8,128)(2,1)S(1)}, u32[]{:S(2)}, u32[]{:S(2)}) collective-permute-start(bf16[4,64,384]{2,1,0:T(8,128)(2,1)S(1)} %get-tuple-element.57), channel_id=1, source_target_pairs={{0,2},{2,0},{4,6},{6,4},{1,3},{3,1},{5,7},{7,5},{8,10},{10,8},{12,... | collective-permute-start | bytes 589832 | tf_op jit(solution)/shard_map/ppermute | solution.py:199
  109.8 2.4 %collective-permute-start.23 = (bf16[4,64,384]{2,1,0:T(8,128)(2,1)S(1)}, bf16[4,64,384]{2,1,0:T(8,128)(2,1)S(1)}, u32[]{:S(2)}, u32[]{:S(2)}) collective-permute-start(bf16[4,64,384]{2,1,0:T(8,128)(2,1)S(1)} %get-tuple-element.59), channel_id=1, source_target_pairs={{0,6},{2,4},{4,2},{6,0},{1,7},{3,5},{5,3},{7,1},{8,14},{10,12},{12... | collective-permute-start | bytes 589832 | tf_op jit(solution)/shard_map/ppermute | solution.py:199
  112.2 5.5 %attend.2.refs_1_ = bf16[16,64,384]{2,1,0:T(8,128)(2,1)S(1)} custom-call(s32[2]{0:T(128)S(1)} %pad_add_fusion.3.refs_0_.me, s32[4,32]{1,0:T(4,128)S(1)} %bitcast.19, bf16[4,4,128,384]{3,2,1,0:T(8,128)(2,1)S(1)} %rearrange.15.k_own, bf16[4,4,128,384]{3,2,1,0:T(8,128)(2,1)S(1)} %collective-permute-done.13.k_swap, ...), custom_call_target="tpu_custom_call" | custom-call | flops 402653184 | bytes 7864320 | tf_op jit(solution)/shard_map/attend/pallas_call | solution.py:169
  117.8 9.1 %collective-permute-done.22.refs_3_.refs_2_ = bf16[4,64,384]{2,1,0:T(8,128)(2,1)S(1)} collective-permute-done((bf16[4,64,384]{2,1,0:T(8,128)(2,1)S(1)}, bf16[4,64,384]{2,1,0:T(8,128)(2,1)S(1)}, u32[]{:S(2)}, u32[]{:S(2)}) %collective-permute-start.22) | collective-permute-done | bytes 196640 | tf_op jit(solution)/shard_map/ppermute | solution.py:199
  130.4 7.4 %all-to-all-start = ((bf16[16,64,384]{2,1,0:T(8,128)(2,1)}), bf16[16,64,384]{2,1,0:T(8,128)(2,1)}, u32[]{:S(2)}, u32[]{:S(2)}) async-start(bf16[16,64,384]{2,1,0:T(8,128)(2,1)} %copy-done.9), calls=%async_computation | async-start | bytes 1572864 | tf_op jit(solution)/shard_map/all_to_all | solution.py:246
  143.4 5.6 %attend.3 = bf16[16,64,384]{2,1,0:T(8,128)(2,1)S(1)} custom-call(s32[2]{0:T(128)S(1)} %pad_add_fusion.3.refs_0_.me, s32[4,32]{1,0:T(4,128)S(1)} %bitcast.20, bf16[4,4,128,384]{3,2,1,0:T(8,128)(2,1)S(1)} %rearrange.15.k_own, bf16[4,4,128,384]{3,2,1,0:T(8,128)(2,1)S(1)} %copy-done.1, bf16[4,4,128,384]{3,2,1,0:T(8,128)(2,1)S(1)} %rearrange.17.v_own, ...), custom_call_target="tpu_custom_call" | custom-call | flops 402653184 | bytes 7864320 | tf_op jit(solution)/shard_map/attend/pallas_call | solution.py:169
  149.9 6.8 %all-to-all-done = bf16[16,64,384]{2,1,0:T(8,128)(2,1)} async-done(((bf16[16,64,384]{2,1,0:T(8,128)(2,1)}), bf16[16,64,384]{2,1,0:T(8,128)(2,1)}, u32[]{:S(2)}, u32[]{:S(2)}) %all-to-all-start) | async-done | bytes 786464 | tf_op jit(solution)/shard_map/all_to_all | solution.py:246
  156.7 4.9 %all-to-all-start.1 = ((bf16[16,64,384]{2,1,0:T(8,128)(2,1)}), bf16[16,64,384]{2,1,0:T(8,128)(2,1)S(1)}, u32[]{:S(2)}, u32[]{:S(2)}) async-start(bf16[16,64,384]{2,1,0:T(8,128)(2,1)} %copy-done.8), calls=%async_computation.1 | async-start | bytes 1572864 | tf_op jit(solution)/shard_map/all_to_all | solution.py:246
  162.8 17.4 %all-to-all-done.1 = bf16[16,64,384]{2,1,0:T(8,128)(2,1)S(1)} async-done(((bf16[16,64,384]{2,1,0:T(8,128)(2,1)}), bf16[16,64,384]{2,1,0:T(8,128)(2,1)S(1)}, u32[]{:S(2)}, u32[]{:S(2)}) %all-to-all-start.1) | async-done | bytes 786464 | tf_op jit(solution)/shard_map/all_to_all | solution.py:246
  (102 shorter events, 22.5 us)
Async XLA Ops:
  1.5 10.5 %copy-start.27 = (s32[1,16]{1,0:T(1,128)S(1)}, s32[1,16]{1,0:T(1,128)}, u32[]{:S(2)}) copy-start(s32[1,16]{1,0:T(1,128)} %param.9) | copy-start | bytes 196
  1.5 19.7 %copy-start.12 = (bf16[128,6144]{1,0:T(8,128)(2,1)S(1)}, bf16[128,6144]{1,0:T(8,128)(2,1)}, u32[]{:S(2)}) copy-start(bf16[128,6144]{1,0:T(8,128)(2,1)} %refs_1_.5) | copy-start | bytes 4718596
  3.0 19.9 %copy-start.21 = (bf16[128,1536]{1,0:T(8,128)(2,1)}, bf16[128,1536]{1,0:T(8,128)(2,1)S(1)}, u32[]{:S(2)}) copy-start(bf16[128,1536]{1,0:T(8,128)(2,1)S(1)} %get-tuple-element.33.refs_1_) | copy-start | bytes 1179652
  3.1 15.0 %collective-permute-start.3 = (bf16[128,1536]{1,0:T(8,128)(2,1)S(1)}, bf16[128,1536]{1,0:T(8,128)(2,1)S(1)}, u32[]{:S(2)}, u32[]{:S(2)}) collective-permute-start(bf16[128,1536]{1,0:T(8,128)(2,1)S(1)} %get-tuple-element.36), channel_id=1, source_target_pairs={{0,6},{2,4},{4,2},{6,0},{1,7},{3,5},{5,3},{7,1},{8,14},{10,12},{12... | collective-permute-start | bytes 1179656 | tf_op jit(solution)/shard_map/ppermute | solution.py:199
  10.4 10.8 %collective-permute-start.4 = (bf16[4,128,384]{2,1,0:T(8,128)(2,1)}, bf16[4,128,384]{2,1,0:T(8,128)(2,1)S(1)}, u32[]{:S(2)}, u32[]{:S(2)}) collective-permute-start(bf16[4,128,384]{2,1,0:T(8,128)(2,1)} %get-tuple-element.37), channel_id=1, source_target_pairs={{0,1},{1,0},{16,17},{17,16},{2,3},{3,2},{18,19},{19,18},{4,5},{5,4... | collective-permute-start | bytes 1179656 | tf_op jit(solution)/shard_map/ppermute | solution.py:204
  11.9 14.9 %collective-permute-start.1 = (bf16[128,1536]{1,0:T(8,128)(2,1)}, bf16[128,1536]{1,0:T(8,128)(2,1)}, u32[]{:S(2)}, u32[]{:S(2)}) collective-permute-start(bf16[128,1536]{1,0:T(8,128)(2,1)} %get-tuple-element.34), channel_id=1, source_target_pairs={{0,2},{2,0},{4,6},{6,4},{1,3},{3,1},{5,7},{7,5},{8,10},{10,8},{12,... | collective-permute-start | bytes 1179656 | tf_op jit(solution)/shard_map/ppermute | solution.py:199
  12.0 14.0 %collective-permute-start = (s32[16,3]{0,1:T(4,128)S(1)}, s32[16,3]{0,1:T(4,128)S(1)}, u32[]{:S(2)}, u32[]{:S(2)}) collective-permute-start(s32[16,3]{0,1:T(4,128)S(1)} %get-tuple-element.62), channel_id=1, source_target_pairs={{0,16},{16,0},{1,17},{17,1},{2,18},{18,2},{3,19},{19,3},{4,20},{20... | collective-permute-start | bytes 584 | tf_op jit(solution)/shard_map/ppermute | solution.py:216
  13.5 28.2 %collective-permute-start.2 = (bf16[128,1536]{1,0:T(8,128)(2,1)}, bf16[128,1536]{1,0:T(8,128)(2,1)}, u32[]{:S(2)}, u32[]{:S(2)}) collective-permute-start(bf16[128,1536]{1,0:T(8,128)(2,1)} %get-tuple-element.35), channel_id=1, source_target_pairs={{0,4},{2,6},{4,0},{6,2},{1,5},{3,7},{5,1},{7,3},{8,12},{10,14},{12... | collective-permute-start | bytes 1179656 | tf_op jit(solution)/shard_map/ppermute | solution.py:199
  22.9 32.5 %copy-start.13 = (bf16[4,128,384]{2,1,0:T(8,128)(2,1)}, bf16[4,128,384]{2,1,0:T(8,128)(2,1)S(1)}, u32[]{:S(2)}) copy-start(bf16[4,128,384]{2,1,0:T(8,128)(2,1)S(1)} %get-tuple-element.45.refs_1_) | copy-start | bytes 1179652
  22.9 21.5 %collective-permute-start.5 = (bf16[4,128,384]{2,1,0:T(8,128)(2,1)}, bf16[4,128,384]{2,1,0:T(8,128)(2,1)S(1)}, u32[]{:S(2)}, u32[]{:S(2)}) collective-permute-start(bf16[4,128,384]{2,1,0:T(8,128)(2,1)} %get-tuple-element.38), channel_id=1, source_target_pairs={{0,1},{1,0},{16,17},{17,16},{2,3},{3,2},{18,19},{19,18},{4,5},{5,4... | collective-permute-start | bytes 1179656 | tf_op jit(solution)/shard_map/ppermute | solution.py:204
  24.4 27.7 %collective-permute-start.6 = (bf16[4,128,384]{2,1,0:T(8,128)(2,1)}, bf16[4,128,384]{2,1,0:T(8,128)(2,1)S(1)}, u32[]{:S(2)}, u32[]{:S(2)}) collective-permute-start(bf16[4,128,384]{2,1,0:T(8,128)(2,1)} %get-tuple-element.39), channel_id=1, source_target_pairs={{0,16},{1,17},{16,0},{17,1},{2,18},{3,19},{18,2},{19,3},{4,20},{5,... | collective-permute-start | bytes 1179656 | tf_op jit(solution)/shard_map/ppermute | solution.py:204
  25.9 26.2 %collective-permute-start.7 = (bf16[4,128,384]{2,1,0:T(8,128)(2,1)}, bf16[4,128,384]{2,1,0:T(8,128)(2,1)S(1)}, u32[]{:S(2)}, u32[]{:S(2)}) collective-permute-start(bf16[4,128,384]{2,1,0:T(8,128)(2,1)} %get-tuple-element.40), channel_id=1, source_target_pairs={{0,17},{1,16},{16,1},{17,0},{2,19},{3,18},{18,3},{19,2},{4,21},{5,... | collective-permute-start | bytes 1179656 | tf_op jit(solution)/shard_map/ppermute | solution.py:204
  26.8 37.2 %collective-permute-start.14 = (bf16[4,128,384]{2,1,0:T(8,128)(2,1)}, bf16[4,128,384]{2,1,0:T(8,128)(2,1)S(1)}, u32[]{:S(2)}, u32[]{:S(2)}) collective-permute-start(bf16[4,128,384]{2,1,0:T(8,128)(2,1)} %get-tuple-element.49), channel_id=1, source_target_pairs={{0,16},{1,17},{16,0},{17,1},{2,18},{3,19},{18,2},{19,3},{4,20},{5,... | collective-permute-start | bytes 1179656 | tf_op jit(solution)/shard_map/ppermute | solution.py:204
  41.8 24.3 %collective-permute-start.15 = (bf16[4,128,384]{2,1,0:T(8,128)(2,1)}, bf16[4,128,384]{2,1,0:T(8,128)(2,1)S(1)}, u32[]{:S(2)}, u32[]{:S(2)}) collective-permute-start(bf16[4,128,384]{2,1,0:T(8,128)(2,1)} %copy-done.25), channel_id=1, source_target_pairs={{0,17},{1,16},{16,1},{17,0},{2,19},{3,18},{18,3},{19,2},{4,21},{5,... | collective-permute-start | bytes 1179656 | tf_op jit(solution)/shard_map/ppermute | solution.py:204
  54.7 22.4 %collective-permute-start.8 = (bf16[4,128,384]{2,1,0:T(8,128)(2,1)S(1)}, bf16[4,128,384]{2,1,0:T(8,128)(2,1)S(1)}, u32[]{:S(2)}, u32[]{:S(2)}) collective-permute-start(bf16[4,128,384]{2,1,0:T(8,128)(2,1)S(1)} %get-tuple-element.42), channel_id=1, source_target_pairs={{0,1},{1,0},{16,17},{17,16},{2,3},{3,2},{18,19},{19,18},{4,5},{5,4... | collective-permute-start | bytes 1179656 | tf_op jit(solution)/shard_map/ppermute | solution.py:204
  55.4 13.5 %collective-permute-start.16 = (bf16[4,64,384]{2,1,0:T(8,128)(2,1)S(1)}, bf16[4,64,384]{2,1,0:T(8,128)(2,1)S(1)}, u32[]{:S(2)}, u32[]{:S(2)}) collective-permute-start(bf16[4,64,384]{2,1,0:T(8,128)(2,1)S(1)} %get-tuple-element.51), channel_id=1, source_target_pairs={{0,6},{2,4},{4,2},{6,0},{1,7},{3,5},{5,3},{7,1},{8,14},{10,12},{12... | collective-permute-start | bytes 589832 | tf_op jit(solution)/shard_map/ppermute | solution.py:199
  55.5 18.5 %collective-permute-start.11 = (bf16[4,64,384]{2,1,0:T(8,128)(2,1)S(1)}, bf16[4,64,384]{2,1,0:T(8,128)(2,1)S(1)}, u32[]{:S(2)}, u32[]{:S(2)}) collective-permute-start(bf16[4,64,384]{2,1,0:T(8,128)(2,1)S(1)} %get-tuple-element.46), channel_id=1, source_target_pairs={{0,2},{2,0},{4,6},{6,4},{1,3},{3,1},{5,7},{7,5},{8,10},{10,8},{12,... | collective-permute-start | bytes 589832 | tf_op jit(solution)/shard_map/ppermute | solution.py:199
  64.0 10.0 %collective-permute-start.12 = (bf16[4,64,384]{2,1,0:T(8,128)(2,1)S(1)}, bf16[4,64,384]{2,1,0:T(8,128)(2,1)S(1)}, u32[]{:S(2)}, u32[]{:S(2)}) collective-permute-start(bf16[4,64,384]{2,1,0:T(8,128)(2,1)S(1)} %get-tuple-element.47), channel_id=1, source_target_pairs={{0,4},{2,6},{4,0},{6,2},{1,5},{3,7},{5,1},{7,3},{8,12},{10,14},{12... | collective-permute-start | bytes 589832 | tf_op jit(solution)/shard_map/ppermute | solution.py:199
  66.1 16.0 %collective-permute-start.9 = (bf16[4,128,384]{2,1,0:T(8,128)(2,1)S(1)}, bf16[4,128,384]{2,1,0:T(8,128)(2,1)S(1)}, u32[]{:S(2)}, u32[]{:S(2)}) collective-permute-start(bf16[4,128,384]{2,1,0:T(8,128)(2,1)S(1)} %get-tuple-element.43), channel_id=1, source_target_pairs={{0,16},{1,17},{16,0},{17,1},{2,18},{3,19},{18,2},{19,3},{4,20},{5,... | collective-permute-start | bytes 1179656 | tf_op jit(solution)/shard_map/ppermute | solution.py:204
  68.9 13.2 %collective-permute-start.10 = (bf16[4,128,384]{2,1,0:T(8,128)(2,1)S(1)}, bf16[4,128,384]{2,1,0:T(8,128)(2,1)S(1)}, u32[]{:S(2)}, u32[]{:S(2)}) collective-permute-start(bf16[4,128,384]{2,1,0:T(8,128)(2,1)S(1)} %get-tuple-element.44), channel_id=1, source_target_pairs={{0,17},{1,16},{16,1},{17,0},{2,19},{3,18},{18,3},{19,2},{4,21},{5,... | collective-permute-start | bytes 1179656 | tf_op jit(solution)/shard_map/ppermute | solution.py:204
  74.0 16.1 %collective-permute-start.17 = (bf16[4,128,384]{2,1,0:T(8,128)(2,1)S(1)}, bf16[4,128,384]{2,1,0:T(8,128)(2,1)S(1)}, u32[]{:S(2)}, u32[]{:S(2)}) collective-permute-start(bf16[4,128,384]{2,1,0:T(8,128)(2,1)S(1)} %get-tuple-element.53), channel_id=1, source_target_pairs={{0,2},{2,0},{4,6},{6,4},{1,3},{3,1},{5,7},{7,5},{8,10},{10,8},{12,... | collective-permute-start | bytes 1179656 | tf_op jit(solution)/shard_map/ppermute | solution.py:199
  74.0 25.8 %collective-permute-start.18 = (bf16[4,128,384]{2,1,0:T(8,128)(2,1)S(1)}, bf16[4,128,384]{2,1,0:T(8,128)(2,1)S(1)}, u32[]{:S(2)}, u32[]{:S(2)}) collective-permute-start(bf16[4,128,384]{2,1,0:T(8,128)(2,1)S(1)} %get-tuple-element.54), channel_id=1, source_target_pairs={{0,4},{2,6},{4,0},{6,2},{1,5},{3,7},{5,1},{7,3},{8,12},{10,14},{12... | collective-permute-start | bytes 1179656 | tf_op jit(solution)/shard_map/ppermute | solution.py:199
  77.1 22.7 %collective-permute-start.19 = (bf16[4,128,384]{2,1,0:T(8,128)(2,1)S(1)}, bf16[4,128,384]{2,1,0:T(8,128)(2,1)S(1)}, u32[]{:S(2)}, u32[]{:S(2)}) collective-permute-start(bf16[4,128,384]{2,1,0:T(8,128)(2,1)S(1)} %get-tuple-element.55), channel_id=1, source_target_pairs={{0,6},{2,4},{4,2},{6,0},{1,7},{3,5},{5,3},{7,1},{8,14},{10,12},{12... | collective-permute-start | bytes 1179656 | tf_op jit(solution)/shard_map/ppermute | solution.py:199
  82.8 29.4 %collective-permute-start.13 = (bf16[4,4,128,384]{3,2,1,0:T(8,128)(2,1)S(1)}, bf16[4,4,128,384]{3,2,1,0:T(8,128)(2,1)S(1)}, u32[]{:S(2)}, u32[]{:S(2)}) collective-permute-start(bf16[4,4,128,384]{3,2,1,0:T(8,128)(2,1)S(1)} %rearrange.15.k_own), channel_id=1, source_target_pairs={{0,8},{8,0},{1,9},{9,1},{2,10},{10,2},{3,11},{11,3},{4,12},{12,4},... | collective-permute-start | bytes 4718600 | tf_op jit(solution)/shard_map/ppermute | solution.py:210
  100.5 11.7 %collective-permute-start.20 = (bf16[4,4,128,384]{3,2,1,0:T(8,128)(2,1)S(1)}, bf16[4,4,128,384]{3,2,1,0:T(8,128)(2,1)S(1)}, u32[]{:S(2)}, u32[]{:S(2)}) collective-permute-start(bf16[4,4,128,384]{3,2,1,0:T(8,128)(2,1)S(1)} %rearrange.17.v_own), channel_id=1, source_target_pairs={{0,8},{8,0},{1,9},{9,1},{2,10},{10,2},{3,11},{11,3},{4,12},{12,4},... | collective-permute-start | bytes 4718600 | tf_op jit(solution)/shard_map/ppermute | solution.py:210
  101.7 16.1 %copy-start.23 = (bf16[4,64,384]{2,1,0:T(8,128)(2,1)}, bf16[4,64,384]{2,1,0:T(8,128)(2,1)S(1)}, u32[]{:S(2)}) copy-start(bf16[4,64,384]{2,1,0:T(8,128)(2,1)S(1)} %get-tuple-element.60.refs_0_) | copy-start | bytes 589828
  101.7 16.1 %collective-permute-start.21 = (bf16[4,64,384]{2,1,0:T(8,128)(2,1)S(1)}, bf16[4,64,384]{2,1,0:T(8,128)(2,1)S(1)}, u32[]{:S(2)}, u32[]{:S(2)}) collective-permute-start(bf16[4,64,384]{2,1,0:T(8,128)(2,1)S(1)} %get-tuple-element.57), channel_id=1, source_target_pairs={{0,2},{2,0},{4,6},{6,4},{1,3},{3,1},{5,7},{7,5},{8,10},{10,8},{12,... | collective-permute-start | bytes 589832 | tf_op jit(solution)/shard_map/ppermute | solution.py:199
  109.8 17.1 %collective-permute-start.22 = (bf16[4,64,384]{2,1,0:T(8,128)(2,1)S(1)}, bf16[4,64,384]{2,1,0:T(8,128)(2,1)S(1)}, u32[]{:S(2)}, u32[]{:S(2)}) collective-permute-start(bf16[4,64,384]{2,1,0:T(8,128)(2,1)S(1)} %get-tuple-element.58), channel_id=1, source_target_pairs={{0,4},{2,6},{4,0},{6,2},{1,5},{3,7},{5,1},{7,3},{8,12},{10,14},{12... | collective-permute-start | bytes 589832 | tf_op jit(solution)/shard_map/ppermute | solution.py:199
  109.8 17.1 %collective-permute-start.23 = (bf16[4,64,384]{2,1,0:T(8,128)(2,1)S(1)}, bf16[4,64,384]{2,1,0:T(8,128)(2,1)S(1)}, u32[]{:S(2)}, u32[]{:S(2)}) collective-permute-start(bf16[4,64,384]{2,1,0:T(8,128)(2,1)S(1)} %get-tuple-element.59), channel_id=1, source_target_pairs={{0,6},{2,4},{4,2},{6,0},{1,7},{3,5},{5,3},{7,1},{8,14},{10,12},{12... | collective-permute-start | bytes 589832 | tf_op jit(solution)/shard_map/ppermute | solution.py:199
  117.8 20.0 %copy-start.24 = (bf16[4,64,384]{2,1,0:T(8,128)(2,1)S(1)}, bf16[4,64,384]{2,1,0:T(8,128)(2,1)}, u32[]{:S(2)}) copy-start(bf16[4,64,384]{2,1,0:T(8,128)(2,1)} %copy-done.23) | copy-start | bytes 589828
  130.4 26.3 %all-to-all-start = ((bf16[16,64,384]{2,1,0:T(8,128)(2,1)}), bf16[16,64,384]{2,1,0:T(8,128)(2,1)}, u32[]{:S(2)}, u32[]{:S(2)}) async-start(bf16[16,64,384]{2,1,0:T(8,128)(2,1)} %copy-done.9), calls=%async_computation | async-start | bytes 1572864 | tf_op jit(solution)/shard_map/all_to_all | solution.py:246
  156.7 23.5 %all-to-all-start.1 = ((bf16[16,64,384]{2,1,0:T(8,128)(2,1)}), bf16[16,64,384]{2,1,0:T(8,128)(2,1)S(1)}, u32[]{:S(2)}, u32[]{:S(2)}) async-start(bf16[16,64,384]{2,1,0:T(8,128)(2,1)} %copy-done.8), calls=%async_computation.1 | async-start | bytes 1572864 | tf_op jit(solution)/shard_map/all_to_all | solution.py:246
  (22 other events, 50.9 us)

commit v5 on v4

--- a/solution.py
+++ b/solution.py
@@ -37,9 +37,9 @@
     )(me, *sources, *after)
 
 
-def far_columns(me, source, *outs):
+def far_columns(blocks, me, source, *outs):
     width = outs[0].shape[1]
-    for k, out in enumerate(outs):
+    for k, out in zip(blocks, outs):
         out[...] = source[:, pl.ds(pl.multiple_of((me[0] ^ k) * width, width), width)]
 
 
@@ -71,8 +71,10 @@
             out[me[1] ^ e] = source[k, pl.ds(start, rows), :]
 
 
-def copy(me, source, out):
-    out[...] = source[...]
+def all_columns(me, source, out):
+    ways, _, width = out.shape
+    for way in range(ways):
+        out[way] = source[:, pl.ds(way * width, width)]
 
 
 def join_near(me, *refs):
@@ -85,21 +87,18 @@
         refs[-1][:, k] = source[...]
 
 
-def attend_kernel(plan, me, table, k_own, k_swap, v_own, v_swap, *refs):
+def attend_kernel(plan, me, table, k_own, k_swap, v_own, v_swap, q, o):
     high, low, part = plan
-    q_refs, o_refs, o = refs[:high], refs[high:-1], refs[-1]
-    near, _, width = q_refs[0].shape
-    rows = v_own.shape[2]
+    near, _, rows, width = v_own.shape
     per_device = rows // TILE
-    spans = k_own.shape[0] // low * CORES
+    spans = near // low * CORES
     tiles_span = high * low * per_device
     keys, values = (k_own, k_swap), (v_own, v_swap)
-
-    for k in range(high):
-        o[pl.ds(k * near, near)] = q_refs[k][...]
+    ways = o.shape[0]
+    near_here = ways // high
 
     def column_of(j):
-        far, near_place = me[0] ^ (j // near), j % near
+        far, near_place = j // near_here, j % near_here
         return near_place // low * tiles_span + (far * low + near_place % low) * per_device + part
 
     def pair(step, carry):
@@ -132,7 +131,7 @@
                         chains.append((j, places, lane < count * (2 * TILE), pl.ds(head * DH, DH)))
                 scores = [
                     lax.dot_general(
-                        o[j, :, cols],
+                        q[j, pl.ds(part * TILE, TILE), cols],
                         gather(keys, places, cols),
                         (((1,), (1,)), ((), ())),
                         preferred_element_type=jnp.float32,
@@ -155,31 +154,25 @@
 
         return carry
 
-    lax.fori_loop(0, high * near // 2, pair, 0)
-    for k in range(high):
-        o_refs[0][pl.ds((me[0] ^ k) * near, near)] = o[pl.ds(k * near, near)]
-
-
-def attend(low, part, me, table, keys, values, q_blocks):
-    high = len(q_blocks)
-    near, rows, width = q_blocks[0].shape
-    ways = high * near
-    shapes = [(ways, rows, width)]
+    lax.fori_loop(0, ways // 2, pair, 0)
+
+
+def attend(high, low, part, me, table, keys, values, q):
+    ways, _, width = q.shape
     seen = keys[0].shape[0] // low * CORES * TILE
     return pl.pallas_call(
         functools.partial(attend_kernel, (high, low, part)),
-        in_specs=[SMEM, SMEM] + [VMEM] * (4 + high),
-        out_specs=[VMEM] * len(shapes),
-        out_shape=[jax.ShapeDtypeStruct(shape, q_blocks[0].dtype) for shape in shapes],
-        scratch_shapes=[pltpu.VMEM((ways, rows, width), q_blocks[0].dtype)],
+        in_specs=[SMEM, SMEM] + [VMEM] * 5,
+        out_specs=VMEM,
+        out_shape=jax.ShapeDtypeStruct((ways, TILE, width), q.dtype),
         compiler_params=pltpu.CompilerParams(vmem_limit_bytes=24 * 2**20),
         cost_estimate=pl.CostEstimate(
-            flops=4 * ways * rows * width * seen,
-            bytes_accessed=8 * keys[0].size + 4 * ways * rows * width,
-            transcendentals=ways * rows * width // DH * seen,
+            flops=4 * ways * TILE * width * seen,
+            bytes_accessed=8 * keys[0].size + 4 * ways * TILE * width,
+            transcendentals=ways * TILE * width // DH * seen,
         ),
         name="attend",
-    )(me, table, *keys, *values, *q_blocks)
+    )(me, table, *keys, *values, q)
 
 
 def body(queries, key_rows, value_rows, tile_lists, span_reach):
@@ -203,6 +196,9 @@
     def around(blocks):
         moved = [lax.ppermute(blocks[e], near_axes, [(i, i ^ e) for i in range(near)]) for e in range(1, near)]
         return [blocks[0]] + moved
+
+    def exchange(x):
+        return lax.all_to_all(x, ("far",) + near_axes, split_axis=0, concat_axis=0, tiled=True)
 
     def with_swapped(x):
         if not split_y:
@@ -224,26 +220,22 @@
     table = table.reshape(-1, 4).T.astype(jnp.int32)
 
     far_block, near_block, full = (near, rows, width), (high, rows, width), (near, high, rows, width)
-    keys = across(rearrange(far_columns, me, [key_rows], [(rows, near * width)] * high))
-    values = around(rearrange(near_columns, me, [value_rows], [near_block] * near))
-    q = around(rearrange(near_columns, me, [queries], [near_block] * near, [keys[-1], values[1]]))
-    q_parts = []
-    for part in range(per_device):
-        pick = functools.partial(far_of_near, part * TILE)
-        before = [values[-1]] if part else []
-        q_parts.append(across(rearrange(pick, me, q, [(near, TILE, width)] * high, before)))
-        if not part:
-            before = [q_parts[0][-1]]
-            values = across(rearrange(functools.partial(far_of_near, 0), me, values, [far_block] * high, before))
-    keys = around(rearrange(near_of_far, me, keys, [near_block] * near, q[1:] + [table]))
-    keys = with_swapped(rearrange(join_near, me, keys, [full], q_parts[0][1:-1])[0])
-    values = with_swapped(rearrange(join_far, me, values, [full])[0])
+    order = [0] + list(range(2, high)) + [1]
+    shape = (rows, near * width)
+    keys = list(rearrange(functools.partial(far_columns, order[:-1]), me, [key_rows], [shape] * (high - 1)))
+    values = around(rearrange(near_columns, me, [value_rows], [near_block] * near, keys[:1]))
+    keys[1:1] = rearrange(functools.partial(far_columns, order[-1:]), me, [key_rows], [shape], values[1:2])
+    keys = across(keys)
+    values = across(rearrange(functools.partial(far_of_near, 0), me, values, [far_block] * high, [keys[-1]]))
+    keys = around(rearrange(near_of_far, me, keys, [near_block] * near))
+    keys = rearrange(join_near, me, keys, [full])[0]
+    values = rearrange(join_far, me, values, [full])[0]
+    q = exchange(rearrange(all_columns, me, [queries], [(high * near, rows, width)], [keys, values])[0])
+    keys, values = with_swapped(keys), with_swapped(values)
     outs = []
     for part in range(per_device):
-        out = attend(low, part, me, table, keys, values, q_parts[part])[0]
-        if part + 1 < per_device:
-            out = rearrange(copy, me, [out], [out.shape], q_parts[part + 1][1:])[0]
-        out = lax.all_to_all(out, ("far",) + near_axes, split_axis=0, concat_axis=0, tiled=True)
+        out = attend(high, low, part, me, table, keys, values, q)
+        out = exchange(out)
         outs.append(out.transpose(1, 0, 2).reshape(TILE, depth))
     return jnp.concatenate(outs, axis=0)
 

time: 182 us -> 180 us (0.989)
  waiting for transfers between devices: 82.7 us -> 98.2 us
  starting transfers between devices: 60.9 us -> 51.2 us
  local copies, waits for them, and re-layouts: 15.4 us -> 8.48 us
    all_to_all x2 -> x3, waiting for transfers between devices: 24.2 us -> 53.4 us  [exchange(): lax.all_to_all(x, ('far',) + near_axes, split_axis=0, concat_axis=0, tile...]
    ppermute x12 -> x6, waiting for transfers between devices: 47.5 us -> 26.3 us  [across(): lax.ppermute(blocks[k], 'far', [(i, i ^ k) for i in range(high)])]
    ppermute x12 -> x6, starting transfers between devices: 35.1 us -> 16.5 us  [across(): lax.ppermute(blocks[k], 'far', [(i, i ^ k) for i in range(high)])]
    all_to_all x2 -> x3, starting transfers between devices: 12.3 us -> 23.6 us  [exchange(): lax.all_to_all(x, ('far',) + near_axes, split_axis=0, concat_axis=0, tile...]
    unnamed x56 -> x18, local copies, waits for them, and re-layouts: 13.3 us -> 6.45 us
    ppermute x1, waiting for transfers between devices: 0.01 us -> 5.51 us  [body(): lax.ppermute(table, 'y', [(i, i ^ step) for i in range(chips)])]
    pallas_call x10 -> x8, Pallas kernels: 9.95 us -> 5.28 us  [rearrange(): pl.pallas_call(held, in_specs=[SMEM] + [VMEM] * len(sources) + [ANY] * co...]
    pallas_call x2, Pallas kernels: 11.1 us -> 14.6 us  [attend(): pl.pallas_call(functools.partial(attend_kernel, (high, low, part)), in_sp...]
  transfers between devices with their start and end apart: 26 -> 18, of which waited for: 11 -> 11; matrix products, arithmetic and copies ran while one was open for 1% -> 1% of each run, Pallas kernels for 10% -> 6%
where the time goes in v5:
time: 180 us; the launch traced here: 179 us
  waiting for transfers between devices  98.2 us (55%)
  starting transfers between devices  51.2 us (28%)
  Pallas kernels  19.9 us (11%)
  local copies, waits for them, and re-layouts  8.48 us (5%)
    all_to_all x3, waiting for transfers between devices, exchange(): lax.all_to_all(x, ('far',) + near_axes, split_axis=0, concat_axis=0, tile...  53.4 us
    ppermute x6, waiting for transfers between devices, across(): lax.ppermute(blocks[k], 'far', [(i, i ^ k) for i in range(high)])  26.3 us
    all_to_all x3, starting transfers between devices, exchange(): lax.all_to_all(x, ('far',) + near_axes, split_axis=0, concat_axis=0, tile...  23.6 us
    ppermute x6, starting transfers between devices, across(): lax.ppermute(blocks[k], 'far', [(i, i ^ k) for i in range(high)])  16.5 us
    pallas_call x2, Pallas kernels, attend(): pl.pallas_call(functools.partial(attend_kernel, (high, low, part)), in_sp...  14.6 us
    ppermute x6, waiting for transfers between devices, around(): lax.ppermute(blocks[e], near_axes, [(i, i ^ e) for i in range(near)])  12.9 us
    ppermute x6, starting transfers between devices, around(): lax.ppermute(blocks[e], near_axes, [(i, i ^ e) for i in range(near)])  8.61 us
    unnamed x18, local copies, waits for them, and re-layouts  6.45 us
  transfers between devices with their start and end apart: 18, of which 11 were waited for; matrix products, arithmetic and copies ran while one was open for 1% of the time, Pallas kernels for 6%

profile of v5, /device:TPU:0, one launch (start us, length us, event | category | flops | bytes accessed | tf_op | source)
XLA Modules:
  0.0 179.3 jit_solution(6950129353128043857)
XLA Ops:
  0.1 1.4 copy-done
  2.1 1.4 copy-done.5
  4.2 3.0 %collective-permute-start.1 = (bf16[4,128,384]{2,1,0:T(8,128)(2,1)S(1)}, bf16[4,128,384]{2,1,0:T(8,128)(2,1)S(1)}, u32[]{:S(2)}, u32[]{:S(2)}) collective-permute-start(bf16[4,128,384]{2,1,0:T(8,128)(2,1)S(1)} %get-tuple-element.21), channel_id=1, source_target_pairs={{0,1},{1,0},{16,17},{17,16},{2,3},{3,2},{18,19},{19,18},{4,5},{5,4... | collective-permute-start | bytes 1179656 | tf_op jit(solution)/shard_map/ppermute | solution.py:197
  7.2 3.6 %collective-permute-start.4 = (bf16[128,1536]{1,0:T(8,128)(2,1)S(1)}, bf16[128,1536]{1,0:T(8,128)(2,1)S(1)}, u32[]{:S(2)}, u32[]{:S(2)}) collective-permute-start(bf16[128,1536]{1,0:T(8,128)(2,1)S(1)} %get-tuple-element.23), channel_id=1, source_target_pairs={{0,6},{2,4},{4,2},{6,0},{1,7},{3,5},{5,3},{7,1},{8,14},{10,12},{12... | collective-permute-start | bytes 1179656 | tf_op jit(solution)/shard_map/ppermute | solution.py:192
  10.8 1.5 collective-permute-start.9
  12.8 4.3 %collective-permute-done.1.refs_2_ = bf16[4,128,384]{2,1,0:T(8,128)(2,1)S(1)} collective-permute-done((bf16[4,128,384]{2,1,0:T(8,128)(2,1)S(1)}, bf16[4,128,384]{2,1,0:T(8,128)(2,1)S(1)}, u32[]{:S(2)}, u32[]{:S(2)}) %collective-permute-start.1) | collective-permute-done | bytes 393248 | tf_op jit(solution)/shard_map/ppermute | solution.py:197
  17.8 2.2 %collective-permute-start.2 = (bf16[128,1536]{1,0:T(8,128)(2,1)S(1)}, bf16[128,1536]{1,0:T(8,128)(2,1)S(1)}, u32[]{:S(2)}, u32[]{:S(2)}) collective-permute-start(bf16[128,1536]{1,0:T(8,128)(2,1)S(1)} %rearrange.10), channel_id=1, source_target_pairs={{0,2},{2,0},{4,6},{6,4},{1,3},{3,1},{5,7},{7,5},{8,10},{10,8},{12,... | collective-permute-start | bytes 1179656 | tf_op jit(solution)/shard_map/ppermute | solution.py:192
  20.0 1.2 collective-permute-done.4.refs_4_.refs_5_
  21.1 8.4 %collective-permute-done.9.refs_3_ = bf16[4,128,384]{2,1,0:T(8,128)(2,1)S(1)} collective-permute-done((bf16[4,128,384]{2,1,0:T(8,128)(2,1)S(1)}, bf16[4,128,384]{2,1,0:T(8,128)(2,1)S(1)}, u32[]{:S(2)}, u32[]{:S(2)}) %collective-permute-start.9) | collective-permute-done | bytes 393248 | tf_op jit(solution)/shard_map/ppermute | solution.py:197
  30.2 7.7 %collective-permute-start.11 = (bf16[4,128,384]{2,1,0:T(8,128)(2,1)S(1)}, bf16[4,128,384]{2,1,0:T(8,128)(2,1)S(1)}, u32[]{:S(2)}, u32[]{:S(2)}) collective-permute-start(bf16[4,128,384]{2,1,0:T(8,128)(2,1)S(1)} %get-tuple-element.32), channel_id=1, source_target_pairs={{0,2},{2,0},{4,6},{6,4},{1,3},{3,1},{5,7},{7,5},{8,10},{10,8},{12,... | collective-permute-start | bytes 1179656 | tf_op jit(solution)/shard_map/ppermute | solution.py:192
  38.0 1.6 collective-permute-start.12
  39.5 1.4 collective-permute-start.13
  40.9 6.1 %collective-permute-done.3.refs_3_ = bf16[128,1536]{1,0:T(8,128)(2,1)S(1)} collective-permute-done((bf16[128,1536]{1,0:T(8,128)(2,1)S(1)}, bf16[128,1536]{1,0:T(8,128)(2,1)S(1)}, u32[]{:S(2)}, u32[]{:S(2)}) %collective-permute-start.3) | collective-permute-done | bytes 393248 | tf_op jit(solution)/shard_map/ppermute | solution.py:192
  48.3 1.5 collective-permute-start.6
  49.8 9.6 %collective-permute-done.11.refs_2_ = bf16[4,128,384]{2,1,0:T(8,128)(2,1)S(1)} collective-permute-done((bf16[4,128,384]{2,1,0:T(8,128)(2,1)S(1)}, bf16[4,128,384]{2,1,0:T(8,128)(2,1)S(1)}, u32[]{:S(2)}, u32[]{:S(2)}) %collective-permute-start.11) | collective-permute-done | bytes 393248 | tf_op jit(solution)/shard_map/ppermute | solution.py:192
  59.4 1.5 collective-permute-start.7
  60.9 9.5 %collective-permute-done.12.refs_3_ = bf16[4,128,384]{2,1,0:T(8,128)(2,1)S(1)} collective-permute-done((bf16[4,128,384]{2,1,0:T(8,128)(2,1)S(1)}, bf16[4,128,384]{2,1,0:T(8,128)(2,1)S(1)}, u32[]{:S(2)}, u32[]{:S(2)}) %collective-permute-start.12) | collective-permute-done | bytes 393248 | tf_op jit(solution)/shard_map/ppermute | solution.py:192
  73.3 1.1 copy-done.2
  74.5 11.4 %all-to-all-start = ((bf16[16,128,384]{2,1,0:T(8,128)(2,1)}), bf16[16,128,384]{2,1,0:T(8,128)(2,1)}, u32[]{:S(2)}, u32[]{:S(2)}) async-start(bf16[16,128,384]{2,1,0:T(8,128)(2,1)} %copy-done.2), calls=%async_computation | async-start | bytes 3145728 | tf_op jit(solution)/shard_map/all_to_all | solution.py:201
  86.5 1.9 %collective-permute-start = (s32[16,3]{0,1:T(4,128)S(1)}, s32[16,3]{0,1:T(4,128)S(1)}, u32[]{:S(2)}, u32[]{:S(2)}) collective-permute-start(s32[16,3]{0,1:T(4,128)S(1)} %get-tuple-element.36), channel_id=1, source_target_pairs={{0,16},{16,0},{1,17},{17,1},{2,18},{18,2},{3,19},{19,3},{4,20},{20... | collective-permute-start | bytes 584 | tf_op jit(solution)/shard_map/ppermute | solution.py:212
  88.4 5.5 %collective-permute-done = s32[16,3]{0,1:T(4,128)S(1)} collective-permute-done((s32[16,3]{0,1:T(4,128)S(1)}, s32[16,3]{0,1:T(4,128)S(1)}, u32[]{:S(2)}, u32[]{:S(2)}) %collective-permute-start) | collective-permute-done | bytes 224 | tf_op jit(solution)/shard_map/ppermute | solution.py:212
  94.7 24.5 %all-to-all-done.q = bf16[16,128,384]{2,1,0:T(8,128)(2,1)} async-done(((bf16[16,128,384]{2,1,0:T(8,128)(2,1)}), bf16[16,128,384]{2,1,0:T(8,128)(2,1)}, u32[]{:S(2)}, u32[]{:S(2)}) %all-to-all-start) | async-done | bytes 1572896 | tf_op jit(solution)/shard_map/all_to_all | solution.py:201
  119.2 7.2 %attend.2 = bf16[16,64,384]{2,1,0:T(8,128)(2,1)S(1)} custom-call(s32[2]{0:T(128)S(1)} %pad_add_fusion.3.refs_0_.me, s32[4,32]{1,0:T(4,128)S(1)} %bitcast.18, bf16[4,4,128,384]{3,2,1,0:T(8,128)(2,1)S(1)} %rearrange.12.refs_2_.k_own, bf16[4,4,128,384]{3,2,1,0:T(8,128)(2,1)} %collective-permute-done.8.k_swap, ...), custom_call_target="tpu_custom_call" | custom-call | flops 402653184 | bytes 7864320 | tf_op jit(solution)/shard_map/attend/pallas_call | solution.py:163
  126.4 0.9 copy-done.4
  127.3 7.3 %all-to-all-start.1 = ((bf16[16,64,384]{2,1,0:T(8,128)(2,1)}), bf16[16,64,384]{2,1,0:T(8,128)(2,1)}, u32[]{:S(2)}, u32[]{:S(2)}) async-start(bf16[16,64,384]{2,1,0:T(8,128)(2,1)} %copy-done.4), calls=%async_computation.1 | async-start | bytes 1572864 | tf_op jit(solution)/shard_map/all_to_all | solution.py:201
  134.6 7.4 %attend.3 = bf16[16,64,384]{2,1,0:T(8,128)(2,1)S(1)} custom-call(s32[2]{0:T(128)S(1)} %pad_add_fusion.3.refs_0_.me, s32[4,32]{1,0:T(4,128)S(1)} %bitcast.19, bf16[4,4,128,384]{3,2,1,0:T(8,128)(2,1)S(1)} %rearrange.12.refs_2_.k_own, bf16[4,4,128,384]{3,2,1,0:T(8,128)(2,1)} %collective-permute-done.8.k_swap, ...), custom_call_target="tpu_custom_call" | custom-call | flops 402653184 | bytes 7864320 | tf_op jit(solution)/shard_map/attend/pallas_call | solution.py:163
  142.0 0.9 copy-done.3
  142.9 11.0 %all-to-all-done.1 = bf16[16,64,384]{2,1,0:T(8,128)(2,1)} async-done(((bf16[16,64,384]{2,1,0:T(8,128)(2,1)}), bf16[16,64,384]{2,1,0:T(8,128)(2,1)}, u32[]{:S(2)}, u32[]{:S(2)}) %all-to-all-start.1) | async-done | bytes 786464 | tf_op jit(solution)/shard_map/all_to_all | solution.py:201
  153.9 4.9 %all-to-all-start.2 = ((bf16[16,64,384]{2,1,0:T(8,128)(2,1)}), bf16[16,64,384]{2,1,0:T(8,128)(2,1)S(1)}, u32[]{:S(2)}, u32[]{:S(2)}) async-start(bf16[16,64,384]{2,1,0:T(8,128)(2,1)} %copy-done.3), calls=%async_computation.2 | async-start | bytes 1572864 | tf_op jit(solution)/shard_map/all_to_all | solution.py:201
  158.8 1.2 copy.10
  160.1 17.9 %all-to-all-done.2 = bf16[16,64,384]{2,1,0:T(8,128)(2,1)S(1)} async-done(((bf16[16,64,384]{2,1,0:T(8,128)(2,1)}), bf16[16,64,384]{2,1,0:T(8,128)(2,1)S(1)}, u32[]{:S(2)}, u32[]{:S(2)}) %all-to-all-start.2) | async-done | bytes 786464 | tf_op jit(solution)/shard_map/all_to_all | solution.py:201
  178.1 1.3 pad_maximum_fusion
  (46 shorter events, 8.7 us)
Async XLA Ops:
  0.1 1.4 copy-start
  1.5 15.7 %copy-start.1 = (bf16[128,6144]{1,0:T(8,128)(2,1)S(1)}, bf16[128,6144]{1,0:T(8,128)(2,1)}, u32[]{:S(2)}) copy-start(bf16[128,6144]{1,0:T(8,128)(2,1)} %refs_1_.6) | copy-start | bytes 4718596
  2.1 1.4 copy-start.5
  4.2 12.9 %collective-permute-start.1 = (bf16[4,128,384]{2,1,0:T(8,128)(2,1)S(1)}, bf16[4,128,384]{2,1,0:T(8,128)(2,1)S(1)}, u32[]{:S(2)}, u32[]{:S(2)}) collective-permute-start(bf16[4,128,384]{2,1,0:T(8,128)(2,1)S(1)} %get-tuple-element.21), channel_id=1, source_target_pairs={{0,1},{1,0},{16,17},{17,16},{2,3},{3,2},{18,19},{19,18},{4,5},{5,4... | collective-permute-start | bytes 1179656 | tf_op jit(solution)/shard_map/ppermute | solution.py:197
  7.2 13.9 %collective-permute-start.4 = (bf16[128,1536]{1,0:T(8,128)(2,1)S(1)}, bf16[128,1536]{1,0:T(8,128)(2,1)S(1)}, u32[]{:S(2)}, u32[]{:S(2)}) collective-permute-start(bf16[128,1536]{1,0:T(8,128)(2,1)S(1)} %get-tuple-element.23), channel_id=1, source_target_pairs={{0,6},{2,4},{4,2},{6,0},{1,7},{3,5},{5,3},{7,1},{8,14},{10,12},{12... | collective-permute-start | bytes 1179656 | tf_op jit(solution)/shard_map/ppermute | solution.py:192
  10.8 18.7 %collective-permute-start.9 = (bf16[4,128,384]{2,1,0:T(8,128)(2,1)S(1)}, bf16[4,128,384]{2,1,0:T(8,128)(2,1)S(1)}, u32[]{:S(2)}, u32[]{:S(2)}) collective-permute-start(bf16[4,128,384]{2,1,0:T(8,128)(2,1)S(1)} %get-tuple-element.29), channel_id=1, source_target_pairs={{0,16},{1,17},{16,0},{17,1},{2,18},{3,19},{18,2},{19,3},{4,20},{5,... | collective-permute-start | bytes 1179656 | tf_op jit(solution)/shard_map/ppermute | solution.py:197
  12.3 17.2 %collective-permute-start.10 = (bf16[4,128,384]{2,1,0:T(8,128)(2,1)S(1)}, bf16[4,128,384]{2,1,0:T(8,128)(2,1)S(1)}, u32[]{:S(2)}, u32[]{:S(2)}) collective-permute-start(bf16[4,128,384]{2,1,0:T(8,128)(2,1)S(1)} %get-tuple-element.30), channel_id=1, source_target_pairs={{0,17},{1,16},{16,1},{17,0},{2,19},{3,18},{18,3},{19,2},{4,21},{5,... | collective-permute-start | bytes 1179656 | tf_op jit(solution)/shard_map/ppermute | solution.py:197
  12.8 34.2 %collective-permute-start.3 = (bf16[128,1536]{1,0:T(8,128)(2,1)S(1)}, bf16[128,1536]{1,0:T(8,128)(2,1)S(1)}, u32[]{:S(2)}, u32[]{:S(2)}) collective-permute-start(bf16[128,1536]{1,0:T(8,128)(2,1)S(1)} %get-tuple-element.22), channel_id=1, source_target_pairs={{0,4},{2,6},{4,0},{6,2},{1,5},{3,7},{5,1},{7,3},{8,12},{10,14},{12... | collective-permute-start | bytes 1179656 | tf_op jit(solution)/shard_map/ppermute | solution.py:192
  17.8 29.3 %collective-permute-start.2 = (bf16[128,1536]{1,0:T(8,128)(2,1)S(1)}, bf16[128,1536]{1,0:T(8,128)(2,1)S(1)}, u32[]{:S(2)}, u32[]{:S(2)}) collective-permute-start(bf16[128,1536]{1,0:T(8,128)(2,1)S(1)} %rearrange.10), channel_id=1, source_target_pairs={{0,2},{2,0},{4,6},{6,4},{1,3},{3,1},{5,7},{7,5},{8,10},{10,8},{12,... | collective-permute-start | bytes 1179656 | tf_op jit(solution)/shard_map/ppermute | solution.py:192
  30.2 29.2 %collective-permute-start.11 = (bf16[4,128,384]{2,1,0:T(8,128)(2,1)S(1)}, bf16[4,128,384]{2,1,0:T(8,128)(2,1)S(1)}, u32[]{:S(2)}, u32[]{:S(2)}) collective-permute-start(bf16[4,128,384]{2,1,0:T(8,128)(2,1)S(1)} %get-tuple-element.32), channel_id=1, source_target_pairs={{0,2},{2,0},{4,6},{6,4},{1,3},{3,1},{5,7},{7,5},{8,10},{10,8},{12,... | collective-permute-start | bytes 1179656 | tf_op jit(solution)/shard_map/ppermute | solution.py:192
  38.0 32.4 %collective-permute-start.12 = (bf16[4,128,384]{2,1,0:T(8,128)(2,1)S(1)}, bf16[4,128,384]{2,1,0:T(8,128)(2,1)S(1)}, u32[]{:S(2)}, u32[]{:S(2)}) collective-permute-start(bf16[4,128,384]{2,1,0:T(8,128)(2,1)S(1)} %get-tuple-element.33), channel_id=1, source_target_pairs={{0,4},{2,6},{4,0},{6,2},{1,5},{3,7},{5,1},{7,3},{8,12},{10,14},{12... | collective-permute-start | bytes 1179656 | tf_op jit(solution)/shard_map/ppermute | solution.py:192
  39.5 30.9 %collective-permute-start.13 = (bf16[4,128,384]{2,1,0:T(8,128)(2,1)S(1)}, bf16[4,128,384]{2,1,0:T(8,128)(2,1)S(1)}, u32[]{:S(2)}, u32[]{:S(2)}) collective-permute-start(bf16[4,128,384]{2,1,0:T(8,128)(2,1)S(1)} %get-tuple-element.34), channel_id=1, source_target_pairs={{0,6},{2,4},{4,2},{6,0},{1,7},{3,5},{5,3},{7,1},{8,14},{10,12},{12... | collective-permute-start | bytes 1179656 | tf_op jit(solution)/shard_map/ppermute | solution.py:192
  47.7 23.4 %collective-permute-start.5 = (bf16[4,128,384]{2,1,0:T(8,128)(2,1)S(1)}, bf16[4,128,384]{2,1,0:T(8,128)(2,1)S(1)}, u32[]{:S(2)}, u32[]{:S(2)}) collective-permute-start(bf16[4,128,384]{2,1,0:T(8,128)(2,1)S(1)} %get-tuple-element.25), channel_id=1, source_target_pairs={{0,1},{1,0},{16,17},{17,16},{2,3},{3,2},{18,19},{19,18},{4,5},{5,4... | collective-permute-start | bytes 1179656 | tf_op jit(solution)/shard_map/ppermute | solution.py:197
  48.3 22.8 %collective-permute-start.6 = (bf16[4,128,384]{2,1,0:T(8,128)(2,1)S(1)}, bf16[4,128,384]{2,1,0:T(8,128)(2,1)S(1)}, u32[]{:S(2)}, u32[]{:S(2)}) collective-permute-start(bf16[4,128,384]{2,1,0:T(8,128)(2,1)S(1)} %get-tuple-element.26), channel_id=1, source_target_pairs={{0,16},{1,17},{16,0},{17,1},{2,18},{3,19},{18,2},{19,3},{4,20},{5,... | collective-permute-start | bytes 1179656 | tf_op jit(solution)/shard_map/ppermute | solution.py:197
  59.4 11.8 %collective-permute-start.7 = (bf16[4,128,384]{2,1,0:T(8,128)(2,1)S(1)}, bf16[4,128,384]{2,1,0:T(8,128)(2,1)S(1)}, u32[]{:S(2)}, u32[]{:S(2)}) collective-permute-start(bf16[4,128,384]{2,1,0:T(8,128)(2,1)S(1)} %get-tuple-element.27), channel_id=1, source_target_pairs={{0,17},{1,16},{16,1},{17,0},{2,19},{3,18},{18,3},{19,2},{4,21},{5,... | collective-permute-start | bytes 1179656 | tf_op jit(solution)/shard_map/ppermute | solution.py:197
  71.2 1.4 copy-start.6
  73.3 1.1 copy-start.2
  74.5 12.0 %copy-start.7 = (s32[1,16,2]{1,2,0:T(2,128)S(1)}, s32[1,16,2]{1,2,0:T(2,128)}, u32[]{:S(2)}) copy-start(s32[1,16,2]{1,2,0:T(2,128)} %param.8) | copy-start | bytes 388
  74.5 12.0 %copy-start.8 = (s32[1,16]{1,0:T(1,128)S(1)}, s32[1,16]{1,0:T(1,128)}, u32[]{:S(2)}) copy-start(s32[1,16]{1,0:T(1,128)} %param.9) | copy-start | bytes 196
  74.5 44.7 %all-to-all-start = ((bf16[16,128,384]{2,1,0:T(8,128)(2,1)}), bf16[16,128,384]{2,1,0:T(8,128)(2,1)}, u32[]{:S(2)}, u32[]{:S(2)}) async-start(bf16[16,128,384]{2,1,0:T(8,128)(2,1)} %copy-done.2), calls=%async_computation | async-start | bytes 3145728 | tf_op jit(solution)/shard_map/all_to_all | solution.py:201
  85.9 8.8 %collective-permute-start.14 = (bf16[4,4,128,384]{3,2,1,0:T(8,128)(2,1)S(1)}, bf16[4,4,128,384]{3,2,1,0:T(8,128)(2,1)}, u32[]{:S(2)}, u32[]{:S(2)}) collective-permute-start(bf16[4,4,128,384]{3,2,1,0:T(8,128)(2,1)S(1)} %rearrange.14.refs_3_.v_own), channel_id=1, source_target_pairs={{0,8},{8,0},{1,9},{9,1},{2,10},{10,2},{3,11},{11,3},{4,12},{12,4},... | collective-permute-start | bytes 4718600 | tf_op jit(solution)/shard_map/ppermute | solution.py:206
  86.0 8.7 %collective-permute-start.8 = (bf16[4,4,128,384]{3,2,1,0:T(8,128)(2,1)S(1)}, bf16[4,4,128,384]{3,2,1,0:T(8,128)(2,1)}, u32[]{:S(2)}, u32[]{:S(2)}) collective-permute-start(bf16[4,4,128,384]{3,2,1,0:T(8,128)(2,1)S(1)} %rearrange.12.refs_2_.k_own), channel_id=1, source_target_pairs={{0,8},{8,0},{1,9},{9,1},{2,10},{10,2},{3,11},{11,3},{4,12},{12,4},... | collective-permute-start | bytes 4718600 | tf_op jit(solution)/shard_map/ppermute | solution.py:206
  86.5 7.4 %collective-permute-start = (s32[16,3]{0,1:T(4,128)S(1)}, s32[16,3]{0,1:T(4,128)S(1)}, u32[]{:S(2)}, u32[]{:S(2)}) collective-permute-start(s32[16,3]{0,1:T(4,128)S(1)} %get-tuple-element.36), channel_id=1, source_target_pairs={{0,16},{16,0},{1,17},{17,1},{2,18},{18,2},{3,19},{19,3},{4,20},{20... | collective-permute-start | bytes 584 | tf_op jit(solution)/shard_map/ppermute | solution.py:212
  126.4 0.9 copy-start.4
  127.3 26.7 %all-to-all-start.1 = ((bf16[16,64,384]{2,1,0:T(8,128)(2,1)}), bf16[16,64,384]{2,1,0:T(8,128)(2,1)}, u32[]{:S(2)}, u32[]{:S(2)}) async-start(bf16[16,64,384]{2,1,0:T(8,128)(2,1)} %copy-done.4), calls=%async_computation.1 | async-start | bytes 1572864 | tf_op jit(solution)/shard_map/all_to_all | solution.py:201
  142.0 0.9 copy-start.3
  153.9 24.0 %all-to-all-start.2 = ((bf16[16,64,384]{2,1,0:T(8,128)(2,1)}), bf16[16,64,384]{2,1,0:T(8,128)(2,1)S(1)}, u32[]{:S(2)}, u32[]{:S(2)}) async-start(bf16[16,64,384]{2,1,0:T(8,128)(2,1)} %copy-done.3), calls=%async_computation.2 | async-start | bytes 1572864 | tf_op jit(solution)/shard_map/all_to_all | solution.py:201

commit v6 on v5

--- a/solution.py
+++ b/solution.py
@@ -71,20 +71,24 @@
             out[me[1] ^ e] = source[k, pl.ds(start, rows), :]
 
 
-def all_columns(me, source, out):
-    ways, _, width = out.shape
-    for way in range(ways):
-        out[way] = source[:, pl.ds(way * width, width)]
-
-
-def join_near(me, *refs):
-    for e, source in enumerate(refs[:-1]):
-        refs[-1][me[1] ^ e] = source[...]
-
-
-def join_far(me, *refs):
-    for k, source in enumerate(refs[:-1]):
-        refs[-1][:, k] = source[...]
+def all_columns(me, source, *outs):
+    for part, out in enumerate(outs):
+        ways, rows, width = out.shape
+        for way in range(ways):
+            out[way] = source[pl.ds(part * rows, rows), pl.ds(way * width, width)]
+
+
+def gather_all(high, near, me, *refs):
+    k_blocks, v_blocks, q, outs = refs[:near], refs[near : near + high], refs[near + high], refs[near + high + 1 :]
+    keys, values, parts = outs[0], outs[1], outs[2:]
+    for part, out in enumerate(parts):
+        ways, rows, width = out.shape
+        for way in range(ways):
+            out[way] = q[pl.ds(part * rows, rows), pl.ds(way * width, width)]
+    for e, block in enumerate(k_blocks):
+        keys[me[1] ^ e] = block[...]
+    for k, block in enumerate(v_blocks):
+        values[:, k] = block[...]
 
 
 def attend_kernel(plan, me, table, k_own, k_swap, v_own, v_swap, q, o):
@@ -131,7 +135,7 @@
                         chains.append((j, places, lane < count * (2 * TILE), pl.ds(head * DH, DH)))
                 scores = [
                     lax.dot_general(
-                        q[j, pl.ds(part * TILE, TILE), cols],
+                        q[j, :, cols],
                         gather(keys, places, cols),
                         (((1,), (1,)), ((), ())),
                         preferred_element_type=jnp.float32,
@@ -228,13 +232,14 @@
     keys = across(keys)
     values = across(rearrange(functools.partial(far_of_near, 0), me, values, [far_block] * high, [keys[-1]]))
     keys = around(rearrange(near_of_far, me, keys, [near_block] * near))
-    keys = rearrange(join_near, me, keys, [full])[0]
-    values = rearrange(join_far, me, values, [full])[0]
-    q = exchange(rearrange(all_columns, me, [queries], [(high * near, rows, width)], [keys, values])[0])
+    shapes = [full, full] + [(high * near, TILE, width)] * per_device
+    gather = functools.partial(gather_all, high, near)
+    keys, values, *q_parts = rearrange(gather, me, [*keys, *values, queries], shapes)
+    q_parts = [exchange(q) for q in q_parts]
     keys, values = with_swapped(keys), with_swapped(values)
     outs = []
     for part in range(per_device):
-        out = attend(high, low, part, me, table, keys, values, q)
+        out = attend(high, low, part, me, table, keys, values, q_parts[part])
         out = exchange(out)
         outs.append(out.transpose(1, 0, 2).reshape(TILE, depth))
     return jnp.concatenate(outs, axis=0)

time: 180 us -> 176 us (0.978)
  waiting for transfers between devices: 98.2 us -> 94.2 us
  starting transfers between devices: 51.2 us -> 53.1 us
    ppermute x1, waiting for transfers between devices: 5.51 us -> 2.25 us  [body(): lax.ppermute(table, 'y', [(i, i ^ step) for i in range(chips)])]
    all_to_all x3 -> x4, starting transfers between devices: 23.6 us -> 25.5 us  [exchange(): lax.all_to_all(x, ('far',) + near_axes, split_axis=0, concat_axis=0, tile...]
    all_to_all x3 -> x4, waiting for transfers between devices: 53.4 us -> 52.1 us  [exchange(): lax.all_to_all(x, ('far',) + near_axes, split_axis=0, concat_axis=0, tile...]
    pallas_call x8 -> x6, Pallas kernels: 5.28 us -> 4.2 us  [rearrange(): pl.pallas_call(held, in_specs=[SMEM] + [VMEM] * len(sources) + [ANY] * co...]
    unnamed x18 -> x20, local copies, waits for them, and re-layouts: 6.45 us -> 6.37 us
  transfers between devices with their start and end apart: 18 -> 19, of which waited for: 11 -> 12; matrix products, arithmetic and copies ran while one was open for 1% -> 1% of each run, Pallas kernels for 6% -> 9%
where the time goes in v6:
time: 176 us; the launch traced here: 175 us
  waiting for transfers between devices  94.2 us (54%)
  starting transfers between devices  53.1 us (30%)
  Pallas kernels  18.1 us (10%)
  local copies, waits for them, and re-layouts  8.4 us (5%)
    all_to_all x4, waiting for transfers between devices, exchange(): lax.all_to_all(x, ('far',) + near_axes, split_axis=0, concat_axis=0, tile...  52.1 us
    ppermute x6, waiting for transfers between devices, across(): lax.ppermute(blocks[k], 'far', [(i, i ^ k) for i in range(high)])  26.3 us
    all_to_all x4, starting transfers between devices, exchange(): lax.all_to_all(x, ('far',) + near_axes, split_axis=0, concat_axis=0, tile...  25.5 us
    ppermute x6, starting transfers between devices, across(): lax.ppermute(blocks[k], 'far', [(i, i ^ k) for i in range(high)])  16.5 us
    pallas_call x2, Pallas kernels, attend(): pl.pallas_call(functools.partial(attend_kernel, (high, low, part)), in_sp...  13.9 us
    ppermute x6, waiting for transfers between devices, around(): lax.ppermute(blocks[e], near_axes, [(i, i ^ e) for i in range(near)])  13.6 us
    ppermute x6, starting transfers between devices, around(): lax.ppermute(blocks[e], near_axes, [(i, i ^ e) for i in range(near)])  8.61 us
    unnamed x20, local copies, waits for them, and re-layouts  6.37 us
  transfers between devices with their start and end apart: 19, of which 12 were waited for; matrix products, arithmetic and copies ran while one was open for 1% of the time, Pallas kernels for 9%

profile of v6, /device:TPU:0, one launch (start us, length us, event | category | flops | bytes accessed | tf_op | source)
XLA Modules:
  0.0 175.4 jit_solution(6144126427357171088)
XLA Ops:
  0.1 1.4 copy-done
  2.1 1.4 copy-done.5
  4.2 3.0 %collective-permute-start.1 = (bf16[4,128,384]{2,1,0:T(8,128)(2,1)S(1)}, bf16[4,128,384]{2,1,0:T(8,128)(2,1)S(1)}, u32[]{:S(2)}, u32[]{:S(2)}) collective-permute-start(bf16[4,128,384]{2,1,0:T(8,128)(2,1)S(1)} %get-tuple-element.25), channel_id=1, source_target_pairs={{0,1},{1,0},{16,17},{17,16},{2,3},{3,2},{18,19},{19,18},{4,5},{5,4... | collective-permute-start | bytes 1179656 | tf_op jit(solution)/shard_map/ppermute | solution.py:201
  7.2 3.6 %collective-permute-start.4 = (bf16[128,1536]{1,0:T(8,128)(2,1)S(1)}, bf16[128,1536]{1,0:T(8,128)(2,1)S(1)}, u32[]{:S(2)}, u32[]{:S(2)}) collective-permute-start(bf16[128,1536]{1,0:T(8,128)(2,1)S(1)} %get-tuple-element.27), channel_id=1, source_target_pairs={{0,6},{2,4},{4,2},{6,0},{1,7},{3,5},{5,3},{7,1},{8,14},{10,12},{12... | collective-permute-start | bytes 1179656 | tf_op jit(solution)/shard_map/ppermute | solution.py:196
  10.8 1.5 collective-permute-start.8
  12.8 4.3 %collective-permute-done.1.refs_2_ = bf16[4,128,384]{2,1,0:T(8,128)(2,1)S(1)} collective-permute-done((bf16[4,128,384]{2,1,0:T(8,128)(2,1)S(1)}, bf16[4,128,384]{2,1,0:T(8,128)(2,1)S(1)}, u32[]{:S(2)}, u32[]{:S(2)}) %collective-permute-start.1) | collective-permute-done | bytes 393248 | tf_op jit(solution)/shard_map/ppermute | solution.py:201
  17.8 2.2 %collective-permute-start.2 = (bf16[128,1536]{1,0:T(8,128)(2,1)S(1)}, bf16[128,1536]{1,0:T(8,128)(2,1)S(1)}, u32[]{:S(2)}, u32[]{:S(2)}) collective-permute-start(bf16[128,1536]{1,0:T(8,128)(2,1)S(1)} %rearrange.8), channel_id=1, source_target_pairs={{0,2},{2,0},{4,6},{6,4},{1,3},{3,1},{5,7},{7,5},{8,10},{10,8},{12,... | collective-permute-start | bytes 1179656 | tf_op jit(solution)/shard_map/ppermute | solution.py:196
  20.0 1.2 collective-permute-done.4.refs_4_.refs_5_
  21.1 8.4 %collective-permute-done.8.refs_3_ = bf16[4,128,384]{2,1,0:T(8,128)(2,1)S(1)} collective-permute-done((bf16[4,128,384]{2,1,0:T(8,128)(2,1)S(1)}, bf16[4,128,384]{2,1,0:T(8,128)(2,1)S(1)}, u32[]{:S(2)}, u32[]{:S(2)}) %collective-permute-start.8) | collective-permute-done | bytes 393248 | tf_op jit(solution)/shard_map/ppermute | solution.py:201
  30.2 7.8 %collective-permute-start.10 = (bf16[4,128,384]{2,1,0:T(8,128)(2,1)S(1)}, bf16[4,128,384]{2,1,0:T(8,128)(2,1)S(1)}, u32[]{:S(2)}, u32[]{:S(2)}) collective-permute-start(bf16[4,128,384]{2,1,0:T(8,128)(2,1)S(1)} %get-tuple-element.36), channel_id=1, source_target_pairs={{0,2},{2,0},{4,6},{6,4},{1,3},{3,1},{5,7},{7,5},{8,10},{10,8},{12,... | collective-permute-start | bytes 1179656 | tf_op jit(solution)/shard_map/ppermute | solution.py:196
  38.0 1.6 collective-permute-start.11
  39.6 1.4 collective-permute-start.12
  40.9 6.1 %collective-permute-done.3.refs_3_ = bf16[128,1536]{1,0:T(8,128)(2,1)S(1)} collective-permute-done((bf16[128,1536]{1,0:T(8,128)(2,1)S(1)}, bf16[128,1536]{1,0:T(8,128)(2,1)S(1)}, u32[]{:S(2)}, u32[]{:S(2)}) %collective-permute-start.3) | collective-permute-done | bytes 393248 | tf_op jit(solution)/shard_map/ppermute | solution.py:196
  48.3 1.5 collective-permute-start.6
  49.8 9.6 %collective-permute-done.10.refs_6_ = bf16[4,128,384]{2,1,0:T(8,128)(2,1)S(1)} collective-permute-done((bf16[4,128,384]{2,1,0:T(8,128)(2,1)S(1)}, bf16[4,128,384]{2,1,0:T(8,128)(2,1)S(1)}, u32[]{:S(2)}, u32[]{:S(2)}) %collective-permute-start.10) | collective-permute-done | bytes 393248 | tf_op jit(solution)/shard_map/ppermute | solution.py:196
  59.4 1.5 collective-permute-start.7
  60.9 9.5 %collective-permute-done.11.refs_7_ = bf16[4,128,384]{2,1,0:T(8,128)(2,1)S(1)} collective-permute-done((bf16[4,128,384]{2,1,0:T(8,128)(2,1)S(1)}, bf16[4,128,384]{2,1,0:T(8,128)(2,1)S(1)}, u32[]{:S(2)}, u32[]{:S(2)}) %collective-permute-start.11) | collective-permute-done | bytes 393248 | tf_op jit(solution)/shard_map/ppermute | solution.py:196
  71.2 0.9 rearrange.11
  74.0 10.7 %all-to-all-start = ((bf16[16,64,384]{2,1,0:T(8,128)(2,1)}), bf16[16,64,384]{2,1,0:T(8,128)(2,1)}, u32[]{:S(2)}, u32[]{:S(2)}) async-start(bf16[16,64,384]{2,1,0:T(8,128)(2,1)} %copy-done.7), calls=%async_computation | async-start | bytes 1572864 | tf_op jit(solution)/shard_map/all_to_all | solution.py:205
  85.3 18.1 %all-to-all-done.q = bf16[16,64,384]{2,1,0:T(8,128)(2,1)} async-done(((bf16[16,64,384]{2,1,0:T(8,128)(2,1)}), bf16[16,64,384]{2,1,0:T(8,128)(2,1)}, u32[]{:S(2)}, u32[]{:S(2)}) %all-to-all-start) | async-done | bytes 786464 | tf_op jit(solution)/shard_map/all_to_all | solution.py:205
  103.3 4.9 %all-to-all-start.2 = ((bf16[16,64,384]{2,1,0:T(8,128)(2,1)}), bf16[16,64,384]{2,1,0:T(8,128)(2,1)}, u32[]{:S(2)}, u32[]{:S(2)}) async-start(bf16[16,64,384]{2,1,0:T(8,128)(2,1)} %copy-done.6), calls=%async_computation.2 | async-start | bytes 1572864 | tf_op jit(solution)/shard_map/all_to_all | solution.py:205
  108.3 1.9 %collective-permute-start = (s32[16,3]{0,1:T(4,128)S(1)}, s32[16,3]{0,1:T(4,128)S(1)}, u32[]{:S(2)}, u32[]{:S(2)}) collective-permute-start(s32[16,3]{0,1:T(4,128)S(1)} %get-tuple-element.44), channel_id=1, source_target_pairs={{0,16},{16,0},{1,17},{17,1},{2,18},{18,2},{3,19},{19,3},{4,20},{20... | collective-permute-start | bytes 584 | tf_op jit(solution)/shard_map/ppermute | solution.py:216
  110.3 2.3 %collective-permute-done = s32[16,3]{0,1:T(4,128)S(1)} collective-permute-done((s32[16,3]{0,1:T(4,128)S(1)}, s32[16,3]{0,1:T(4,128)S(1)}, u32[]{:S(2)}, u32[]{:S(2)}) %collective-permute-start) | collective-permute-done | bytes 224 | tf_op jit(solution)/shard_map/ppermute | solution.py:216
  113.3 6.9 %attend.2 = bf16[16,64,384]{2,1,0:T(8,128)(2,1)S(1)} custom-call(s32[2]{0:T(128)S(1)} %pad_add_fusion.3.refs_0_.me, s32[4,32]{1,0:T(4,128)S(1)} %bitcast.18, bf16[4,4,128,384]{3,2,1,0:T(8,128)(2,1)S(1)} %get-tuple-element.39.k_own, bf16[4,4,128,384]{3,2,1,0:T(8,128)(2,1)} %collective-permute-done.13.k_swap, ...), custom_call_target="tpu_custom_call" | custom-call | flops 402653184 | bytes 7864320 | tf_op jit(solution)/shard_map/attend/pallas_call | solution.py:167
  121.1 5.8 %all-to-all-done.2.q = bf16[16,64,384]{2,1,0:T(8,128)(2,1)} async-done(((bf16[16,64,384]{2,1,0:T(8,128)(2,1)}), bf16[16,64,384]{2,1,0:T(8,128)(2,1)}, u32[]{:S(2)}, u32[]{:S(2)}) %all-to-all-start.2) | async-done | bytes 786464 | tf_op jit(solution)/shard_map/all_to_all | solution.py:205
  126.9 4.9 %all-to-all-start.1 = ((bf16[16,64,384]{2,1,0:T(8,128)(2,1)}), bf16[16,64,384]{2,1,0:T(8,128)(2,1)}, u32[]{:S(2)}, u32[]{:S(2)}) async-start(bf16[16,64,384]{2,1,0:T(8,128)(2,1)} %copy-done.2), calls=%async_computation.1 | async-start | bytes 1572864 | tf_op jit(solution)/shard_map/all_to_all | solution.py:205
  131.9 6.9 %attend.3 = bf16[16,64,384]{2,1,0:T(8,128)(2,1)S(1)} custom-call(s32[2]{0:T(128)S(1)} %pad_add_fusion.3.refs_0_.me, s32[4,32]{1,0:T(4,128)S(1)} %bitcast.19, bf16[4,4,128,384]{3,2,1,0:T(8,128)(2,1)S(1)} %get-tuple-element.39.k_own, bf16[4,4,128,384]{3,2,1,0:T(8,128)(2,1)} %collective-permute-done.13.k_swap, ...), custom_call_target="tpu_custom_call" | custom-call | flops 402653184 | bytes 7864320 | tf_op jit(solution)/shard_map/attend/pallas_call | solution.py:167
  139.7 10.8 %all-to-all-done.1 = bf16[16,64,384]{2,1,0:T(8,128)(2,1)} async-done(((bf16[16,64,384]{2,1,0:T(8,128)(2,1)}), bf16[16,64,384]{2,1,0:T(8,128)(2,1)}, u32[]{:S(2)}, u32[]{:S(2)}) %all-to-all-start.1) | async-done | bytes 786464 | tf_op jit(solution)/shard_map/all_to_all | solution.py:205
  150.5 4.9 %all-to-all-start.3 = ((bf16[16,64,384]{2,1,0:T(8,128)(2,1)}), bf16[16,64,384]{2,1,0:T(8,128)(2,1)S(1)}, u32[]{:S(2)}, u32[]{:S(2)}) async-start(bf16[16,64,384]{2,1,0:T(8,128)(2,1)} %copy-done.3), calls=%async_computation.3 | async-start | bytes 1572864 | tf_op jit(solution)/shard_map/all_to_all | solution.py:205
  155.4 1.2 copy.10
  156.7 17.4 %all-to-all-done.3 = bf16[16,64,384]{2,1,0:T(8,128)(2,1)S(1)} async-done(((bf16[16,64,384]{2,1,0:T(8,128)(2,1)}), bf16[16,64,384]{2,1,0:T(8,128)(2,1)S(1)}, u32[]{:S(2)}, u32[]{:S(2)}) %all-to-all-start.3) | async-done | bytes 786464 | tf_op jit(solution)/shard_map/all_to_all | solution.py:205
  174.1 1.3 pad_maximum_fusion
  (48 shorter events, 10.2 us)
Async XLA Ops:
  0.1 1.4 copy-start
  1.5 15.7 %copy-start.1 = (bf16[128,6144]{1,0:T(8,128)(2,1)S(1)}, bf16[128,6144]{1,0:T(8,128)(2,1)}, u32[]{:S(2)}) copy-start(bf16[128,6144]{1,0:T(8,128)(2,1)} %refs_1_.5) | copy-start | bytes 4718596
  2.1 1.4 copy-start.5
  4.2 12.9 %collective-permute-start.1 = (bf16[4,128,384]{2,1,0:T(8,128)(2,1)S(1)}, bf16[4,128,384]{2,1,0:T(8,128)(2,1)S(1)}, u32[]{:S(2)}, u32[]{:S(2)}) collective-permute-start(bf16[4,128,384]{2,1,0:T(8,128)(2,1)S(1)} %get-tuple-element.25), channel_id=1, source_target_pairs={{0,1},{1,0},{16,17},{17,16},{2,3},{3,2},{18,19},{19,18},{4,5},{5,4... | collective-permute-start | bytes 1179656 | tf_op jit(solution)/shard_map/ppermute | solution.py:201
  7.2 13.9 %collective-permute-start.4 = (bf16[128,1536]{1,0:T(8,128)(2,1)S(1)}, bf16[128,1536]{1,0:T(8,128)(2,1)S(1)}, u32[]{:S(2)}, u32[]{:S(2)}) collective-permute-start(bf16[128,1536]{1,0:T(8,128)(2,1)S(1)} %get-tuple-element.27), channel_id=1, source_target_pairs={{0,6},{2,4},{4,2},{6,0},{1,7},{3,5},{5,3},{7,1},{8,14},{10,12},{12... | collective-permute-start | bytes 1179656 | tf_op jit(solution)/shard_map/ppermute | solution.py:196
  10.8 18.7 %collective-permute-start.8 = (bf16[4,128,384]{2,1,0:T(8,128)(2,1)S(1)}, bf16[4,128,384]{2,1,0:T(8,128)(2,1)S(1)}, u32[]{:S(2)}, u32[]{:S(2)}) collective-permute-start(bf16[4,128,384]{2,1,0:T(8,128)(2,1)S(1)} %get-tuple-element.33), channel_id=1, source_target_pairs={{0,16},{1,17},{16,0},{17,1},{2,18},{3,19},{18,2},{19,3},{4,20},{5,... | collective-permute-start | bytes 1179656 | tf_op jit(solution)/shard_map/ppermute | solution.py:201
  12.3 17.2 %collective-permute-start.9 = (bf16[4,128,384]{2,1,0:T(8,128)(2,1)S(1)}, bf16[4,128,384]{2,1,0:T(8,128)(2,1)S(1)}, u32[]{:S(2)}, u32[]{:S(2)}) collective-permute-start(bf16[4,128,384]{2,1,0:T(8,128)(2,1)S(1)} %get-tuple-element.34), channel_id=1, source_target_pairs={{0,17},{1,16},{16,1},{17,0},{2,19},{3,18},{18,3},{19,2},{4,21},{5,... | collective-permute-start | bytes 1179656 | tf_op jit(solution)/shard_map/ppermute | solution.py:201
  12.8 34.2 %collective-permute-start.3 = (bf16[128,1536]{1,0:T(8,128)(2,1)S(1)}, bf16[128,1536]{1,0:T(8,128)(2,1)S(1)}, u32[]{:S(2)}, u32[]{:S(2)}) collective-permute-start(bf16[128,1536]{1,0:T(8,128)(2,1)S(1)} %get-tuple-element.26), channel_id=1, source_target_pairs={{0,4},{2,6},{4,0},{6,2},{1,5},{3,7},{5,1},{7,3},{8,12},{10,14},{12... | collective-permute-start | bytes 1179656 | tf_op jit(solution)/shard_map/ppermute | solution.py:196
  17.8 29.3 %collective-permute-start.2 = (bf16[128,1536]{1,0:T(8,128)(2,1)S(1)}, bf16[128,1536]{1,0:T(8,128)(2,1)S(1)}, u32[]{:S(2)}, u32[]{:S(2)}) collective-permute-start(bf16[128,1536]{1,0:T(8,128)(2,1)S(1)} %rearrange.8), channel_id=1, source_target_pairs={{0,2},{2,0},{4,6},{6,4},{1,3},{3,1},{5,7},{7,5},{8,10},{10,8},{12,... | collective-permute-start | bytes 1179656 | tf_op jit(solution)/shard_map/ppermute | solution.py:196
  29.6 41.7 %copy-start.4 = (bf16[128,6144]{1,0:T(8,128)(2,1)S(1)}, bf16[128,6144]{1,0:T(8,128)(2,1)}, u32[]{:S(2)}) copy-start(bf16[128,6144]{1,0:T(8,128)(2,1)} %refs_9_.1) | copy-start | bytes 4718596
  30.2 29.2 %collective-permute-start.10 = (bf16[4,128,384]{2,1,0:T(8,128)(2,1)S(1)}, bf16[4,128,384]{2,1,0:T(8,128)(2,1)S(1)}, u32[]{:S(2)}, u32[]{:S(2)}) collective-permute-start(bf16[4,128,384]{2,1,0:T(8,128)(2,1)S(1)} %get-tuple-element.36), channel_id=1, source_target_pairs={{0,2},{2,0},{4,6},{6,4},{1,3},{3,1},{5,7},{7,5},{8,10},{10,8},{12,... | collective-permute-start | bytes 1179656 | tf_op jit(solution)/shard_map/ppermute | solution.py:196
  38.0 32.4 %collective-permute-start.11 = (bf16[4,128,384]{2,1,0:T(8,128)(2,1)S(1)}, bf16[4,128,384]{2,1,0:T(8,128)(2,1)S(1)}, u32[]{:S(2)}, u32[]{:S(2)}) collective-permute-start(bf16[4,128,384]{2,1,0:T(8,128)(2,1)S(1)} %get-tuple-element.37), channel_id=1, source_target_pairs={{0,4},{2,6},{4,0},{6,2},{1,5},{3,7},{5,1},{7,3},{8,12},{10,14},{12... | collective-permute-start | bytes 1179656 | tf_op jit(solution)/shard_map/ppermute | solution.py:196
  39.6 30.9 %collective-permute-start.12 = (bf16[4,128,384]{2,1,0:T(8,128)(2,1)S(1)}, bf16[4,128,384]{2,1,0:T(8,128)(2,1)S(1)}, u32[]{:S(2)}, u32[]{:S(2)}) collective-permute-start(bf16[4,128,384]{2,1,0:T(8,128)(2,1)S(1)} %get-tuple-element.38), channel_id=1, source_target_pairs={{0,6},{2,4},{4,2},{6,0},{1,7},{3,5},{5,3},{7,1},{8,14},{10,12},{12... | collective-permute-start | bytes 1179656 | tf_op jit(solution)/shard_map/ppermute | solution.py:196
  47.7 22.7 %collective-permute-start.5 = (bf16[4,128,384]{2,1,0:T(8,128)(2,1)S(1)}, bf16[4,128,384]{2,1,0:T(8,128)(2,1)S(1)}, u32[]{:S(2)}, u32[]{:S(2)}) collective-permute-start(bf16[4,128,384]{2,1,0:T(8,128)(2,1)S(1)} %get-tuple-element.29), channel_id=1, source_target_pairs={{0,1},{1,0},{16,17},{17,16},{2,3},{3,2},{18,19},{19,18},{4,5},{5,4... | collective-permute-start | bytes 1179656 | tf_op jit(solution)/shard_map/ppermute | solution.py:201
  48.3 22.1 %collective-permute-start.6 = (bf16[4,128,384]{2,1,0:T(8,128)(2,1)S(1)}, bf16[4,128,384]{2,1,0:T(8,128)(2,1)S(1)}, u32[]{:S(2)}, u32[]{:S(2)}) collective-permute-start(bf16[4,128,384]{2,1,0:T(8,128)(2,1)S(1)} %get-tuple-element.30), channel_id=1, source_target_pairs={{0,16},{1,17},{16,0},{17,1},{2,18},{3,19},{18,2},{19,3},{4,20},{5,... | collective-permute-start | bytes 1179656 | tf_op jit(solution)/shard_map/ppermute | solution.py:201
  59.4 11.8 %collective-permute-start.7 = (bf16[4,128,384]{2,1,0:T(8,128)(2,1)S(1)}, bf16[4,128,384]{2,1,0:T(8,128)(2,1)S(1)}, u32[]{:S(2)}, u32[]{:S(2)}) collective-permute-start(bf16[4,128,384]{2,1,0:T(8,128)(2,1)S(1)} %get-tuple-element.31), channel_id=1, source_target_pairs={{0,17},{1,16},{16,1},{17,0},{2,19},{3,18},{18,3},{19,2},{4,21},{5,... | collective-permute-start | bytes 1179656 | tf_op jit(solution)/shard_map/ppermute | solution.py:201
  72.2 0.9 copy-start.6
  73.1 0.9 copy-start.7
  74.0 34.3 %copy-start.8 = (s32[1,16,2]{1,2,0:T(2,128)S(1)}, s32[1,16,2]{1,2,0:T(2,128)}, u32[]{:S(2)}) copy-start(s32[1,16,2]{1,2,0:T(2,128)} %param.8) | copy-start | bytes 388
  74.0 34.3 %copy-start.9 = (s32[1,16]{1,0:T(1,128)S(1)}, s32[1,16]{1,0:T(1,128)}, u32[]{:S(2)}) copy-start(s32[1,16]{1,0:T(1,128)} %param.9) | copy-start | bytes 196
  74.0 29.4 %all-to-all-start = ((bf16[16,64,384]{2,1,0:T(8,128)(2,1)}), bf16[16,64,384]{2,1,0:T(8,128)(2,1)}, u32[]{:S(2)}, u32[]{:S(2)}) async-start(bf16[16,64,384]{2,1,0:T(8,128)(2,1)} %copy-done.7), calls=%async_computation | async-start | bytes 1572864 | tf_op jit(solution)/shard_map/all_to_all | solution.py:205
  84.7 28.6 %collective-permute-start.13 = (bf16[4,4,128,384]{3,2,1,0:T(8,128)(2,1)S(1)}, bf16[4,4,128,384]{3,2,1,0:T(8,128)(2,1)}, u32[]{:S(2)}, u32[]{:S(2)}) collective-permute-start(bf16[4,4,128,384]{3,2,1,0:T(8,128)(2,1)S(1)} %get-tuple-element.39.k_own), channel_id=1, source_target_pairs={{0,8},{8,0},{1,9},{9,1},{2,10},{10,2},{3,11},{11,3},{4,12},{12,4},... | collective-permute-start | bytes 4718600 | tf_op jit(solution)/shard_map/ppermute | solution.py:210
  84.8 28.5 %collective-permute-start.14 = (bf16[4,4,128,384]{3,2,1,0:T(8,128)(2,1)S(1)}, bf16[4,4,128,384]{3,2,1,0:T(8,128)(2,1)}, u32[]{:S(2)}, u32[]{:S(2)}) collective-permute-start(bf16[4,4,128,384]{3,2,1,0:T(8,128)(2,1)S(1)} %get-tuple-element.40.v_own), channel_id=1, source_target_pairs={{0,8},{8,0},{1,9},{9,1},{2,10},{10,2},{3,11},{11,3},{4,12},{12,4},... | collective-permute-start | bytes 4718600 | tf_op jit(solution)/shard_map/ppermute | solution.py:210
  103.3 23.6 %all-to-all-start.2 = ((bf16[16,64,384]{2,1,0:T(8,128)(2,1)}), bf16[16,64,384]{2,1,0:T(8,128)(2,1)}, u32[]{:S(2)}, u32[]{:S(2)}) async-start(bf16[16,64,384]{2,1,0:T(8,128)(2,1)} %copy-done.6), calls=%async_computation.2 | async-start | bytes 1572864 | tf_op jit(solution)/shard_map/all_to_all | solution.py:205
  108.3 4.2 %collective-permute-start = (s32[16,3]{0,1:T(4,128)S(1)}, s32[16,3]{0,1:T(4,128)S(1)}, u32[]{:S(2)}, u32[]{:S(2)}) collective-permute-start(s32[16,3]{0,1:T(4,128)S(1)} %get-tuple-element.44), channel_id=1, source_target_pairs={{0,16},{16,0},{1,17},{17,1},{2,18},{18,2},{3,19},{19,3},{4,20},{20... | collective-permute-start | bytes 584 | tf_op jit(solution)/shard_map/ppermute | solution.py:216
  120.2 0.9 copy-start.2
  126.9 23.6 %all-to-all-start.1 = ((bf16[16,64,384]{2,1,0:T(8,128)(2,1)}), bf16[16,64,384]{2,1,0:T(8,128)(2,1)}, u32[]{:S(2)}, u32[]{:S(2)}) async-start(bf16[16,64,384]{2,1,0:T(8,128)(2,1)} %copy-done.2), calls=%async_computation.1 | async-start | bytes 1572864 | tf_op jit(solution)/shard_map/all_to_all | solution.py:205
  138.8 0.9 copy-start.3
  150.5 23.5 %all-to-all-start.3 = ((bf16[16,64,384]{2,1,0:T(8,128)(2,1)}), bf16[16,64,384]{2,1,0:T(8,128)(2,1)S(1)}, u32[]{:S(2)}, u32[]{:S(2)}) async-start(bf16[16,64,384]{2,1,0:T(8,128)(2,1)} %copy-done.3), calls=%async_computation.3 | async-start | bytes 1572864 | tf_op jit(solution)/shard_map/all_to_all | solution.py:205

commit v7 on v6

--- a/solution.py
+++ b/solution.py
@@ -62,13 +62,12 @@
             out[k] = source[:, pl.ds(start, width)]
 
 
-def far_of_near(start, me, *refs):
+def far_of_near(blocks, me, *refs):
     near = refs[-1].shape[0]
     sources, outs = refs[:near], refs[near:]
-    rows = outs[0].shape[1]
-    for k, out in enumerate(outs):
+    for k, out in zip(blocks, outs):
         for e, source in enumerate(sources):
-            out[me[1] ^ e] = source[k, pl.ds(start, rows), :]
+            out[me[1] ^ e] = source[k]
 
 
 def all_columns(me, source, *outs):
@@ -230,8 +229,12 @@
     values = around(rearrange(near_columns, me, [value_rows], [near_block] * near, keys[:1]))
     keys[1:1] = rearrange(functools.partial(far_columns, order[-1:]), me, [key_rows], [shape], values[1:2])
     keys = across(keys)
-    values = across(rearrange(functools.partial(far_of_near, 0), me, values, [far_block] * high, [keys[-1]]))
-    keys = around(rearrange(near_of_far, me, keys, [near_block] * near))
+    crossing = functools.partial(far_of_near, order[:-1])
+    v_far = list(rearrange(crossing, me, values, [far_block] * (high - 1), [keys[-1]]))
+    keys = rearrange(near_of_far, me, keys, [near_block] * near)
+    v_far[1:1] = rearrange(functools.partial(far_of_near, order[-1:]), me, values, [far_block], keys[:1])
+    values = across(v_far)
+    keys = around(keys)
     shapes = [full, full] + [(high * near, TILE, width)] * per_device
     gather = functools.partial(gather_all, high, near)
     keys, values, *q_parts = rearrange(gather, me, [*keys, *values, queries], shapes)

time: 176 us -> 177 us (level)
  starting transfers between devices: 53.1 us -> 45.2 us
  waiting for transfers between devices: 94.2 us -> 102 us
    ppermute x6, waiting for transfers between devices: 13.6 us -> 23.5 us  [around(): lax.ppermute(blocks[e], near_axes, [(i, i ^ e) for i in range(near)])]
    all_to_all x4, starting transfers between devices: 25.5 us -> 18.1 us  [exchange(): lax.all_to_all(x, ('far',) + near_axes, split_axis=0, concat_axis=0, tile...]
    all_to_all x4, waiting for transfers between devices: 52.1 us -> 50.2 us  [exchange(): lax.all_to_all(x, ('far',) + near_axes, split_axis=0, concat_axis=0, tile...]
    pallas_call x6 -> x7, Pallas kernels: 4.2 us -> 4.74 us  [rearrange(): pl.pallas_call(held, in_specs=[SMEM] + [VMEM] * len(sources) + [ANY] * co...]
  transfers between devices with their start and end apart: 19 -> 19, of which waited for: 12 -> 13; matrix products, arithmetic and copies ran while one was open for 1% -> 1% of each run, Pallas kernels for 9% -> 9%
where the time goes in v7:
time: 177 us; the launch traced here: 176 us
  waiting for transfers between devices  102 us (58%)
  starting transfers between devices  45.2 us (26%)
  Pallas kernels  18.8 us (11%)
  local copies, waits for them, and re-layouts  8.4 us (5%)
    all_to_all x4, waiting for transfers between devices, exchange(): lax.all_to_all(x, ('far',) + near_axes, split_axis=0, concat_axis=0, tile...  50.2 us
    ppermute x6, waiting for transfers between devices, across(): lax.ppermute(blocks[k], 'far', [(i, i ^ k) for i in range(high)])  26.4 us
    ppermute x6, waiting for transfers between devices, around(): lax.ppermute(blocks[e], near_axes, [(i, i ^ e) for i in range(near)])  23.5 us
    all_to_all x4, starting transfers between devices, exchange(): lax.all_to_all(x, ('far',) + near_axes, split_axis=0, concat_axis=0, tile...  18.1 us
    ppermute x6, starting transfers between devices, across(): lax.ppermute(blocks[k], 'far', [(i, i ^ k) for i in range(high)])  16 us
    pallas_call x2, Pallas kernels, attend(): pl.pallas_call(functools.partial(attend_kernel, (high, low, part)), in_sp...  14 us
    ppermute x6, starting transfers between devices, around(): lax.ppermute(blocks[e], near_axes, [(i, i ^ e) for i in range(near)])  8.55 us
    unnamed x20, local copies, waits for them, and re-layouts  6.37 us
  transfers between devices with their start and end apart: 19, of which 13 were waited for; matrix products, arithmetic and copies ran while one was open for 1% of the time, Pallas kernels for 9%

profile of v7, /device:TPU:0, one launch (start us, length us, event | category | flops | bytes accessed | tf_op | source)
XLA Modules:
  0.0 176.3 jit_solution(8457156286341506193)
XLA Ops:
  0.1 1.4 copy-done
  2.1 1.4 copy-done.5
  4.2 3.0 %collective-permute-start.1 = (bf16[4,128,384]{2,1,0:T(8,128)(2,1)S(1)}, bf16[4,128,384]{2,1,0:T(8,128)(2,1)S(1)}, u32[]{:S(2)}, u32[]{:S(2)}) collective-permute-start(bf16[4,128,384]{2,1,0:T(8,128)(2,1)S(1)} %get-tuple-element.24), channel_id=1, source_target_pairs={{0,1},{1,0},{16,17},{17,16},{2,3},{3,2},{18,19},{19,18},{4,5},{5,4... | collective-permute-start | bytes 1179656 | tf_op jit(solution)/shard_map/ppermute | solution.py:200
  7.2 3.6 %collective-permute-start.4 = (bf16[128,1536]{1,0:T(8,128)(2,1)S(1)}, bf16[128,1536]{1,0:T(8,128)(2,1)S(1)}, u32[]{:S(2)}, u32[]{:S(2)}) collective-permute-start(bf16[128,1536]{1,0:T(8,128)(2,1)S(1)} %get-tuple-element.26), channel_id=1, source_target_pairs={{0,6},{2,4},{4,2},{6,0},{1,7},{3,5},{5,3},{7,1},{8,14},{10,12},{12... | collective-permute-start | bytes 1179656 | tf_op jit(solution)/shard_map/ppermute | solution.py:195
  10.8 1.5 collective-permute-start.8
  12.8 4.3 %collective-permute-done.1.refs_2_ = bf16[4,128,384]{2,1,0:T(8,128)(2,1)S(1)} collective-permute-done((bf16[4,128,384]{2,1,0:T(8,128)(2,1)S(1)}, bf16[4,128,384]{2,1,0:T(8,128)(2,1)S(1)}, u32[]{:S(2)}, u32[]{:S(2)}) %collective-permute-start.1) | collective-permute-done | bytes 393248 | tf_op jit(solution)/shard_map/ppermute | solution.py:200
  17.8 2.2 %collective-permute-start.2 = (bf16[128,1536]{1,0:T(8,128)(2,1)S(1)}, bf16[128,1536]{1,0:T(8,128)(2,1)S(1)}, u32[]{:S(2)}, u32[]{:S(2)}) collective-permute-start(bf16[128,1536]{1,0:T(8,128)(2,1)S(1)} %rearrange.9), channel_id=1, source_target_pairs={{0,2},{2,0},{4,6},{6,4},{1,3},{3,1},{5,7},{7,5},{8,10},{10,8},{12,... | collective-permute-start | bytes 1179656 | tf_op jit(solution)/shard_map/ppermute | solution.py:195
  20.0 1.2 collective-permute-done.4.refs_4_.refs_5_
  21.1 8.4 %collective-permute-done.8.refs_3_ = bf16[4,128,384]{2,1,0:T(8,128)(2,1)S(1)} collective-permute-done((bf16[4,128,384]{2,1,0:T(8,128)(2,1)S(1)}, bf16[4,128,384]{2,1,0:T(8,128)(2,1)S(1)}, u32[]{:S(2)}, u32[]{:S(2)}) %collective-permute-start.8) | collective-permute-done | bytes 393248 | tf_op jit(solution)/shard_map/ppermute | solution.py:200
  30.2 9.2 %collective-permute-start.11 = (bf16[4,128,384]{2,1,0:T(8,128)(2,1)S(1)}, bf16[4,128,384]{2,1,0:T(8,128)(2,1)S(1)}, u32[]{:S(2)}, u32[]{:S(2)}) collective-permute-start(bf16[4,128,384]{2,1,0:T(8,128)(2,1)S(1)} %get-tuple-element.35), channel_id=1, source_target_pairs={{0,4},{2,6},{4,0},{6,2},{1,5},{3,7},{5,1},{7,3},{8,12},{10,14},{12... | collective-permute-start | bytes 1179656 | tf_op jit(solution)/shard_map/ppermute | solution.py:195
  40.3 21.6 %collective-permute-done.3.refs_3_ = bf16[128,1536]{1,0:T(8,128)(2,1)S(1)} collective-permute-done((bf16[128,1536]{1,0:T(8,128)(2,1)S(1)}, bf16[128,1536]{1,0:T(8,128)(2,1)S(1)}, u32[]{:S(2)}, u32[]{:S(2)}) %collective-permute-start.3) | collective-permute-done | bytes 393248 | tf_op jit(solution)/shard_map/ppermute | solution.py:195
  63.3 1.5 collective-permute-start.6
  64.8 1.4 collective-permute-start.7
  66.8 3.6 %collective-permute-done.11.refs_7_ = bf16[4,128,384]{2,1,0:T(8,128)(2,1)S(1)} collective-permute-done((bf16[4,128,384]{2,1,0:T(8,128)(2,1)S(1)}, bf16[4,128,384]{2,1,0:T(8,128)(2,1)S(1)}, u32[]{:S(2)}, u32[]{:S(2)}) %collective-permute-start.11) | collective-permute-done | bytes 393248 | tf_op jit(solution)/shard_map/ppermute | solution.py:195
  70.5 4.3 %collective-permute-done.5.refs_2_ = bf16[4,128,384]{2,1,0:T(8,128)(2,1)S(1)} collective-permute-done((bf16[4,128,384]{2,1,0:T(8,128)(2,1)S(1)}, bf16[4,128,384]{2,1,0:T(8,128)(2,1)S(1)}, u32[]{:S(2)}, u32[]{:S(2)}) %collective-permute-start.5) | collective-permute-done | bytes 393248 | tf_op jit(solution)/shard_map/ppermute | solution.py:200
  74.8 4.8 %collective-permute-done.6.refs_3_ = bf16[4,128,384]{2,1,0:T(8,128)(2,1)S(1)} collective-permute-done((bf16[4,128,384]{2,1,0:T(8,128)(2,1)S(1)}, bf16[4,128,384]{2,1,0:T(8,128)(2,1)S(1)}, u32[]{:S(2)}, u32[]{:S(2)}) %collective-permute-start.6) | collective-permute-done | bytes 393248 | tf_op jit(solution)/shard_map/ppermute | solution.py:200
  79.6 1.6 collective-permute-done.7.refs_4_
  81.2 1.0 rearrange.13
  84.0 4.8 %all-to-all-start = ((bf16[16,64,384]{2,1,0:T(8,128)(2,1)}), bf16[16,64,384]{2,1,0:T(8,128)(2,1)}, u32[]{:S(2)}, u32[]{:S(2)}) async-start(bf16[16,64,384]{2,1,0:T(8,128)(2,1)} %copy-done.7), calls=%async_computation | async-start | bytes 1572864 | tf_op jit(solution)/shard_map/all_to_all | solution.py:204
  89.3 17.0 %all-to-all-done.q = bf16[16,64,384]{2,1,0:T(8,128)(2,1)} async-done(((bf16[16,64,384]{2,1,0:T(8,128)(2,1)}), bf16[16,64,384]{2,1,0:T(8,128)(2,1)}, u32[]{:S(2)}, u32[]{:S(2)}) %all-to-all-start) | async-done | bytes 786464 | tf_op jit(solution)/shard_map/all_to_all | solution.py:204
  106.3 4.4 %all-to-all-start.2 = ((bf16[16,64,384]{2,1,0:T(8,128)(2,1)}), bf16[16,64,384]{2,1,0:T(8,128)(2,1)}, u32[]{:S(2)}, u32[]{:S(2)}) async-start(bf16[16,64,384]{2,1,0:T(8,128)(2,1)} %copy-done.6), calls=%async_computation.2 | async-start | bytes 1572864 | tf_op jit(solution)/shard_map/all_to_all | solution.py:204
  110.7 1.9 %collective-permute-start = (s32[16,3]{0,1:T(4,128)S(1)}, s32[16,3]{0,1:T(4,128)S(1)}, u32[]{:S(2)}, u32[]{:S(2)}) collective-permute-start(s32[16,3]{0,1:T(4,128)S(1)} %get-tuple-element.42), channel_id=1, source_target_pairs={{0,16},{16,0},{1,17},{17,1},{2,18},{18,2},{3,19},{19,3},{4,20},{20... | collective-permute-start | bytes 584 | tf_op jit(solution)/shard_map/ppermute | solution.py:215
  112.7 2.3 %collective-permute-done = s32[16,3]{0,1:T(4,128)S(1)} collective-permute-done((s32[16,3]{0,1:T(4,128)S(1)}, s32[16,3]{0,1:T(4,128)S(1)}, u32[]{:S(2)}, u32[]{:S(2)}) %collective-permute-start) | collective-permute-done | bytes 224 | tf_op jit(solution)/shard_map/ppermute | solution.py:215
  115.7 6.9 %attend.2 = bf16[16,64,384]{2,1,0:T(8,128)(2,1)S(1)} custom-call(s32[2]{0:T(128)S(1)} %pad_add_fusion.3.refs_0_.me, s32[4,32]{1,0:T(4,128)S(1)} %bitcast.18, bf16[4,4,128,384]{3,2,1,0:T(8,128)(2,1)S(1)} %get-tuple-element.37.k_own, bf16[4,4,128,384]{3,2,1,0:T(8,128)(2,1)} %collective-permute-done.13.k_swap, ...), custom_call_target="tpu_custom_call" | custom-call | flops 402653184 | bytes 7864320 | tf_op jit(solution)/shard_map/attend/pallas_call | solution.py:166
  123.6 5.3 %all-to-all-done.2.q = bf16[16,64,384]{2,1,0:T(8,128)(2,1)} async-done(((bf16[16,64,384]{2,1,0:T(8,128)(2,1)}), bf16[16,64,384]{2,1,0:T(8,128)(2,1)}, u32[]{:S(2)}, u32[]{:S(2)}) %all-to-all-start.2) | async-done | bytes 786464 | tf_op jit(solution)/shard_map/all_to_all | solution.py:204
  128.8 4.4 %all-to-all-start.1 = ((bf16[16,64,384]{2,1,0:T(8,128)(2,1)}), bf16[16,64,384]{2,1,0:T(8,128)(2,1)}, u32[]{:S(2)}, u32[]{:S(2)}) async-start(bf16[16,64,384]{2,1,0:T(8,128)(2,1)} %copy-done.2), calls=%async_computation.1 | async-start | bytes 1572864 | tf_op jit(solution)/shard_map/all_to_all | solution.py:204
  133.2 7.1 %attend.3 = bf16[16,64,384]{2,1,0:T(8,128)(2,1)S(1)} custom-call(s32[2]{0:T(128)S(1)} %pad_add_fusion.3.refs_0_.me, s32[4,32]{1,0:T(4,128)S(1)} %bitcast.19, bf16[4,4,128,384]{3,2,1,0:T(8,128)(2,1)S(1)} %get-tuple-element.37.k_own, bf16[4,4,128,384]{3,2,1,0:T(8,128)(2,1)} %collective-permute-done.13.k_swap, ...), custom_call_target="tpu_custom_call" | custom-call | flops 402653184 | bytes 7864320 | tf_op jit(solution)/shard_map/attend/pallas_call | solution.py:166
  141.2 10.6 %all-to-all-done.1 = bf16[16,64,384]{2,1,0:T(8,128)(2,1)} async-done(((bf16[16,64,384]{2,1,0:T(8,128)(2,1)}), bf16[16,64,384]{2,1,0:T(8,128)(2,1)}, u32[]{:S(2)}, u32[]{:S(2)}) %all-to-all-start.1) | async-done | bytes 786464 | tf_op jit(solution)/shard_map/all_to_all | solution.py:204
  151.8 4.5 %all-to-all-start.3 = ((bf16[16,64,384]{2,1,0:T(8,128)(2,1)}), bf16[16,64,384]{2,1,0:T(8,128)(2,1)S(1)}, u32[]{:S(2)}, u32[]{:S(2)}) async-start(bf16[16,64,384]{2,1,0:T(8,128)(2,1)} %copy-done.3), calls=%async_computation.3 | async-start | bytes 1572864 | tf_op jit(solution)/shard_map/all_to_all | solution.py:204
  156.4 1.2 copy.10
  157.6 17.4 %all-to-all-done.3 = bf16[16,64,384]{2,1,0:T(8,128)(2,1)S(1)} async-done(((bf16[16,64,384]{2,1,0:T(8,128)(2,1)}), bf16[16,64,384]{2,1,0:T(8,128)(2,1)S(1)}, u32[]{:S(2)}, u32[]{:S(2)}) %all-to-all-start.3) | async-done | bytes 786464 | tf_op jit(solution)/shard_map/all_to_all | solution.py:204
  175.1 1.3 pad_maximum_fusion
  (49 shorter events, 11.0 us)
Async XLA Ops:
  0.1 1.4 copy-start
  1.5 15.7 %copy-start.1 = (bf16[128,6144]{1,0:T(8,128)(2,1)S(1)}, bf16[128,6144]{1,0:T(8,128)(2,1)}, u32[]{:S(2)}) copy-start(bf16[128,6144]{1,0:T(8,128)(2,1)} %refs_1_.5) | copy-start | bytes 4718596
  2.1 1.4 copy-start.5
  4.2 12.9 %collective-permute-start.1 = (bf16[4,128,384]{2,1,0:T(8,128)(2,1)S(1)}, bf16[4,128,384]{2,1,0:T(8,128)(2,1)S(1)}, u32[]{:S(2)}, u32[]{:S(2)}) collective-permute-start(bf16[4,128,384]{2,1,0:T(8,128)(2,1)S(1)} %get-tuple-element.24), channel_id=1, source_target_pairs={{0,1},{1,0},{16,17},{17,16},{2,3},{3,2},{18,19},{19,18},{4,5},{5,4... | collective-permute-start | bytes 1179656 | tf_op jit(solution)/shard_map/ppermute | solution.py:200
  7.2 13.9 %collective-permute-start.4 = (bf16[128,1536]{1,0:T(8,128)(2,1)S(1)}, bf16[128,1536]{1,0:T(8,128)(2,1)S(1)}, u32[]{:S(2)}, u32[]{:S(2)}) collective-permute-start(bf16[128,1536]{1,0:T(8,128)(2,1)S(1)} %get-tuple-element.26), channel_id=1, source_target_pairs={{0,6},{2,4},{4,2},{6,0},{1,7},{3,5},{5,3},{7,1},{8,14},{10,12},{12... | collective-permute-start | bytes 1179656 | tf_op jit(solution)/shard_map/ppermute | solution.py:195
  10.8 18.7 %collective-permute-start.8 = (bf16[4,128,384]{2,1,0:T(8,128)(2,1)S(1)}, bf16[4,128,384]{2,1,0:T(8,128)(2,1)S(1)}, u32[]{:S(2)}, u32[]{:S(2)}) collective-permute-start(bf16[4,128,384]{2,1,0:T(8,128)(2,1)S(1)} %get-tuple-element.32), channel_id=1, source_target_pairs={{0,16},{1,17},{16,0},{17,1},{2,18},{3,19},{18,2},{19,3},{4,20},{5,... | collective-permute-start | bytes 1179656 | tf_op jit(solution)/shard_map/ppermute | solution.py:200
  12.3 17.2 %collective-permute-start.9 = (bf16[4,128,384]{2,1,0:T(8,128)(2,1)S(1)}, bf16[4,128,384]{2,1,0:T(8,128)(2,1)S(1)}, u32[]{:S(2)}, u32[]{:S(2)}) collective-permute-start(bf16[4,128,384]{2,1,0:T(8,128)(2,1)S(1)} %get-tuple-element.33), channel_id=1, source_target_pairs={{0,17},{1,16},{16,1},{17,0},{2,19},{3,18},{18,3},{19,2},{4,21},{5,... | collective-permute-start | bytes 1179656 | tf_op jit(solution)/shard_map/ppermute | solution.py:200
  12.8 49.1 %collective-permute-start.3 = (bf16[128,1536]{1,0:T(8,128)(2,1)S(1)}, bf16[128,1536]{1,0:T(8,128)(2,1)S(1)}, u32[]{:S(2)}, u32[]{:S(2)}) collective-permute-start(bf16[128,1536]{1,0:T(8,128)(2,1)S(1)} %get-tuple-element.25), channel_id=1, source_target_pairs={{0,4},{2,6},{4,0},{6,2},{1,5},{3,7},{5,1},{7,3},{8,12},{10,14},{12... | collective-permute-start | bytes 1179656 | tf_op jit(solution)/shard_map/ppermute | solution.py:195
  17.8 44.2 %collective-permute-start.2 = (bf16[128,1536]{1,0:T(8,128)(2,1)S(1)}, bf16[128,1536]{1,0:T(8,128)(2,1)S(1)}, u32[]{:S(2)}, u32[]{:S(2)}) collective-permute-start(bf16[128,1536]{1,0:T(8,128)(2,1)S(1)} %rearrange.9), channel_id=1, source_target_pairs={{0,2},{2,0},{4,6},{6,4},{1,3},{3,1},{5,7},{7,5},{8,10},{10,8},{12,... | collective-permute-start | bytes 1179656 | tf_op jit(solution)/shard_map/ppermute | solution.py:195
  30.2 40.2 %collective-permute-start.11 = (bf16[4,128,384]{2,1,0:T(8,128)(2,1)S(1)}, bf16[4,128,384]{2,1,0:T(8,128)(2,1)S(1)}, u32[]{:S(2)}, u32[]{:S(2)}) collective-permute-start(bf16[4,128,384]{2,1,0:T(8,128)(2,1)S(1)} %get-tuple-element.35), channel_id=1, source_target_pairs={{0,4},{2,6},{4,0},{6,2},{1,5},{3,7},{5,1},{7,3},{8,12},{10,14},{12... | collective-permute-start | bytes 1179656 | tf_op jit(solution)/shard_map/ppermute | solution.py:195
  39.4 31.1 %collective-permute-start.12 = (bf16[4,128,384]{2,1,0:T(8,128)(2,1)S(1)}, bf16[4,128,384]{2,1,0:T(8,128)(2,1)S(1)}, u32[]{:S(2)}, u32[]{:S(2)}) collective-permute-start(bf16[4,128,384]{2,1,0:T(8,128)(2,1)S(1)} %get-tuple-element.36), channel_id=1, source_target_pairs={{0,6},{2,4},{4,2},{6,0},{1,7},{3,5},{5,3},{7,1},{8,14},{10,12},{12... | collective-permute-start | bytes 1179656 | tf_op jit(solution)/shard_map/ppermute | solution.py:195
  62.6 18.6 %copy-start.4 = (bf16[128,6144]{1,0:T(8,128)(2,1)S(1)}, bf16[128,6144]{1,0:T(8,128)(2,1)}, u32[]{:S(2)}) copy-start(bf16[128,6144]{1,0:T(8,128)(2,1)} %refs_9_.1) | copy-start | bytes 4718596
  62.7 12.1 %collective-permute-start.5 = (bf16[4,128,384]{2,1,0:T(8,128)(2,1)S(1)}, bf16[4,128,384]{2,1,0:T(8,128)(2,1)S(1)}, u32[]{:S(2)}, u32[]{:S(2)}) collective-permute-start(bf16[4,128,384]{2,1,0:T(8,128)(2,1)S(1)} %get-tuple-element.28), channel_id=1, source_target_pairs={{0,1},{1,0},{16,17},{17,16},{2,3},{3,2},{18,19},{19,18},{4,5},{5,4... | collective-permute-start | bytes 1179656 | tf_op jit(solution)/shard_map/ppermute | solution.py:200
  63.3 16.4 %collective-permute-start.6 = (bf16[4,128,384]{2,1,0:T(8,128)(2,1)S(1)}, bf16[4,128,384]{2,1,0:T(8,128)(2,1)S(1)}, u32[]{:S(2)}, u32[]{:S(2)}) collective-permute-start(bf16[4,128,384]{2,1,0:T(8,128)(2,1)S(1)} %get-tuple-element.29), channel_id=1, source_target_pairs={{0,16},{1,17},{16,0},{17,1},{2,18},{3,19},{18,2},{19,3},{4,20},{5,... | collective-permute-start | bytes 1179656 | tf_op jit(solution)/shard_map/ppermute | solution.py:200
  64.8 16.5 %collective-permute-start.7 = (bf16[4,128,384]{2,1,0:T(8,128)(2,1)S(1)}, bf16[4,128,384]{2,1,0:T(8,128)(2,1)S(1)}, u32[]{:S(2)}, u32[]{:S(2)}) collective-permute-start(bf16[4,128,384]{2,1,0:T(8,128)(2,1)S(1)} %get-tuple-element.30), channel_id=1, source_target_pairs={{0,17},{1,16},{16,1},{17,0},{2,19},{3,18},{18,3},{19,2},{4,21},{5,... | collective-permute-start | bytes 1179656 | tf_op jit(solution)/shard_map/ppermute | solution.py:200
  70.4 10.9 %collective-permute-start.10 = (bf16[4,128,384]{2,1,0:T(8,128)(2,1)S(1)}, bf16[4,128,384]{2,1,0:T(8,128)(2,1)S(1)}, u32[]{:S(2)}, u32[]{:S(2)}) collective-permute-start(bf16[4,128,384]{2,1,0:T(8,128)(2,1)S(1)} %rearrange.12), channel_id=1, source_target_pairs={{0,2},{2,0},{4,6},{6,4},{1,3},{3,1},{5,7},{7,5},{8,10},{10,8},{12,... | collective-permute-start | bytes 1179656 | tf_op jit(solution)/shard_map/ppermute | solution.py:195
  82.2 0.9 copy-start.6
  83.1 0.9 copy-start.7
  84.0 26.7 %copy-start.8 = (s32[1,16,2]{1,2,0:T(2,128)S(1)}, s32[1,16,2]{1,2,0:T(2,128)}, u32[]{:S(2)}) copy-start(s32[1,16,2]{1,2,0:T(2,128)} %param.8) | copy-start | bytes 388
  84.0 26.7 %copy-start.9 = (s32[1,16]{1,0:T(1,128)S(1)}, s32[1,16]{1,0:T(1,128)}, u32[]{:S(2)}) copy-start(s32[1,16]{1,0:T(1,128)} %param.9) | copy-start | bytes 196
  84.0 22.3 %all-to-all-start = ((bf16[16,64,384]{2,1,0:T(8,128)(2,1)}), bf16[16,64,384]{2,1,0:T(8,128)(2,1)}, u32[]{:S(2)}, u32[]{:S(2)}) async-start(bf16[16,64,384]{2,1,0:T(8,128)(2,1)} %copy-done.7), calls=%async_computation | async-start | bytes 1572864 | tf_op jit(solution)/shard_map/all_to_all | solution.py:204
  88.7 27.0 %collective-permute-start.13 = (bf16[4,4,128,384]{3,2,1,0:T(8,128)(2,1)S(1)}, bf16[4,4,128,384]{3,2,1,0:T(8,128)(2,1)}, u32[]{:S(2)}, u32[]{:S(2)}) collective-permute-start(bf16[4,4,128,384]{3,2,1,0:T(8,128)(2,1)S(1)} %get-tuple-element.37.k_own), channel_id=1, source_target_pairs={{0,8},{8,0},{1,9},{9,1},{2,10},{10,2},{3,11},{11,3},{4,12},{12,4},... | collective-permute-start | bytes 4718600 | tf_op jit(solution)/shard_map/ppermute | solution.py:209
  88.8 26.9 %collective-permute-start.14 = (bf16[4,4,128,384]{3,2,1,0:T(8,128)(2,1)S(1)}, bf16[4,4,128,384]{3,2,1,0:T(8,128)(2,1)}, u32[]{:S(2)}, u32[]{:S(2)}) collective-permute-start(bf16[4,4,128,384]{3,2,1,0:T(8,128)(2,1)S(1)} %get-tuple-element.38.v_own), channel_id=1, source_target_pairs={{0,8},{8,0},{1,9},{9,1},{2,10},{10,2},{3,11},{11,3},{4,12},{12,4},... | collective-permute-start | bytes 4718600 | tf_op jit(solution)/shard_map/ppermute | solution.py:209
  106.3 22.5 %all-to-all-start.2 = ((bf16[16,64,384]{2,1,0:T(8,128)(2,1)}), bf16[16,64,384]{2,1,0:T(8,128)(2,1)}, u32[]{:S(2)}, u32[]{:S(2)}) async-start(bf16[16,64,384]{2,1,0:T(8,128)(2,1)} %copy-done.6), calls=%async_computation.2 | async-start | bytes 1572864 | tf_op jit(solution)/shard_map/all_to_all | solution.py:204
  110.7 4.2 %collective-permute-start = (s32[16,3]{0,1:T(4,128)S(1)}, s32[16,3]{0,1:T(4,128)S(1)}, u32[]{:S(2)}, u32[]{:S(2)}) collective-permute-start(s32[16,3]{0,1:T(4,128)S(1)} %get-tuple-element.42), channel_id=1, source_target_pairs={{0,16},{16,0},{1,17},{17,1},{2,18},{18,2},{3,19},{19,3},{4,20},{20... | collective-permute-start | bytes 584 | tf_op jit(solution)/shard_map/ppermute | solution.py:215
  122.6 0.9 copy-start.2
  128.8 23.0 %all-to-all-start.1 = ((bf16[16,64,384]{2,1,0:T(8,128)(2,1)}), bf16[16,64,384]{2,1,0:T(8,128)(2,1)}, u32[]{:S(2)}, u32[]{:S(2)}) async-start(bf16[16,64,384]{2,1,0:T(8,128)(2,1)} %copy-done.2), calls=%async_computation.1 | async-start | bytes 1572864 | tf_op jit(solution)/shard_map/all_to_all | solution.py:204
  140.4 0.9 copy-start.3
  151.8 23.1 %all-to-all-start.3 = ((bf16[16,64,384]{2,1,0:T(8,128)(2,1)}), bf16[16,64,384]{2,1,0:T(8,128)(2,1)S(1)}, u32[]{:S(2)}, u32[]{:S(2)}) async-start(bf16[16,64,384]{2,1,0:T(8,128)(2,1)} %copy-done.3), calls=%async_computation.3 | async-start | bytes 1572864 | tf_op jit(solution)/shard_map/all_to_all | solution.py:204

commit v8 on v2

--- a/solution.py
+++ b/solution.py
@@ -39,7 +39,7 @@
         in_specs=[VMEM] * 3,
         out_specs=[VMEM] * len(shapes),
         out_shape=[jax.ShapeDtypeStruct(shape, k.dtype) for shape in shapes],
-        compiler_params=pltpu.CompilerParams(vmem_limit_bytes=24 * 2**20),
+        compiler_params=pltpu.CompilerParams(vmem_limit_bytes=16 * 2**20),
         cost_estimate=pl.CostEstimate(flops=0, bytes_accessed=12 * k.size, transcendentals=0),
         name="pack",
     )(k, v, q)
@@ -116,7 +116,7 @@
         in_specs=[SMEM, VMEM, VMEM, VMEM],
         out_specs=VMEM,
         out_shape=jax.ShapeDtypeStruct((ways, TILE, width), q.dtype),
-        compiler_params=pltpu.CompilerParams(vmem_limit_bytes=24 * 2**20),
+        compiler_params=pltpu.CompilerParams(vmem_limit_bytes=16 * 2**20),
         cost_estimate=pl.CostEstimate(
             flops=4 * ways * TILE * width * keys,
             bytes_accessed=4 * own.size + 4 * ways * TILE * width,

time: 176 us -> 176 us (level)
  no operation moved by 1% of the time
where the time goes in v8:
time: 176 us
  blocking collectives  96.9 us (55%)
  waiting for transfers between devices  37.4 us (21%)
  Pallas kernels  20.2 us (11%)
  starting transfers between devices  14.5 us (8%)
  local copies, waits for them, and re-layouts  5.3 us (3%)
    all_to_all x1, blocking collectives, exchange(): return lax.all_to_all(x, axes, split_axis=0, concat_axis=0, tiled=True)  96.9 us
    all_to_all x3, waiting for transfers between devices, exchange(): return lax.all_to_all(x, axes, split_axis=0, concat_axis=0, tiled=True)  33.3 us
    pallas_call x2, Pallas kernels, attend(): pl.pallas_call(functools.partial(attend_kernel, (rest, spans, rows, q_sta...  18.9 us
    all_to_all x3, starting transfers between devices, exchange(): return lax.all_to_all(x, axes, split_axis=0, concat_axis=0, tiled=True)  12.5 us
    unnamed x10, local copies, waits for them, and re-layouts  4.23 us
    ppermute x1, waiting for transfers between devices, body(): lax.ppermute(table, 'y', [(i, i ^ step) for i in range(chips)])  4.12 us
  transfers between devices with their start and end apart: 5, of which 4 were waited for; matrix products, arithmetic and copies ran while one was open for 1% of the time, Pallas kernels for 11%

profile of v8, /device:TPU:0, one launch (start us, length us, event | category | flops | bytes accessed | tf_op | source)
XLA Modules:
  0.0 175.6 jit_solution(14107704328360295115)
XLA Ops:
  0.0 0.0 copy-start
  0.0 1.4 copy-done
  1.4 0.0 copy-start.1
  1.4 1.4 copy-done.1
  2.8 0.0 copy-start.2
  2.8 1.4 copy-done.2
  4.2 1.3 pack.1
  5.5 96.9 %all_to_all.20.own.q = bf16[16,320,384]{2,1,0:T(8,128)(2,1)} all-to-all(bf16[16,320,384]{2,1,0:T(8,128)(2,1)S(1)} %get-tuple-element.7), channel_id=1, replica_groups=mesh['y'=2,'core'=2,'half'=2,'rest'=4] {'y','rest','half'}, dimensions={0} | all-to-all | bytes 7864320 | tf_op jit(solution)/shard_map/all_to_all | solution.py:145
  102.4 0.0 copy-start.3
  102.4 0.0 copy-start.4
  102.4 0.0 collective-permute-start.1
  102.4 3.9 %all-to-all-start.2 = ((bf16[16,64,384]{2,1,0:T(8,128)(2,1)}), bf16[16,64,384]{2,1,0:T(8,128)(2,1)S(1)}, u32[]{:S(2)}, u32[]{:S(2)}) async-start(bf16[16,64,384]{2,1,0:T(8,128)(2,1)} %get-tuple-element.8), calls=%async_computation.2 | async-start | bytes 1572864 | tf_op jit(solution)/shard_map/all_to_all | solution.py:145
  106.3 0.0 copy-done.3
  106.3 0.0 copy-done.4
  106.3 2.0 %collective-permute-start = (s32[16,3]{0,1:T(4,128)S(1)}, s32[16,3]{0,1:T(4,128)S(1)}, u32[]{:S(2)}, u32[]{:S(2)}) collective-permute-start(s32[16,3]{0,1:T(4,128)S(1)} %get-tuple-element.12), channel_id=1, source_target_pairs={{0,16},{16,0},{1,17},{17,1},{2,18},{18,2},{3,19},{19,3},{4,20},{20... | collective-permute-start | bytes 584 | tf_op jit(solution)/shard_map/ppermute | solution.py:151
  108.3 4.1 %collective-permute-done = s32[16,3]{0,1:T(4,128)S(1)} collective-permute-done((s32[16,3]{0,1:T(4,128)S(1)}, s32[16,3]{0,1:T(4,128)S(1)}, u32[]{:S(2)}, u32[]{:S(2)}) %collective-permute-start) | collective-permute-done | bytes 224 | tf_op jit(solution)/shard_map/ppermute | solution.py:151
  112.4 0.6 gather_fusion
  113.0 0.1 broadcast_in_dim.2
  113.1 0.1 copy.10
  113.2 0.1 copy.12
  113.3 0.0 collective-permute-done.1.swapped
  113.3 10.0 %attend.2 = bf16[16,64,384]{2,1,0:T(8,128)(2,1)} custom-call(s32[4,16]{1,0:T(4,128)S(1)} %bitcast.24, bf16[16,320,384]{2,1,0:T(8,128)(2,1)} %all_to_all.20.own.q, bf16[16,320,384]{2,1,0:T(8,128)(2,1)} %collective-permute-done.1.swapped, bf16[16,320,384]{2,1,0:T(8,128)(2,1)} %all_to_all.20.own.q), custom_call_target="tpu_custom_call" | custom-call | flops 402653184 | bytes 9437184 | tf_op jit(solution)/shard_map/attend/pallas_call | solution.py:114
  123.3 3.9 %all-to-all-done.2.q = bf16[16,64,384]{2,1,0:T(8,128)(2,1)S(1)} async-done(((bf16[16,64,384]{2,1,0:T(8,128)(2,1)}), bf16[16,64,384]{2,1,0:T(8,128)(2,1)S(1)}, u32[]{:S(2)}, u32[]{:S(2)}) %all-to-all-start.2) | async-done | bytes 786464 | tf_op jit(solution)/shard_map/all_to_all | solution.py:145
  127.3 4.3 %all-to-all-start.1 = ((bf16[16,64,384]{2,1,0:T(8,128)(2,1)}), bf16[16,64,384]{2,1,0:T(8,128)(2,1)S(1)}, u32[]{:S(2)}, u32[]{:S(2)}) async-start(bf16[16,64,384]{2,1,0:T(8,128)(2,1)} %attend.2), calls=%async_computation.1 | async-start | bytes 1572864 | tf_op jit(solution)/shard_map/all_to_all | solution.py:145
  131.6 0.1 copy.14
  131.7 8.9 %attend.3 = bf16[16,64,384]{2,1,0:T(8,128)(2,1)} custom-call(s32[4,16]{1,0:T(4,128)S(1)} %bitcast.23, bf16[16,320,384]{2,1,0:T(8,128)(2,1)} %all_to_all.20.own.q, bf16[16,320,384]{2,1,0:T(8,128)(2,1)} %collective-permute-done.1.swapped, bf16[16,64,384]{2,1,0:T(8,128)(2,1)S(1)} %all-to-all-done.2.q), custom_call_target="tpu_custom_call" | custom-call | flops 402653184 | bytes 9437184 | tf_op jit(solution)/shard_map/attend/pallas_call | solution.py:114
  140.5 10.8 %all-to-all-done.1 = bf16[16,64,384]{2,1,0:T(8,128)(2,1)S(1)} async-done(((bf16[16,64,384]{2,1,0:T(8,128)(2,1)}), bf16[16,64,384]{2,1,0:T(8,128)(2,1)S(1)}, u32[]{:S(2)}, u32[]{:S(2)}) %all-to-all-start.1) | async-done | bytes 786464 | tf_op jit(solution)/shard_map/all_to_all | solution.py:145
  151.3 4.3 %all-to-all-start.3 = ((bf16[16,64,384]{2,1,0:T(8,128)(2,1)}), bf16[16,64,384]{2,1,0:T(8,128)(2,1)S(1)}, u32[]{:S(2)}, u32[]{:S(2)}) async-start(bf16[16,64,384]{2,1,0:T(8,128)(2,1)} %attend.3), calls=%async_computation.3 | async-start | bytes 1572864 | tf_op jit(solution)/shard_map/all_to_all | solution.py:145
  155.6 0.1 copy.16
  155.7 18.6 %all-to-all-done.3 = bf16[16,64,384]{2,1,0:T(8,128)(2,1)S(1)} async-done(((bf16[16,64,384]{2,1,0:T(8,128)(2,1)}), bf16[16,64,384]{2,1,0:T(8,128)(2,1)S(1)}, u32[]{:S(2)}, u32[]{:S(2)}) %all-to-all-start.3) | async-done | bytes 786464 | tf_op jit(solution)/shard_map/all_to_all | solution.py:145
  174.3 0.1 copy.17
  174.3 1.3 pad_maximum_fusion
  (8 shorter events, 0.1 us)
Async XLA Ops:
  0.0 1.4 copy-start
  1.4 1.4 copy-start.1
  2.8 1.4 copy-start.2
  102.4 3.9 %copy-start.3 = (s32[1,16,2]{1,2,0:T(2,128)S(1)}, s32[1,16,2]{1,2,0:T(2,128)}, u32[]{:S(2)}) copy-start(s32[1,16,2]{1,2,0:T(2,128)} %param.8) | copy-start | bytes 388
  102.4 3.9 %copy-start.4 = (s32[1,16]{1,0:T(1,128)S(1)}, s32[1,16]{1,0:T(1,128)}, u32[]{:S(2)}) copy-start(s32[1,16]{1,0:T(1,128)} %param.9) | copy-start | bytes 196
  102.4 10.9 %collective-permute-start.1 = (bf16[16,320,384]{2,1,0:T(8,128)(2,1)}, bf16[16,320,384]{2,1,0:T(8,128)(2,1)}, u32[]{:S(2)}, u32[]{:S(2)}) collective-permute-start(bf16[16,320,384]{2,1,0:T(8,128)(2,1)} %all_to_all.20.own.q), channel_id=1, source_target_pairs={{0,8},{8,0},{1,9},{9,1},{2,10},{10,2},{3,11},{11,3},{4,12},{12,4},... | collective-permute-start | bytes 11796488 | tf_op jit(solution)/shard_map/ppermute | solution.py:165
  102.4 24.8 %all-to-all-start.2 = ((bf16[16,64,384]{2,1,0:T(8,128)(2,1)}), bf16[16,64,384]{2,1,0:T(8,128)(2,1)S(1)}, u32[]{:S(2)}, u32[]{:S(2)}) async-start(bf16[16,64,384]{2,1,0:T(8,128)(2,1)} %get-tuple-element.8), calls=%async_computation.2 | async-start | bytes 1572864 | tf_op jit(solution)/shard_map/all_to_all | solution.py:145
  106.3 6.1 %collective-permute-start = (s32[16,3]{0,1:T(4,128)S(1)}, s32[16,3]{0,1:T(4,128)S(1)}, u32[]{:S(2)}, u32[]{:S(2)}) collective-permute-start(s32[16,3]{0,1:T(4,128)S(1)} %get-tuple-element.12), channel_id=1, source_target_pairs={{0,16},{16,0},{1,17},{17,1},{2,18},{18,2},{3,19},{19,3},{4,20},{20... | collective-permute-start | bytes 584 | tf_op jit(solution)/shard_map/ppermute | solution.py:151
  127.3 24.1 %all-to-all-start.1 = ((bf16[16,64,384]{2,1,0:T(8,128)(2,1)}), bf16[16,64,384]{2,1,0:T(8,128)(2,1)S(1)}, u32[]{:S(2)}, u32[]{:S(2)}) async-start(bf16[16,64,384]{2,1,0:T(8,128)(2,1)} %attend.2), calls=%async_computation.1 | async-start | bytes 1572864 | tf_op jit(solution)/shard_map/all_to_all | solution.py:145
  151.3 22.9 %all-to-all-start.3 = ((bf16[16,64,384]{2,1,0:T(8,128)(2,1)}), bf16[16,64,384]{2,1,0:T(8,128)(2,1)S(1)}, u32[]{:S(2)}, u32[]{:S(2)}) async-start(bf16[16,64,384]{2,1,0:T(8,128)(2,1)} %attend.3), calls=%async_computation.3 | async-start | bytes 1572864 | tf_op jit(solution)/shard_map/all_to_all | solution.py:145
